TPU v7x, 32 devices: a whole 2x2x4 slice. The times are simulated.
32 devices in a mesh: section: 2 (over x), ctx: 4 (over z), wt: 4 (over y, core).
Axes of the slice: x: 2, y: 2, z: 4, core: 2. Of those that a mesh axis runs over, the one named last changes fastest.
Arguments:
- boundary: bfloat16 [2, 3, 2048, 1024], P('section', None, ('wt', 'ctx')), may hold values from -6 to 6
- lengths: int32 [3, 4, 4], replicated, may hold values from 1 to 256, 512 in all within a row
- valid: int32 [3, 2048], P(None, ('wt', 'ctx')), may hold values from 0 to 1, as said below
- w_qkv: bfloat16 [2, 1024, 3072], P('section', 'wt'), may hold values from -0.1875 to 0.1875
- w_out: bfloat16 [2, 1024, 1024], P('section', 'wt'), may hold values from -1 to 1
- w_in: bfloat16 [2, 1024, 4096], P('section', 'wt'), may hold values from -0.1875 to 0.1875
- w_down: bfloat16 [2, 4096, 1024], P('section', 'wt'), may hold values from -0.09375 to 0.09375
- bias_in: bfloat16 [2, 4096], P('section', 'wt'), may hold values from -2 to 2
- vectors: bfloat16 [2, 8, 1024], P('section', None, 'wt'), may hold values from -1 to 2
Outputs:
- results: bfloat16 [2, 3, 2048, 1024], P('section', None, ('wt', 'ctx'))
- grad_qkv: float32 [2, 1024, 3072], P('section', 'wt')
- grad_out: float32 [2, 1024, 1024], P('section', 'wt')
- grad_in: float32 [2, 1024, 4096], P('section', 'wt')
- grad_down: float32 [2, 4096, 1024], P('section', 'wt')
- grad_bias_in: float32 [2, 4096], P('section', 'wt')
- grad_vectors: float32 [2, 8, 1024], P('section', None, 'wt')
Inputs may be any that keep to these rules, and one draw needn't show every extreme that they name: Each pack's 4 lengths in natural order sum to 512; one of them is 256. `valid`: the last row of every micro-batch is 1.
All inputs are finite; a program needn't handle non-finite values.
Results may differ from a plain program's by a relative error of at most 0.022.
Values may be sent and summed in bfloat16 or wider, within the bound.
A program may use at most 256 MiB of HBM per device.

v0:
```python
import jax
import jax.numpy as jnp
from jax import lax
from jax.sharding import PartitionSpec as P

HEADS = 16
LOSS_SCALE = 1024


def shifted(block, axis, distance):
    devices = range(lax.axis_size(axis))
    route = [(i - distance, i) for i in devices if i - distance in devices]
    return lax.ppermute(block, axis, route)


def as_sent(x):

    def short(part):
        return part.astype(jnp.bfloat16) if part.dtype == jnp.float32 else part

    return jax.tree.map(short, x)


def layer_norm(values, gain, shift):
    center = jnp.mean(values, axis=-1, keepdims=True)
    offset = values - center
    spread = jnp.mean(offset * offset, axis=-1, keepdims=True)
    return offset * lax.rsqrt(spread + 1e-05) * gain + shift


def exact_gelu(values):
    return jax.nn.gelu(values, approximate=False)


def dealt_ids(length_row, pack_size, ctx_count):
    ends = jnp.cumsum(length_row)
    places = jnp.arange(pack_size, dtype=jnp.int32)
    natural = jnp.sum((places[:, None] >= ends[None, :]).astype(jnp.int32), axis=1)
    return natural.reshape(pack_size // ctx_count, ctx_count).T.reshape(pack_size)


def split_blocks(full_kv, ids_keys):
    block = min(512, full_kv.shape[0])
    count_blocks = full_kv.shape[0] // block
    return (
        full_kv.reshape(count_blocks, block, full_kv.shape[1]),
        ids_keys.reshape(count_blocks, block),
    )


def split_kv(block_kv, heads):
    half = block_kv.shape[1] // 2
    keys = block_kv[:, :half].reshape(block_kv.shape[0], heads, -1)
    values = block_kv[:, half:].reshape(block_kv.shape[0], heads, -1)
    return (keys, values)


def block_scores(queries, keys, ids_query, ids_keys, scale):
    scores = jnp.einsum("qhd,khd->hqk", queries, keys, preferred_element_type=jnp.float32) * scale
    same = ids_query[:, None] == ids_keys[None, :]
    return jnp.where(same[None], scores, -1000000000.0)


def attend_forward(queries, full_kv, ids_query, ids_keys, heads, scale):
    blocks, id_blocks = split_blocks(full_kv, ids_keys)
    query_rows = queries.shape[0]

    def total_step(carry, items):
        run_max, run_sum = carry
        keys, values = split_kv(items[0], heads)
        scores = block_scores(queries, keys, ids_query, items[1], scale)
        new_max = jnp.maximum(run_max, jnp.max(scores, axis=-1))
        run_sum = run_sum * jnp.exp(run_max - new_max) + jnp.sum(
            jnp.exp(scores - new_max[..., None]), axis=-1
        )
        return ((new_max, run_sum), None)

    start = (
        jnp.full((heads, query_rows), -1e30, jnp.float32),
        jnp.zeros((heads, query_rows), jnp.float32),
    )
    (run_max, run_sum), _ = lax.scan(total_step, start, (blocks, id_blocks))
    log_total = run_max + jnp.log(run_sum)

    def mix_step(carry, items):
        keys, values = split_kv(items[0], heads)
        scores = block_scores(queries, keys, ids_query, items[1], scale)
        probs = jnp.exp(scores - log_total[..., None]).astype(jnp.bfloat16)
        return (
            carry + jnp.einsum("hqk,khd->qhd", probs, values, preferred_element_type=jnp.float32),
            None,
        )

    mixed, _ = lax.scan(mix_step, jnp.zeros(queries.shape, jnp.float32), (blocks, id_blocks))
    return (mixed.reshape(query_rows, -1), log_total)


def attend_backward(queries, full_kv, ids_query, ids_keys, mixed_grad, log_total, heads, scale):
    blocks, id_blocks = split_blocks(full_kv, ids_keys)
    grad_heads = mixed_grad.reshape(queries.shape)

    def inner_step(carry, items):
        keys, values = split_kv(items[0], heads)
        scores = block_scores(queries, keys, ids_query, items[1], scale)
        probs = jnp.exp(scores - log_total[..., None])
        prob_grad = jnp.einsum(
            "qhd,khd->hqk", grad_heads, values, preferred_element_type=jnp.float32
        )
        return (carry + jnp.sum(probs * prob_grad, axis=-1), None)

    inner, _ = lax.scan(inner_step, jnp.zeros(log_total.shape, jnp.float32), (blocks, id_blocks))

    def grad_step(carry, items):
        keys, values = split_kv(items[0], heads)
        scores = block_scores(queries, keys, ids_query, items[1], scale)
        probs = jnp.exp(scores - log_total[..., None])
        prob_grad = jnp.einsum(
            "qhd,khd->hqk", grad_heads, values, preferred_element_type=jnp.float32
        )
        score_grad = (probs * (prob_grad - inner[..., None])).astype(jnp.bfloat16)
        carry = (
            carry
            + jnp.einsum("hqk,khd->qhd", score_grad, keys, preferred_element_type=jnp.float32)
            * scale
        )
        key_grad = (
            jnp.einsum("hqk,qhd->khd", score_grad, queries, preferred_element_type=jnp.float32)
            * scale
        )
        value_grad = jnp.einsum(
            "hqk,qhd->khd",
            probs.astype(jnp.bfloat16),
            grad_heads,
            preferred_element_type=jnp.float32,
        )
        block = keys.shape[0]
        return (
            carry,
            jnp.concatenate([key_grad.reshape(block, -1), value_grad.reshape(block, -1)], axis=1),
        )

    query_grad, partial_kv = lax.scan(
        grad_step, jnp.zeros(queries.shape, jnp.float32), (blocks, id_blocks)
    )
    query_grad = query_grad.reshape(queries.shape[0], -1)
    return (query_grad, partial_kv.reshape(-1, partial_kv.shape[-1]), inner)


def shards(boundary, lengths, valid, w_qkv, w_out, w_in, w_down, bias_in, vectors):
    section_at = lax.axis_index("section")
    ctx_count = lax.axis_size("ctx")
    ctx_at = lax.axis_index("ctx")
    wt_at = lax.axis_index("wt")
    micro_count = boundary.shape[1]
    row_count = boundary.shape[2]
    width = boundary.shape[3]
    pack_size = row_count * ctx_count
    head_size = width // HEADS
    scale = head_size ** (-0.5)
    gathered = (
        lax.all_gather(w_qkv[0], "wt", axis=0, tiled=True),
        lax.all_gather(w_out[0], "wt", axis=0, tiled=True),
        lax.all_gather(w_in[0], "wt", axis=0, tiled=True),
        lax.all_gather(w_down[0], "wt", axis=0, tiled=True),
        lax.all_gather(bias_in[0], "wt", axis=0, tiled=True),
        lax.all_gather(vectors[0], "wt", axis=1, tiled=True),
    )
    weight_qkv, weight_out, weight_in, weight_down, in_bias, vector_rows = gathered
    in_bias = in_bias.astype(jnp.float32)
    vector_rows = vector_rows.astype(jnp.float32)
    qkv_bias = jnp.concatenate([vector_rows[0], jnp.zeros((width,), jnp.float32), vector_rows[1]])
    my_lengths = lax.dynamic_index_in_dim(lengths, wt_at, 1, keepdims=False)

    def ids_of(length_row):
        return dealt_ids(length_row, pack_size, ctx_count)

    pack_ids = jax.vmap(ids_of)(my_lengths)
    query_ids = lax.dynamic_slice_in_dim(pack_ids, ctx_at * row_count, row_count, 1)
    count = lax.psum(jnp.sum(valid.astype(jnp.float32)), ("ctx", "wt"))
    factor = LOSS_SCALE / count
    empty_rows = jnp.zeros((row_count, width), jnp.bfloat16)
    arriving = empty_rows
    kept_list = []
    cotangents = []
    final_states = []
    for tick_at in range(micro_count + 1):
        own_input = boundary[0, tick_at] if tick_at < micro_count else empty_rows
        inputs = jnp.where(section_at == 0, own_input, arriving)
        micro_here = jnp.clip(tick_at - section_at, 0, micro_count - 1)
        ids_keys = lax.dynamic_index_in_dim(pack_ids, micro_here, 0, keepdims=False)
        ids_query = lax.dynamic_index_in_dim(query_ids, micro_here, 0, keepdims=False)
        residual = inputs.astype(jnp.float32)
        projected = jnp.dot(inputs, weight_qkv, preferred_element_type=jnp.float32) + qkv_bias
        layer_queries = (
            projected[:, :width].astype(jnp.bfloat16).reshape(row_count, HEADS, head_size)
        )
        layer_local_kv = projected[:, width:].astype(jnp.bfloat16)
        layer_full_kv = lax.all_gather(layer_local_kv, "ctx", axis=0, tiled=True)
        mixed, layer_log_total = attend_forward(
            layer_queries, layer_full_kv, ids_query, ids_keys, HEADS, scale
        )
        layer_mixed_low = mixed.astype(jnp.bfloat16)
        branch = (
            jnp.dot(layer_mixed_low, weight_out, preferred_element_type=jnp.float32)
            + vector_rows[2]
        )
        layer_summed = residual + branch
        first = layer_norm(layer_summed, vector_rows[3], vector_rows[4])
        layer_first_low = first.astype(jnp.bfloat16)
        layer_hidden_pre = (
            jnp.dot(layer_first_low, weight_in, preferred_element_type=jnp.float32) + in_bias
        )
        layer_hidden_low = exact_gelu(layer_hidden_pre).astype(jnp.bfloat16)
        layer_second = first + (
            jnp.dot(layer_hidden_low, weight_down, preferred_element_type=jnp.float32)
            + vector_rows[5]
        )
        output = layer_norm(layer_second, vector_rows[6], vector_rows[7])
        layer_kept = (
            inputs,
            layer_queries,
            layer_local_kv,
            layer_full_kv,
            layer_mixed_low,
            layer_log_total,
            layer_summed,
            layer_first_low,
            layer_hidden_pre,
            layer_hidden_low,
            layer_second,
            ids_keys,
            ids_query,
        )
        output, kept = (output, layer_kept)
        kept_list.append(kept)
        if tick_at > 0:
            teacher = boundary[0, tick_at - 1].astype(jnp.float32)
            covered = valid[tick_at - 1].astype(jnp.float32)[:, None]
            cotangents.append(factor * covered * (output - teacher))
            final_states.append(output.astype(jnp.bfloat16))
        else:
            cotangents.append(jnp.zeros((row_count, width), jnp.float32))
        if tick_at < micro_count:
            arriving = shifted(output.astype(jnp.bfloat16), "section", 1)
    returning = empty_rows
    totals = None
    input_grads = [None] * micro_count
    for back_at in range(micro_count + 1):
        forward_at = micro_count - back_at
        grad_output = jnp.where(
            section_at == 1, cotangents[forward_at], returning.astype(jnp.float32)
        )
        (
            layer_inputs,
            queries,
            local_kv,
            full_kv,
            mixed_low,
            log_total,
            summed,
            first_low,
            hidden_pre,
            hidden_low,
            second,
            layer_ids_keys,
            layer_ids_query,
        ) = kept_list[forward_at]
        full_kv = lax.all_gather(local_kv, "ctx", axis=0, tiled=True)
        _, pull_last = jax.vjp(layer_norm, second, vector_rows[6], vector_rows[7])
        grad_second, grad_gain_two, grad_shift_two = pull_last(grad_output)
        down_low = grad_second.astype(jnp.bfloat16)
        layer_grad_down = jnp.einsum(
            "rf,rd->fd", hidden_low, down_low, preferred_element_type=jnp.float32
        )
        grad_bias_two = jnp.sum(down_low.astype(jnp.float32), axis=0)
        _, pull_gelu = jax.vjp(exact_gelu, hidden_pre)
        (grad_pre,) = pull_gelu(
            jnp.einsum("rd,fd->rf", down_low, weight_down, preferred_element_type=jnp.float32)
        )
        pre_low = grad_pre.astype(jnp.bfloat16)
        layer_grad_in = jnp.einsum(
            "rd,rf->df", first_low, pre_low, preferred_element_type=jnp.float32
        )
        layer_grad_bias_in = jnp.sum(pre_low.astype(jnp.float32), axis=0)
        grad_first = grad_second + jnp.einsum(
            "rf,df->rd", pre_low, weight_in, preferred_element_type=jnp.float32
        )
        _, pull_first = jax.vjp(layer_norm, summed, vector_rows[3], vector_rows[4])
        grad_summed, grad_gain_one, grad_shift_one = pull_first(grad_first)
        branch_low = grad_summed.astype(jnp.bfloat16)
        layer_grad_out = jnp.einsum(
            "rd,re->de", mixed_low, branch_low, preferred_element_type=jnp.float32
        )
        grad_bias_out = jnp.sum(branch_low.astype(jnp.float32), axis=0)
        mixed_grad = jnp.einsum(
            "re,de->rd", branch_low, weight_out, preferred_element_type=jnp.float32
        ).astype(jnp.bfloat16)
        query_grad, partial_kv, inner = attend_backward(
            queries, full_kv, layer_ids_query, layer_ids_keys, mixed_grad, log_total, HEADS, scale
        )
        kv_grad = lax.psum_scatter(
            partial_kv.astype(jnp.bfloat16), "ctx", scatter_dimension=0, tiled=True
        )
        query_low = query_grad.astype(jnp.bfloat16)
        projected_grad = jnp.concatenate([query_low, kv_grad], axis=1)
        layer_grad_qkv = jnp.einsum(
            "rd,re->de", layer_inputs, projected_grad, preferred_element_type=jnp.float32
        )
        vector_grad = jnp.stack(
            [
                jnp.sum(query_low.astype(jnp.float32), axis=0),
                jnp.sum(kv_grad[:, width:].astype(jnp.float32), axis=0),
                grad_bias_out,
                grad_gain_one,
                grad_shift_one,
                grad_bias_two,
                grad_gain_two,
                grad_shift_two,
            ]
        )
        grad_inputs = grad_summed + jnp.einsum(
            "re,de->rd", projected_grad, weight_qkv, preferred_element_type=jnp.float32
        )
        grad_inputs, grads = (
            grad_inputs,
            (
                layer_grad_qkv,
                layer_grad_out,
                layer_grad_in,
                layer_grad_down,
                layer_grad_bias_in,
                vector_grad,
            ),
        )
        totals = grads if totals is None else jax.tree.map(jnp.add, totals, grads)
        if forward_at < micro_count:
            input_grads[forward_at] = grad_inputs
        if back_at < micro_count:
            returning = shifted(grad_inputs.astype(jnp.bfloat16), "section", -1)
    results = jnp.stack(
        [
            jnp.where(section_at == 0, input_grads[index].astype(jnp.bfloat16), final_states[index])
            for index in range(micro_count)
        ]
    )[None]
    shares = (
        lax.psum_scatter(
            totals[0].astype(jnp.bfloat16), "wt", scatter_dimension=0, tiled=True
        ).astype(jnp.float32),
        lax.psum_scatter(
            totals[1].astype(jnp.bfloat16), "wt", scatter_dimension=0, tiled=True
        ).astype(jnp.float32),
        lax.psum_scatter(
            totals[2].astype(jnp.bfloat16), "wt", scatter_dimension=0, tiled=True
        ).astype(jnp.float32),
        lax.psum_scatter(
            totals[3].astype(jnp.bfloat16), "wt", scatter_dimension=0, tiled=True
        ).astype(jnp.float32),
        lax.psum_scatter(
            totals[4].astype(jnp.bfloat16), "wt", scatter_dimension=0, tiled=True
        ).astype(jnp.float32),
        lax.psum_scatter(
            totals[5].astype(jnp.bfloat16), "wt", scatter_dimension=1, tiled=True
        ).astype(jnp.float32),
    )
    shares = jax.tree.map(lambda part: part.astype(jnp.float32), lax.psum(as_sent(shares), "ctx"))
    grad_qkv, grad_out, grad_in, grad_down, grad_bias_in, grad_vectors = shares
    return (
        results,
        grad_qkv[None],
        grad_out[None],
        grad_in[None],
        grad_down[None],
        grad_bias_in[None],
        grad_vectors[None],
    )


def solution(mesh):
    in_specs = (
        P("section", None, ("wt", "ctx"), None),
        P(),
        P(None, ("wt", "ctx")),
        P("section", "wt", None),
        P("section", "wt", None),
        P("section", "wt", None),
        P("section", "wt", None),
        P("section", "wt"),
        P("section", None, "wt"),
    )
    out_specs = (
        P("section", None, ("wt", "ctx"), None),
        P("section", "wt", None),
        P("section", "wt", None),
        P("section", "wt", None),
        P("section", "wt", None),
        P("section", "wt"),
        P("section", None, "wt"),
    )
    return jax.shard_map(shards, mesh=mesh, in_specs=in_specs, out_specs=out_specs, check_vma=False)
```

profile of v0, /device:TPU:4, one launch (start us, length us, event | category | flops | bytes accessed | tf_op | source)
XLA Modules:
  0.0 1373.1 jit_solution(4366697255076378141)
XLA Ops:
  13.9 42.1 %all-gather.23.cloned.1.call-done = bf16[1,1024,3072]{2,1,0:T(8,128)(2,1)} async-done(((bf16[1,256,3072]{2,1,0:T(8,128)(2,1)}), bf16[1,1024,3072]{2,1,0:T(8,128)(2,1)}) %all-gather.23.cloned.1.call-update) | async-done | bytes 6291472 | tf_op jit(solution)/shard_map/all_gather | solution.py:161
  70.8 37.2 %all-gather.15.cloned.1.call-done = bf16[512,2048]{1,0:T(8,128)(2,1)} async-done(((bf16[128,2048]{1,0:T(8,128)(2,1)}), bf16[512,2048]{1,0:T(8,128)(2,1)}) %all-gather.15.cloned.1.call-update) | async-done | bytes 2097168 | tf_op jit(solution)/shard_map/all_gather | solution.py:198
  115.4 14.4 %all-gather.25.cloned.1.call-done = bf16[1,1024,1024]{2,1,0:T(8,128)(2,1)} async-done(((bf16[1,256,1024]{2,1,0:T(8,128)(2,1)}), bf16[1,1024,1024]{2,1,0:T(8,128)(2,1)}) %all-gather.25.cloned.1.call-update) | async-done | bytes 2097168 | tf_op jit(solution)/shard_map/all_gather | solution.py:162
  132.2 57.3 %all-gather.27.cloned.1.call-done = bf16[1,1024,4096]{2,1,0:T(8,128)(2,1)} async-done(((bf16[1,256,4096]{2,1,0:T(8,128)(2,1)}), bf16[1,1024,4096]{2,1,0:T(8,128)(2,1)}) %all-gather.27.cloned.1.call-update) | async-done | bytes 8388624 | tf_op jit(solution)/shard_map/all_gather | solution.py:163
  195.6 53.7 %all-gather.29.cloned.1.call-done = bf16[1,4096,1024]{2,1,0:T(8,128)(2,1)} async-done(((bf16[1,1024,1024]{2,1,0:T(8,128)(2,1)}), bf16[1,4096,1024]{2,1,0:T(8,128)(2,1)}) %all-gather.29.cloned.1.call-update) | async-done | bytes 8388624 | tf_op jit(solution)/shard_map/all_gather | solution.py:164
  249.3 9.7 fusion.337
  272.0 47.7 %all-gather.17.cloned.1.call-done = bf16[512,2048]{1,0:T(8,128)(2,1)} async-done(((bf16[128,2048]{1,0:T(8,128)(2,1)}), bf16[512,2048]{1,0:T(8,128)(2,1)}) %all-gather.17.cloned.1.call-update) | async-done | bytes 2097168 | tf_op jit(solution)/shard_map/all_gather | solution.py:198
  330.6 8.4 multiply_convert_fusion.10
  355.5 43.9 %all-gather.19.cloned.1.call-done = bf16[512,2048]{1,0:T(8,128)(2,1)} async-done(((bf16[128,2048]{1,0:T(8,128)(2,1)}), bf16[512,2048]{1,0:T(8,128)(2,1)}) %all-gather.19.cloned.1.call-update) | async-done | bytes 2097168 | tf_op jit(solution)/shard_map/all_gather | solution.py:198
  411.7 9.4 multiply_convert_fusion.9
  437.9 27.5 %psum.49 = f32[]{:T(128)} all-reduce(f32[]{:T(128)} %convert_reduce_fusion.21), channel_id=1, replica_groups=mesh['section'=2,'ctx'=4,'wt'=4] {'ctx','wt'}, use_global_device_ids=true, to_apply=%region_1.2 | all-reduce | flops 1 | bytes 8 | tf_op jit(solution)/shard_map/psum | solution.py:179
  471.0 11.9 all-gather.21.cloned.1.call-done
  509.3 8.5 convert_reduce_fusion.3
  544.2 39.2 %reduce-scatter.28.cloned.1.call-done = bf16[128,2048]{1,0:T(8,128)(2,1)} async-done(((bf16[512,2048]{1,0:T(8,128)(2,1)}), bf16[128,2048]{1,0:T(8,128)(2,1)}) %reduce-scatter.28.cloned.1.call-update) | async-done | bytes 524304
  592.5 8.3 collective-permute-done.3
  603.8 10.2 convert_reduce_fusion.2
  639.6 38.4 %reduce-scatter.30.cloned.1.call-done = bf16[128,2048]{1,0:T(8,128)(2,1)} async-done(((bf16[512,2048]{1,0:T(8,128)(2,1)}), bf16[128,2048]{1,0:T(8,128)(2,1)}) %reduce-scatter.30.cloned.1.call-update) | async-done | bytes 524304
  697.6 10.2 convert_reduce_fusion.1
  733.0 39.6 %reduce-scatter.32.cloned.1.call-done = bf16[128,2048]{1,0:T(8,128)(2,1)} async-done(((bf16[512,2048]{1,0:T(8,128)(2,1)}), bf16[128,2048]{1,0:T(8,128)(2,1)}) %reduce-scatter.32.cloned.1.call-update) | async-done | bytes 524304
  780.7 8.5 collective-permute-done.5
  791.1 10.2 convert_reduce_fusion
  844.1 20.1 %reduce-scatter.34.cloned.1.call-done = bf16[128,2048]{1,0:T(8,128)(2,1)} async-done(((bf16[512,2048]{1,0:T(8,128)(2,1)}), bf16[128,2048]{1,0:T(8,128)(2,1)}) %reduce-scatter.34.cloned.1.call-update) | async-done | bytes 524304
  873.2 17.2 %add_convert_fusion.2 = bf16[1024,3072]{1,0:T(8,128)(2,1)} fusion(f32[1024,3072]{1,0:T(8,128)} %fusion.241, f32[1024,3072]{1,0:T(8,128)} %fusion.244, f32[1024,3072]{1,0:T(8,128)} %fusion.243, bf16[128,1024]{1,0:T(8,128)(2,1)S(1)} %copy-done.53, bf16[128,2048]{0,1:T(8,128)(2,1)S(1)} %copy-done.44, bf16[128,1024]{0,1:T(8,128)(2,1)S(1)} %bitcast.517), kind=kOutput, calls=%fused_computation.2 | convolution fusion | flops 819462144 | bytes 45088768 | tf_op jit(solution)/shard_map/rd,re->de/dot_general | solution.py:306
  891.8 8.3 fusion.311
  900.1 10.0 fusion.314
  910.0 8.4 fusion.317
  918.4 21.4 %add_convert_fusion.1 = bf16[1024,4096]{1,0:T(8,128)(2,1)} fusion(f32[1024,4096]{1,0:T(8,128)} %fusion.317, f32[1024,4096]{1,0:T(8,128)} %fusion.311, f32[1024,4096]{1,0:T(8,128)} %fusion.314, bf16[128,4096]{1,0:T(8,128)(2,1)S(1)} %copy-done.62, f32[128,1024]{1,0:T(8,128)S(1)} %copy-done.12, f32[1024]{0:T(1024)S(1)} %bitcast.545, f32[1024]{0:T(1024)S(1)} %bitcast.515, ...), kind=kOutput, calls=%fused_computation.1 | convolution fusion | flops 1091174400 | bytes 60302336 | tf_op jit(solution)/shard_map/rd,rf->df/dot_general | solution.py:281
  965.6 25.2 %add_convert_fusion = bf16[4096,1024]{1,0:T(8,128)(2,1)} fusion(f32[4096,1024]{1,0:T(8,128)} %fusion.349, f32[4096,1024]{1,0:T(8,128)} %fusion.347, f32[4096,1024]{1,0:T(8,128)} %fusion.348, bf16[128,1024]{1,0:T(8,128)(2,1)S(1)} %copy-done.134, f32[128,4096]{1,0:T(8,128)S(1)} %copy-done.100), kind=kOutput, calls=%fused_computation | convolution fusion | flops 1124597760 | bytes 61079552 | tf_op jit(solution)/shard_map/rf,rd->fd/dot_general | solution.py:272
  993.9 38.1 %reduce-scatter.22.cloned.1.call-done = bf16[256,4096]{1,0:T(8,128)(2,1)} async-done(((bf16[1024,4096]{1,0:T(8,128)(2,1)}), bf16[256,4096]{1,0:T(8,128)(2,1)}) %reduce-scatter.22.cloned.1.call-update) | async-done | bytes 2097168 | tf_op jit(solution)/shard_map/reduce_scatter | solution.py:353
  1032.1 74.4 %reduce-scatter.24.cloned.1.call-done = bf16[1024,1024]{1,0:T(8,128)(2,1)} async-done(((bf16[4096,1024]{1,0:T(8,128)(2,1)}), bf16[1024,1024]{1,0:T(8,128)(2,1)}) %reduce-scatter.24.cloned.1.call-update) | async-done | bytes 2097168 | tf_op jit(solution)/shard_map/reduce_scatter | solution.py:356
  1128.5 12.3 all-reduce.1
  1142.0 214.3 %all-reduce.5.cloned.1.call-done = (bf16[1,256,3072]{2,1,0:T(8,128)(2,1)}, bf16[1,256,1024]{2,1,0:T(8,128)(2,1)}, bf16[1,256,4096]{2,1,0:T(8,128)(2,1)}, bf16[1,1024,1024]{2,1,0:T(8,128)(2,1)}) async-done(((bf16[1,256,3072]{2,1,0:T(8,128)(2,1)}, bf16[1,256,1024]{2,1,0:T(8,128)(2,1)}, bf16[1,256,4096]{2,1,0:T(8,128)(2,1)}, bf16[1,1024,1024]{2,1,0:T(8,128)(2,1)}), (bf16[1,256,3072]{2,1,0:T(8,128)(2,1)}, ...) | async-done | bytes 6291472 | tf_op jit(solution)/shard_map/psum | solution.py:366
  (794 shorter events, 367.6 us)
Async XLA Ops:
  7.2 48.9 %all-gather.23.cloned.1.call-start = ((), (), s32[]{:S(2)}) async-start(), calls=%async_computation.18 | async-start | bytes 7864320 | tf_op jit(solution)/shard_map/all_gather | solution.py:161
  7.9 100.1 %all-gather.15.cloned.1.call-start = ((), (), s32[]{:S(2)}) async-start(), calls=%async_computation.9 | async-start | bytes 2621440 | tf_op jit(solution)/shard_map/all_gather | solution.py:198
  13.9 490.0 %copy-start.103 = (f32[1,1,1024]{2,1,0:T(1,128)}, f32[1,1,1024]{2,1,0:T(1,128)S(1)}, u32[]{:S(2)}) copy-start(f32[1,1,1024]{2,1,0:T(1,128)S(1)} %get-tuple-element.420) | copy-start | bytes 12292
  60.8 69.0 %all-gather.25.cloned.1.call-start = ((), (), s32[]{:S(2)}) async-start(), calls=%async_computation.19 | async-start | bytes 2621440 | tf_op jit(solution)/shard_map/all_gather | solution.py:162
  61.5 128.0 %all-gather.27.cloned.1.call-start = ((), (), s32[]{:S(2)}) async-start(), calls=%async_computation.20 | async-start | bytes 10485760 | tf_op jit(solution)/shard_map/all_gather | solution.py:163
  62.1 187.1 %all-gather.29.cloned.1.call-start = ((), (), s32[]{:S(2)}) async-start(), calls=%async_computation.21 | async-start | bytes 10485760 | tf_op jit(solution)/shard_map/all_gather | solution.py:164
  62.7 257.0 %all-gather.17.cloned.1.call-start = ((), (), s32[]{:S(2)}) async-start(), calls=%async_computation.10 | async-start | bytes 2621440 | tf_op jit(solution)/shard_map/all_gather | solution.py:198
  70.6 255.0 %copy-start.107 = (pred[128,512]{1,0:T(8,128)(4,1)}, pred[128,512]{1,0:T(8,128)(4,1)S(1)}, u32[]{:S(2)}) copy-start(pred[128,512]{1,0:T(8,128)(4,1)S(1)} %get-tuple-element.542) | copy-start | bytes 196612
  115.3 80.3 %copy-start.127 = (bf16[16,64,128]{2,1,0:T(8,128)(2,1)}, bf16[16,64,128]{2,1,0:T(8,128)(2,1)S(1)}, u32[]{:S(2)}) copy-start(bf16[16,64,128]{2,1,0:T(8,128)(2,1)S(1)} %convolution_convert_fusion.7) | copy-start | bytes 786436
  131.9 117.3 %copy-start.11 = (f32[128,1024]{1,0:T(8,128)}, f32[128,1024]{1,0:T(8,128)S(1)}, u32[]{:S(2)}) copy-start(f32[128,1024]{1,0:T(8,128)S(1)} %get-tuple-element.457) | copy-start | bytes 1572868
  132.0 117.3 %copy-start.157 = (f32[128]{0:T(128)}, f32[128]{0:T(128)S(1)}, u32[]{:S(2)}) copy-start(f32[128]{0:T(128)S(1)} %broadcast_multiply_fusion.7) | copy-start | bytes 1540
  132.2 117.1 %copy-start.193 = (f32[128]{0:T(128)}, f32[128]{0:T(128)S(1)}, u32[]{:S(2)}) copy-start(f32[128]{0:T(128)S(1)} %fusion.275) | copy-start | bytes 1540
  260.1 9.6 collective-permute-start
  271.7 127.6 %all-gather.19.cloned.1.call-start = ((), (), s32[]{:S(2)}) async-start(), calls=%async_computation.11 | async-start | bytes 2621440 | tf_op jit(solution)/shard_map/all_gather | solution.py:198
  342.3 8.9 collective-permute-start.1
  353.3 129.6 %all-gather.21.cloned.1.call-start = ((), (), s32[]{:S(2)}) async-start(), calls=%async_computation.12 | async-start | bytes 2621440 | tf_op jit(solution)/shard_map/all_gather | solution.py:198
  410.9 206.9 %copy-start.17 = (f32[128,1024]{1,0:T(8,128)}, f32[128,1024]{1,0:T(8,128)S(1)}, u32[]{:S(2)}) copy-start(f32[128,1024]{1,0:T(8,128)S(1)} %get-tuple-element.479) | copy-start | bytes 1572868
  422.7 180.2 %copy-start.13 = (f32[128,1024]{1,0:T(8,128)}, f32[128,1024]{1,0:T(8,128)S(1)}, u32[]{:S(2)}) copy-start(f32[128,1024]{1,0:T(8,128)S(1)} %get-tuple-element.493) | copy-start | bytes 1572868
  424.8 8.9 collective-permute-start.2
  436.5 146.9 %reduce-scatter.28.cloned.1.call-start = ((), (), s32[]{:S(2)}) async-start(), calls=%async_computation.22 | async-start | bytes 2621440
  540.7 137.2 %reduce-scatter.30.cloned.1.call-start = ((), (), s32[]{:S(2)}) async-start(), calls=%async_computation.23 | async-start | bytes 2621440
  590.9 9.9 collective-permute-start.3
  635.3 137.3 %reduce-scatter.32.cloned.1.call-start = ((), (), s32[]{:S(2)}) async-start(), calls=%async_computation.24 | async-start | bytes 2621440
  684.7 9.9 collective-permute-start.4
  729.9 134.3 %reduce-scatter.34.cloned.1.call-start = ((), (), s32[]{:S(2)}) async-start(), calls=%async_computation.25 | async-start | bytes 2621440
  779.3 9.9 collective-permute-start.5
  821.5 172.4 %reduce-scatter.20.cloned.1.call-start = ((), (), s32[]{:S(2)}) async-start(), calls=%async_computation.14 | async-start | bytes 2621440 | tf_op jit(solution)/shard_map/reduce_scatter | solution.py:350
  828.3 165.6 %reduce-scatter.18.cloned.1.call-start = ((), (), s32[]{:S(2)}) async-start(), calls=%async_computation.13 | async-start | bytes 7864320 | tf_op jit(solution)/shard_map/reduce_scatter | solution.py:347
  890.4 141.7 %reduce-scatter.22.cloned.1.call-start = ((), (), s32[]{:S(2)}) async-start(), calls=%async_computation.15 | async-start | bytes 10485760 | tf_op jit(solution)/shard_map/reduce_scatter | solution.py:353
  939.9 166.5 %reduce-scatter.24.cloned.1.call-start = ((), (), s32[]{:S(2)}) async-start(), calls=%async_computation.16 | async-start | bytes 10485760 | tf_op jit(solution)/shard_map/reduce_scatter | solution.py:356
  991.1 137.3 %reduce-scatter.26.cloned.1.call-start = ((), (), s32[]{:S(2)}) async-start(), calls=%async_computation.17 | async-start | bytes 20480 | tf_op jit(solution)/shard_map/reduce_scatter | solution.py:362
  993.8 362.5 %all-reduce.5.cloned.1.call-start = ((), (), s32[]{:S(2)}) async-start(), calls=%async_computation.26 | async-start | bytes 12582912 | tf_op jit(solution)/shard_map/psum | solution.py:366
  (246 other events, 2283.9 us)
Sparse Core Ops, SparseCore 0:
  9.6 46.4 all-gather.22
  60.9 47.0 all-gather.14
  109.6 20.1 all-gather.24
  131.2 58.2 all-gather.26
  190.9 58.2 all-gather.28
  271.8 47.8 all-gather.16
  353.4 45.8 all-gather.18
  436.7 46.1 all-gather.20
  540.8 42.5 reduce-scatter.27
  635.4 42.4 reduce-scatter.29
  730.0 42.4 reduce-scatter.31
  821.7 42.4 reduce-scatter.33
  867.3 29.5 reduce-scatter.19
  899.5 58.3 reduce-scatter.17
  960.3 71.7 reduce-scatter.21
  1034.7 71.6 reduce-scatter.23
  1109.2 19.1 reduce-scatter.25
  1131.1 225.1 all-reduce.4
where the time goes:
time: 1380 us; the launch traced here: 1370 us
  waiting for transfers between devices  821 us (59%)
  matrix products  321 us (23%)
  local copies, waits for them, and re-layouts  80.6 us (6%)
  blocking collectives  57.9 us (4%)
  other arithmetic  55.3 us (4%)
  between operations  19.3 us (1%)
  starting transfers between devices  17.6 us (1%)
    psum x1, waiting for transfers between devices, shards(): lax.psum(as_sent(shares), 'ctx')  214 us
    all_gather x4, waiting for transfers between devices, shards(): layer_full_kv = lax.all_gather(layer_local_kv, 'ctx', axis=0, tiled=True)  141 us
    unnamed x22, waiting for transfers between devices  140 us
    reduce_scatter x1, waiting for transfers between devices, shards(): lax.psum_scatter(totals[3].astype(jnp.bfloat16), 'wt', scatter_dimension=...  74.4 us
    all_gather x1, waiting for transfers between devices, shards(): lax.all_gather(w_in[0], 'wt', axis=0, tiled=True)  57.3 us
    all_gather x1, waiting for transfers between devices, shards(): lax.all_gather(w_down[0], 'wt', axis=0, tiled=True)  53.7 us
    dot_general x4, matrix products, shards(): jnp.einsum('rf,rd->fd', hidden_low, down_low, preferred_element_type=jnp....  49.7 us
    dot_general x4, matrix products, shards(): jnp.einsum('rd,rf->df', first_low, pre_low, preferred_element_type=jnp.fl...  48 us
  transfers between devices with their start and end apart: 24, of which 22 were waited for; matrix products, arithmetic and copies ran while one was open for 14% of the time, Pallas kernels for 0%

commit v1 on v0

--- a/solution.py
+++ b/solution.py
@@ -1,6 +1,10 @@
+import functools
+
 import jax
 import jax.numpy as jnp
 from jax import lax
+from jax.experimental import pallas as pl
+from jax.experimental.pallas import tpu as pltpu
 from jax.sharding import PartitionSpec as P
 
 HEADS = 16
@@ -376,6 +380,300 @@
     )
 
 
+PAIR = 128
+FAR = -1000000000.0
+VMEM = pltpu.VMEM
+
+
+def dot(left, right, dims=((1,), (0,))):
+    return lax.dot_general(left, right, (dims, ((), ())), preferred_element_type=jnp.float32)
+
+
+def head_lanes(size):
+    lane = lax.broadcasted_iota(jnp.int32, (1, PAIR), 1)
+    return [lane // size == index for index in range(PAIR // size)]
+
+
+def only(mask, values):
+    return jnp.where(mask, values, jnp.zeros_like(values))
+
+
+def attend_kernel(size, ids_row, ids_col, states, weight, bias, qkv, mixed):
+    local = mixed.shape[2]
+    projected = dot(states[0], weight[...]) + bias[...]
+    qkv[0] = projected.astype(jnp.bfloat16)
+    same = ids_col[0] == ids_row[0]
+    masks = head_lanes(size)
+    for pair in range(local // PAIR):
+        at = pair * PAIR
+        q = qkv[0, :, at : at + PAIR] * jnp.bfloat16(size**-0.5)
+        k = qkv[0, :, local + at : local + at + PAIR]
+        v = qkv[0, :, 2 * local + at : 2 * local + at + PAIR]
+        total = None
+        for mask in masks:
+            scores = jnp.where(same, dot(only(mask, k), q, ((1,), (1,))), FAR)
+            probs = jnp.exp(scores - jnp.max(scores, axis=0, keepdims=True))
+            scale = 1.0 / jnp.sum(probs, axis=0, keepdims=True)
+            low = (probs * scale).astype(jnp.bfloat16)
+            term = dot(only(mask, v), low, ((0,), (0,)))
+            total = term if total is None else total + term
+        mixed[0, :, at : at + PAIR] = total.T.astype(jnp.bfloat16)
+
+
+def attend_heads(states, weight, bias, ids, size):
+    packs, rows, width = states.shape
+    local = weight.shape[1] // 3
+    whole = lambda *shape: pl.BlockSpec(shape, lambda m: (0,) * len(shape))
+    block = lambda *shape: pl.BlockSpec((1,) + shape, lambda m: (m, 0, 0))
+    return pl.pallas_call(
+        functools.partial(attend_kernel, size),
+        grid=(packs,),
+        in_specs=[
+            block(1, rows),
+            block(rows, 1),
+            block(rows, width),
+            whole(width, 3 * local),
+            whole(1, 3 * local),
+        ],
+        out_specs=[block(rows, 3 * local), block(rows, local)],
+        out_shape=[
+            jax.ShapeDtypeStruct((packs, rows, 3 * local), jnp.bfloat16),
+            jax.ShapeDtypeStruct((packs, rows, local), jnp.bfloat16),
+        ],
+        compiler_params=pltpu.CompilerParams(vmem_limit_bytes=48 * 2**20),
+        name="attend_heads",
+    )(ids[:, None, :], ids[:, :, None], states, weight, bias)
+
+
+def attend_back_kernel(size, ids_row, ids_col, qkv, mixed_grad, weight, projected_grad, part):
+    local = mixed_grad.shape[2]
+    same = ids_col[0] == ids_row[0]
+    masks = head_lanes(size)
+    scale = jnp.bfloat16(size**-0.5)
+    for pair in range(local // PAIR):
+        at = pair * PAIR
+        q = qkv[0, :, at : at + PAIR] * scale
+        k = qkv[0, :, local + at : local + at + PAIR]
+        v = qkv[0, :, 2 * local + at : 2 * local + at + PAIR]
+        grad = mixed_grad[0, :, at : at + PAIR]
+        totals = [None] * 3
+        for mask in masks:
+            own_k = only(mask, k)
+            scores = jnp.where(same, dot(own_k, q, ((1,), (1,))), FAR)
+            probs = jnp.exp(scores - jnp.max(scores, axis=0, keepdims=True))
+            probs = probs * (1.0 / jnp.sum(probs, axis=0, keepdims=True))
+            prob_grad = dot(only(mask, v), grad, ((1,), (1,)))
+            inner = jnp.sum(probs * prob_grad, axis=0, keepdims=True)
+            score_grad = (probs * (prob_grad - inner)).astype(jnp.bfloat16)
+            terms = (
+                dot(own_k, score_grad, ((0,), (0,))),
+                dot(score_grad, only(mask, q)),
+                dot(probs.astype(jnp.bfloat16), only(mask, grad)),
+            )
+            totals = [t if o is None else o + t for o, t in zip(totals, terms)]
+        query_grad = totals[0].T * size**-0.5
+        projected_grad[0, :, at : at + PAIR] = query_grad.astype(jnp.bfloat16)
+        projected_grad[0, :, local + at : local + at + PAIR] = totals[1].astype(jnp.bfloat16)
+        projected_grad[0, :, 2 * local + at : 2 * local + at + PAIR] = totals[2].astype(
+            jnp.bfloat16
+        )
+    part[0] = dot(projected_grad[0], weight[...], ((1,), (1,))).astype(jnp.bfloat16)
+
+
+def attend_heads_back(qkv, mixed_grad, weight, ids, size):
+    packs, rows, local = mixed_grad.shape
+    width = weight.shape[0]
+    whole = lambda *shape: pl.BlockSpec(shape, lambda m: (0,) * len(shape))
+    block = lambda *shape: pl.BlockSpec((1,) + shape, lambda m: (m, 0, 0))
+    return pl.pallas_call(
+        functools.partial(attend_back_kernel, size),
+        grid=(packs,),
+        in_specs=[
+            block(1, rows),
+            block(rows, 1),
+            block(rows, 3 * local),
+            block(rows, local),
+            whole(width, 3 * local),
+        ],
+        out_specs=[block(rows, 3 * local), block(rows, width)],
+        out_shape=[
+            jax.ShapeDtypeStruct((packs, rows, 3 * local), jnp.bfloat16),
+            jax.ShapeDtypeStruct((packs, rows, width), jnp.bfloat16),
+        ],
+        compiler_params=pltpu.CompilerParams(vmem_limit_bytes=48 * 2**20),
+        name="attend_heads_back",
+    )(ids[:, None, :], ids[:, :, None], qkv, mixed_grad, weight)
+
+
+def normal_tail(values):
+    size = jnp.abs(values)
+    bell = jnp.exp(-0.5 * values * values)
+    t = 1.0 / (1.0 + 0.3275911 * (2.0**-0.5) * size)
+    poly = t * (
+        0.254829592
+        + t * (-0.284496736 + t * (1.421413741 + t * (-1.453152027 + t * 1.061405429)))
+    )
+    tail = 0.5 * poly * bell
+    return (jnp.where(values >= 0, 1.0 - tail, tail), bell)
+
+
+def gelu_both(values):
+    below, bell = normal_tail(values)
+    return (values * below, below + values * bell * 0.3989422804014327)
+
+
+def norm_parts(values):
+    center = jnp.mean(values, axis=-1, keepdims=True)
+    offset = values - center
+    spread = jnp.mean(offset * offset, axis=-1, keepdims=True)
+    inverse = lax.rsqrt(spread + 1e-05)
+    return (offset * inverse, inverse)
+
+
+def norm_back(grad, gain, normal, inverse):
+    inner = grad * gain
+    mean = jnp.mean(inner, axis=-1, keepdims=True)
+    along = jnp.mean(inner * normal, axis=-1, keepdims=True)
+    return inverse * (inner - mean - normal * along)
+
+
+def relay(boundary, lengths, valid, w_qkv, w_out, w_in, w_down, bias_in, vectors):
+    section_at = lax.axis_index("section")
+    count_ctx = lax.axis_size("ctx")
+    ctx_at = lax.axis_index("ctx")
+    wt_at = lax.axis_index("wt")
+    micro, rows, width = boundary.shape[1:]
+    pack = rows * count_ctx
+    size = width // HEADS
+    local = width // lax.axis_size("wt")
+    tokens = micro * rows
+    swap = [
+        (c * count_ctx + w, w * count_ctx + c) for c in range(count_ctx) for w in range(count_ctx)
+    ]
+
+    def swapped(block):
+        return lax.ppermute(block, ("ctx", "wt"), swap)
+
+    def gather_rows(block):
+        return lax.all_gather(block, "wt", axis=1, tiled=True)
+
+    def scatter_rows(block):
+        return lax.psum_scatter(block, "wt", scatter_dimension=1, tiled=True)
+
+    def rows_of_heads(block):
+        split = block.reshape(micro, count_ctx, rows, local)
+        return lax.all_to_all(split, "wt", 1, 3, tiled=True).reshape(tokens, width)
+
+    def heads_of_rows(block):
+        split = block.reshape(micro, 1, rows, width)
+        return lax.all_to_all(split, "wt", 3, 1, tiled=True).reshape(micro, pack, local)
+
+    own = swapped(boundary[0])
+    shard = w_qkv[0].reshape(local, 3, count_ctx, local)
+    weight_qkv = lax.all_to_all(shard, "wt", 2, 0, tiled=True).reshape(width, 3 * local)
+    weight_out = lax.all_gather(w_out[0], "wt", axis=0, tiled=True)
+    weight_in = lax.all_gather(w_in[0], "wt", axis=0, tiled=True)
+    weight_down = lax.all_gather(w_down[0], "wt", axis=0, tiled=True)
+    small = jnp.concatenate([vectors[0], bias_in[0].reshape(-1, local)], axis=0)
+    small = lax.all_gather(small, "wt", axis=0)
+    vector_rows = small[:, :8].transpose(1, 0, 2).reshape(8, width).astype(jnp.float32)
+    in_bias = small[:, 8:].reshape(-1).astype(jnp.float32)
+    own_rows = vectors[0].astype(jnp.float32)
+    qkv_bias = jnp.concatenate([own_rows[0], jnp.zeros((local,), jnp.float32), own_rows[1]])[None]
+    my_lengths = lax.dynamic_index_in_dim(lengths, ctx_at, 1, keepdims=False)
+    ids = jax.vmap(lambda row: dealt_ids(row, pack, count_ctx))(my_lengths)
+    marks = lax.all_gather(valid, ("wt", "ctx"), axis=1, tiled=True)
+    count = jnp.sum(marks.astype(jnp.float32))
+    at = (ctx_at * count_ctx + wt_at) * rows
+    marks = lax.dynamic_slice_in_dim(marks, at, rows, 1).reshape(tokens, 1).astype(jnp.float32)
+    factor = LOSS_SCALE / count
+
+    def forward(states):
+        full = gather_rows(states.reshape(micro, rows, width))
+        qkv, mixed = attend_heads(full, weight_qkv, qkv_bias, ids, size)
+        mixed = rows_of_heads(mixed)
+        summed = states.astype(jnp.float32) + (dot(mixed, weight_out) + vector_rows[2])
+        normal_one, inverse_one = norm_parts(summed)
+        first = normal_one * vector_rows[3] + vector_rows[4]
+        first_low = first.astype(jnp.bfloat16)
+        hidden, slope = gelu_both(dot(first_low, weight_in) + in_bias)
+        hidden = hidden.astype(jnp.bfloat16)
+        second = first + (dot(hidden, weight_down) + vector_rows[5])
+        normal_two, inverse_two = norm_parts(second)
+        output = normal_two * vector_rows[6] + vector_rows[7]
+        kept = (full, qkv, mixed, normal_one, inverse_one, first_low, hidden, slope)
+        return (output, kept + (normal_two, inverse_two))
+
+    def backward(grad, kept):
+        full, qkv, mixed, normal_one, inverse_one, first_low, hidden, slope = kept[:8]
+        normal_two, inverse_two = kept[8:]
+        grad_second = norm_back(grad, vector_rows[6], normal_two, inverse_two)
+        down_low = grad_second.astype(jnp.bfloat16)
+        pre_low = (dot(down_low, weight_down, ((1,), (1,))) * slope).astype(jnp.bfloat16)
+        grad_first = grad_second + dot(pre_low, weight_in, ((1,), (1,)))
+        grad_summed = norm_back(grad_first, vector_rows[3], normal_one, inverse_one)
+        branch_low = grad_summed.astype(jnp.bfloat16)
+        mixed_grad = dot(branch_low, weight_out, ((1,), (1,))).astype(jnp.bfloat16)
+        mixed_grad = heads_of_rows(mixed_grad)
+        projected_grad, part = attend_heads_back(qkv, mixed_grad, weight_qkv, ids, size)
+        grad_states = grad_summed + scatter_rows(part).reshape(tokens, width)
+
+        def weight_grads():
+            along = ((0,), (0,))
+            flat = projected_grad.reshape(-1, 3 * local)
+            total = lambda values: jnp.sum(values.astype(jnp.float32), axis=0)
+            bias_qkv = total(flat)
+            rows_local = jnp.stack([bias_qkv[:local], bias_qkv[2 * local :]])
+            rows_whole = jnp.stack(
+                [
+                    total(branch_low),
+                    total(grad_first * normal_one),
+                    total(grad_first),
+                    total(down_low),
+                    total(grad * normal_two),
+                    total(grad),
+                ]
+            )
+            return (
+                dot(full.reshape(-1, width), flat, along),
+                dot(mixed, branch_low, along),
+                dot(first_low, pre_low, along),
+                dot(hidden, down_low, along),
+                total(pre_low),
+                rows_local,
+                rows_whole,
+            )
+
+        return (grad_states, weight_grads)
+
+    states = own.reshape(tokens, width)
+    output, _ = forward(states)
+    arrived = shifted(output.astype(jnp.bfloat16), "section", 1)
+    states = jnp.where(section_at == 0, states, arrived)
+    output, kept = forward(states)
+    distance = output - own.reshape(tokens, width).astype(jnp.float32)
+    cotangent = factor * marks * distance
+    grad_states, _ = backward(cotangent, kept)
+    returned = shifted(grad_states.astype(jnp.bfloat16), "section", -1)
+    cotangent = jnp.where(section_at == 1, cotangent, returned.astype(jnp.float32))
+    grad_states, weight_grads = backward(cotangent, kept)
+    results = jnp.where(section_at == 0, grad_states, output).astype(jnp.bfloat16)
+    results = swapped(results.reshape(micro, rows, width))[None]
+    grads = weight_grads()
+    low = lambda part: part.astype(jnp.bfloat16)
+    qkv_back = low(grads[0]).reshape(count_ctx, local, 3, 1, local)
+    qkv_back = lax.all_to_all(qkv_back, "wt", 0, 3, tiled=True).reshape(local, 3 * width)
+    out_back, in_back, down_back = [
+        lax.psum_scatter(low(part), "wt", scatter_dimension=0, tiled=True) for part in grads[1:4]
+    ]
+    bias_back = lax.psum_scatter(grads[4], "wt", scatter_dimension=0, tiled=True)
+    whole_back = lax.psum_scatter(grads[6], "wt", scatter_dimension=1, tiled=True)
+    rows_back = jnp.concatenate([grads[5], whole_back])
+    shares = lax.psum((qkv_back, out_back, in_back, down_back, bias_back, rows_back), "ctx")
+    shares = tuple(part.astype(jnp.float32)[None] for part in shares)
+    return (results,) + shares
+
+
 def solution(mesh):
     in_specs = (
         P("section", None, ("wt", "ctx"), None),
@@ -397,4 +695,5 @@
         P("section", "wt"),
         P("section", None, "wt"),
     )
-    return jax.shard_map(shards, mesh=mesh, in_specs=in_specs, out_specs=out_specs, check_vma=False)
+    square = mesh.shape["ctx"] == mesh.shape["wt"]
+    return jax.shard_map(relay if square else shards, mesh=mesh, in_specs=in_specs, out_specs=out_specs, check_vma=False)

time: 1380 us -> 1060 us (0.77)
  waiting for transfers between devices: 821 us -> 578 us
  matrix products: 321 us -> 113 us
  blocking collectives: 57.9 us -> 170 us
  Pallas kernels: 0 us -> 55.7 us
  local copies, waits for them, and re-layouts: 80.6 us -> 49.5 us
  other arithmetic: 55.3 us -> 28.2 us
  starting transfers between devices: 17.6 us -> 37.9 us
    dot_general x72 -> x14, matrix products: 321 us -> 113 us  [dot(): lax.dot_general(left, right, (dims, ((), ())), preferred_element_type=jnp...]
    all_gather x8 -> x5, waiting for transfers between devices: 308 us -> 136 us  [the longest x1 59.7 us: relay(): weight_down = lax.all_gather(w_down[0], 'wt', axis=0, tiled=True)]
    unnamed x22 -> x12, waiting for transfers between devices: 140 us -> 2.08 us
    pallas_call x0 -> x4, Pallas kernels: none -> 55.7 us  [the longest x2 35.3 us: attend_heads_back(): pl.pallas_call(functools.partial(attend_back_kernel, size), grid=(packs,)...]
    all_gather x2, blocking collectives: 10.5 us -> 63.8 us  [the longest x1 32.2 us: relay(): small = lax.all_gather(small, 'wt', axis=0)]
    all_to_all x0 -> x4, waiting for transfers between devices: none -> 41.8 us  [the longest x1 31.4 us: relay(): lax.all_to_all(qkv_back, 'wt', 0, 3, tiled=True).reshape(local, 3 * width)]
    psum x1, waiting for transfers between devices: 214 us -> 177 us  [relay(): lax.psum((qkv_back, out_back, in_back, down_back, bias_back, rows_back),...]
    ppermute x0 -> x2, waiting for transfers between devices: none -> 36.3 us  [swapped(): return lax.ppermute(block, ('ctx', 'wt'), swap)]
  transfers between devices with their start and end apart: 24 -> 20, of which waited for: 22 -> 13; matrix products, arithmetic and copies ran while one was open for 14% -> 7% of each run, Pallas kernels for 0% -> 3%
where the time goes in v1:
time: 1060 us; the launch traced here: 1050 us
  waiting for transfers between devices  578 us (55%)
  blocking collectives  170 us (16%)
  matrix products  113 us (11%)
  Pallas kernels  55.7 us (5%)
  local copies, waits for them, and re-layouts  49.5 us (5%)
  starting transfers between devices  37.9 us (4%)
  other arithmetic  28.2 us (3%)
  between operations  16.4 us (2%)
    psum x1, waiting for transfers between devices, relay(): lax.psum((qkv_back, out_back, in_back, down_back, bias_back, rows_back),...  177 us
    dot_general x14, matrix products, dot(): lax.dot_general(left, right, (dims, ((), ())), preferred_element_type=jnp...  113 us
    reduce_scatter x2, waiting for transfers between devices, scatter_rows(): return lax.psum_scatter(block, 'wt', scatter_dimension=1, tiled=True)  76.1 us
    reduce_scatter x3, waiting for transfers between devices, relay(): lax.psum_scatter(low(part), 'wt', scatter_dimension=0, tiled=True)  71.9 us
    psum x1, blocking collectives, relay(): lax.psum((qkv_back, out_back, in_back, down_back, bias_back, rows_back),...  61.2 us
    all_gather x1, waiting for transfers between devices, relay(): weight_down = lax.all_gather(w_down[0], 'wt', axis=0, tiled=True)  59.7 us
    all_gather x1, waiting for transfers between devices, relay(): weight_in = lax.all_gather(w_in[0], 'wt', axis=0, tiled=True)  45.9 us
    ppermute x2, waiting for transfers between devices, shifted(): return lax.ppermute(block, axis, route)  36.6 us
  transfers between devices with their start and end apart: 20, of which 13 were waited for; matrix products, arithmetic and copies ran while one was open for 7% of the time, Pallas kernels for 3%

profile of v1, /device:TPU:4, one launch (start us, length us, event | category | flops | bytes accessed | tf_op | source)
XLA Modules:
  0.0 1049.3 jit_solution(7773248933353575274)
XLA Ops:
  11.7 36.3 %collective-permute-done = bf16[3,128,1024]{2,1,0:T(8,128)(2,1)S(1)} collective-permute-done((bf16[3,128,1024]{2,1,0:T(8,128)(2,1)}, bf16[3,128,1024]{2,1,0:T(8,128)(2,1)S(1)}, u32[]{:S(2)}, u32[]{:S(2)}) %collective-permute-start) | collective-permute-done | bytes 786464 | tf_op jit(solution)/shard_map/ppermute | solution.py:555
  59.1 32.2 %all-gather.4 = bf16[4,12,256]{2,1,0:T(8,128)(2,1)S(1)} all-gather(bf16[1,12,256]{2,1,0:T(8,128)(2,1)S(1)} %maximum_bitcast_fusion), channel_id=3, replica_groups=mesh['section'=2,'ctx'=4,'wt'=4] {'wt'}, dimensions={0}, use_global_device_ids=true | all-gather | bytes 30720 | tf_op jit(solution)/shard_map/all_gather | solution.py:578
  95.8 10.2 attend_heads.2
  112.3 10.4 all-to-all-done.1
  131.3 45.9 %all-gather.17.cloned.1.call-done = bf16[1,1024,4096]{2,1,0:T(8,128)(2,1)} async-done(((bf16[1,256,4096]{2,1,0:T(8,128)(2,1)}), bf16[1,1024,4096]{2,1,0:T(8,128)(2,1)}) %all-gather.17.cloned.1.call-update) | async-done | bytes 8388624 | tf_op jit(solution)/shard_map/all_gather | solution.py:575
  177.1 59.7 %all-gather.19.cloned.1.call-done = bf16[1,4096,1024]{2,1,0:T(8,128)(2,1)} async-done(((bf16[1,1024,1024]{2,1,0:T(8,128)(2,1)}), bf16[1,4096,1024]{2,1,0:T(8,128)(2,1)}) %all-gather.19.cloned.1.call-update) | async-done | bytes 8388624 | tf_op jit(solution)/shard_map/all_gather | solution.py:576
  236.8 16.9 %fusion.129 = (f32[384]{0:T(512)S(1)}, f32[384,1024]{1,0:T(8,128)}) fusion(f32[1024]{0:T(1024)S(1)} %bitcast.260, bf16[1,4096,1024]{2,1,0:T(8,128)(2,1)} %all-gather.19.cloned.1.call-done, bf16[1,1024,4096]{2,1,0:T(8,128)(2,1)} %all-gather.17.cloned.1.call-done, f32[4096]{0:T(1024)S(1)} %bitcast.248, f32[384,1024]{1,0:T(8,128)} %copy-done.19, ...), kind=kOutput, calls=%fused_computation.161 | convolution fusion | flops 6483344896 | bytes 19956224 | tf_op jit(solution)/shard_map/dot_general | solution.py:389
  261.8 16.2 %collective-permute-done.1 = bf16[384,1024]{1,0:T(8,128)(2,1)} collective-permute-done((bf16[384,1024]{1,0:T(8,128)(2,1)}, bf16[384,1024]{1,0:T(8,128)(2,1)}, u32[]{:S(2)}, u32[]{:S(2)}) %collective-permute-start.1) | collective-permute-done | bytes 786464 | tf_op jit(solution)/shard_map/ppermute | solution.py:17
  279.0 30.6 %all-gather.13.cloned.1.call-done.states = bf16[3,512,1024]{2,1,0:T(8,128)(2,1)} async-done(((bf16[3,128,1024]{2,1,0:T(8,128)(2,1)}), bf16[3,512,1024]{2,1,0:T(8,128)(2,1)}) %all-gather.13.cloned.1.call-update) | async-done | bytes 3145744 | tf_op jit(solution)/shard_map/all_gather | solution.py:558
  309.6 10.2 attend_heads.3
  322.2 5.9 all-to-all-start.2
  328.0 31.6 %all_gather.31 = s32[3,2048]{1,0:T(4,128)S(1)} all-gather(s32[3,128]{1,0:T(4,128)S(1)} %copy-done.24), channel_id=1, replica_groups=mesh['section'=2,'ctx'=4,'wt'=4] {'wt','ctx'}, dimensions={1}, use_global_device_ids=true | all-gather | bytes 26112 | tf_op jit(solution)/shard_map/all_gather | solution.py:585
  364.5 12.4 %multiply_convert_fusion.2 = (bf16[384,4096]{1,0:T(8,128)(2,1)S(1)}, f32[384,4096]{1,0:T(8,128)}) fusion(f32[4096]{0:T(1024)S(1)} %bitcast.249, bf16[1,1024,4096]{2,1,0:T(8,128)(2,1)} %all-gather.17.cloned.1.call-done, f32[1024]{0:T(1024)S(1)} %bitcast.257, f32[1024]{0:T(1024)S(1)} %bitcast.240, f32[384]{0:T(512)S(1)} %add_rsqrt_fusion.1, ...), kind=kOutput, calls=%fused_computation.34 | convolution fusion | flops 3259367424 | bytes 19426304 | tf_op jit(solution)/shard_map/dot_general | solution.py:389
  381.8 22.1 %fusion.124 = (f32[384]{0:T(512)S(1)}, f32[384]{0:T(512)S(1)}, f32[384,1024]{1,0:T(8,128)}) fusion(f32[384]{0:T(512)S(1)} %add_rsqrt_fusion.1, f32[384,1024]{1,0:T(8,128)} %copy-done.10, f32[384]{0:T(512)S(1)} %broadcast_multiply_fusion.9, f32[1024]{0:T(1024)S(1)} %bitcast.242, bf16[1,1024,4096]{2,1,0:T(8,128)(2,1)} %all-gather.17.cloned.1.call-done, ...), kind=kOutput, calls=%fused_computation.156 | convolution fusion | flops 6495927296 | bytes 28616192 | tf_op jit(solution)/shard_map/dot_general | solution.py:389
  410.2 17.1 %all_to_all.90 = bf16[3,1,128,1024]{2,0,1,3:T(4,128)(2,1)S(1)} all-to-all(bf16[3,1,128,1024]{2,0,1,3:T(4,128)(2,1)S(1)} %copy.126), channel_id=1, replica_groups=mesh['section'=2,'ctx'=4,'wt'=4] {'wt'}, dimensions={3} | all-to-all | bytes 1572864 | tf_op jit(solution)/shard_map/all_to_all | solution.py:569
  429.6 17.5 %attend_heads_back.2 = (bf16[3,512,768]{2,1,0:T(8,128)(2,1)}, bf16[3,512,1024]{2,1,0:T(8,128)(2,1)}) custom-call(s32[3,1,512]{2,1,0:T(1,128)S(1)} %bitcast.200, s32[3,512,1]{2,1,0:T(8,128)S(1)} %reshape.235.ids_col, bf16[3,512,768]{2,1,0:T(8,128)(2,1)} %copy-done.2, bf16[3,512,256]{2,1,0:T(8,128)(2,1)S(1)} %bitcast.195, bf16[1024,768]{1,0:T(8,128)(2,1)S(1)} %bitcast.192), custom_call_target="tpu_custom_call" | custom-call | tf_op jit(solution)/shard_map/attend_heads_back/pallas_call | solution.py:488
  447.3 35.3 %reduce-scatter.7.cloned.1.call-done = bf16[3,128,1024]{2,1,0:T(8,128)(2,1)} async-done(((bf16[3,512,1024]{2,1,0:T(8,128)(2,1)}), bf16[3,128,1024]{2,1,0:T(8,128)(2,1)}) %reduce-scatter.7.cloned.1.call-update) | async-done | bytes 786448 | tf_op jit(solution)/shard_map/reduce_scatter | solution.py:561
  487.4 20.3 %collective-permute-done.2 = bf16[384,1024]{1,0:T(8,128)(2,1)} collective-permute-done((bf16[384,1024]{1,0:T(8,128)(2,1)}, bf16[384,1024]{1,0:T(8,128)(2,1)}, u32[]{:S(2)}, u32[]{:S(2)}) %collective-permute-start.2) | collective-permute-done | bytes 786464 | tf_op jit(solution)/shard_map/ppermute | solution.py:17
  512.8 12.4 %convert_reduce_fusion = (f32[4096]{0:T(1024)S(1)}, bf16[384,4096]{1,0:T(8,128)(2,1)S(1)}) fusion(f32[384,4096]{1,0:T(8,128)} %get-tuple-element.86, f32[4096]{0:T(1024)S(1)} %bitcast.251, bf16[1,4096,1024]{2,1,0:T(8,128)(2,1)} %all-gather.19.cloned.1.call-done, f32[384,1024]{1,0:T(8,128)S(1)} %get-tuple-element.66), kind=kOutput, calls=%fused_computation.31 | convolution fusion | flops 3265654784 | bytes 19431424 | tf_op jit(solution)/shard_map/dot_general | solution.py:389
  534.0 10.2 convolution_convert_fusion
  544.3 10.3 convolution_convert_fusion.1
  560.4 16.9 %all_to_all.91 = bf16[3,1,128,1024]{2,0,1,3:T(4,128)(2,1)S(1)} all-to-all(bf16[3,1,128,1024]{2,0,1,3:T(4,128)(2,1)S(1)} %copy.131), channel_id=1, replica_groups=mesh['section'=2,'ctx'=4,'wt'=4] {'wt'}, dimensions={3} | all-to-all | bytes 1572864 | tf_op jit(solution)/shard_map/all_to_all | solution.py:569
  579.8 17.8 %attend_heads_back.3 = (bf16[3,512,768]{2,1,0:T(8,128)(2,1)S(1)}, bf16[3,512,1024]{2,1,0:T(8,128)(2,1)}) custom-call(s32[3,1,512]{2,1,0:T(1,128)S(1)} %bitcast.201, s32[3,512,1]{2,1,0:T(8,128)S(1)} %reshape.235.ids_col, bf16[3,512,768]{2,1,0:T(8,128)(2,1)} %copy-done.2, bf16[3,512,256]{2,1,0:T(8,128)(2,1)S(1)} %bitcast.194, bf16[1024,768]{1,0:T(8,128)(2,1)S(1)} %bitcast.193), custom_call_target="tpu_custom_call" | custom-call | tf_op jit(solution)/shard_map/attend_heads_back/pallas_call | solution.py:488
  600.7 5.7 bitcast_convert_fusion
  615.8 5.9 all-to-all-start.5
  622.5 31.4 %all-to-all-done.5 = bf16[4,256,3,1,256]{1,4,2,3,0:T(8,128)(2,1)} async-done(((bf16[4,256,3,1,256]{1,4,2,3,0:T(8,128)(2,1)}), bf16[4,256,3,1,256]{1,4,2,3,0:T(8,128)(2,1)}, u32[]{:S(2)}, u32[]{:S(2)}) %all-to-all-start.5) | async-done | bytes 1572896 | tf_op jit(solution)/shard_map/all_to_all | solution.py:665
  656.6 71.9 %reduce-scatter.13.cloned.1.call-done = bf16[256,4096]{1,0:T(8,128)(2,1)} async-done(((bf16[1024,4096]{1,0:T(8,128)(2,1)}), bf16[256,4096]{1,0:T(8,128)(2,1)}) %reduce-scatter.13.cloned.1.call-update) | async-done | bytes 2097168 | tf_op jit(solution)/shard_map/reduce_scatter | solution.py:667
  728.5 40.9 %reduce-scatter.9.cloned.1.call-done = bf16[3,128,1024]{2,1,0:T(8,128)(2,1)} async-done(((bf16[3,512,1024]{2,1,0:T(8,128)(2,1)}), bf16[3,128,1024]{2,1,0:T(8,128)(2,1)}) %reduce-scatter.9.cloned.1.call-update) | async-done | bytes 786448 | tf_op jit(solution)/shard_map/reduce_scatter | solution.py:561
  772.8 5.5 collective-permute-start.3
  779.6 11.1 %all-reduce = f32[4096]{0:T(1024)S(1)} all-reduce(f32[4096]{0:T(1024)S(1)} %get-tuple-element.91), channel_id=11, replica_groups=mesh['section'=2,'ctx'=4,'wt'=4] {'wt'}, use_global_device_ids=true, to_apply=%region_29.30.clone | all-reduce | flops 4096 | bytes 32768
  792.4 61.2 %all-reduce.1 = (f32[1,1024]{1,0:T(1,128)}, f32[1,8,256]{2,1,0:T(8,128)}) all-reduce(f32[1,1024]{1,0:T(1,128)S(1)} %bitcast.247, f32[1,8,256]{2,1,0:T(8,128)S(1)} %maximum_bitcast_fusion.1), channel_id=1, replica_groups=mesh['section'=2,'ctx'=4,'wt'=4] {'ctx'}, use_global_device_ids=true, to_apply=%region_30.31 | all-reduce | flops 3072 | bytes 24576 | tf_op jit(solution)/shard_map/psum | solution.py:672
  853.7 176.8 %all-reduce.5.cloned.1.call-done = (bf16[1,256,3072]{1,2,0:T(8,128)(2,1)}, bf16[1,256,1024]{2,1,0:T(8,128)(2,1)}, bf16[1,256,4096]{2,1,0:T(8,128)(2,1)}, bf16[1,1024,1024]{2,1,0:T(8,128)(2,1)}) async-done(((bf16[1,256,3072]{1,2,0:T(8,128)(2,1)}, bf16[1,256,1024]{2,1,0:T(8,128)(2,1)}, bf16[1,256,4096]{2,1,0:T(8,128)(2,1)}, bf16[1,1024,1024]{2,1,0:T(8,128)(2,1)}), (bf16[1,256,3072]{1,2,0:T(8,128)(2,1)}, ...) | async-done | bytes 6291472 | tf_op jit(solution)/shard_map/psum | solution.py:672
  (190 shorter events, 124.3 us)
Async XLA Ops:
  7.2 50.5 %copy-start = (s32[3,4,4]{2,1,0:T(4,128)S(1)}, s32[3,4,4]{2,1,0:T(4,128)}, u32[]{:S(2)}) copy-start(s32[3,4,4]{2,1,0:T(4,128)} %param.10) | copy-start | bytes 580
  7.2 88.6 %all-gather.11.cloned.1.call-start = ((), (), s32[]{:S(2)}) async-start(), calls=%async_computation.12 | async-start | bytes 3932160 | tf_op jit(solution)/shard_map/all_gather | solution.py:558
  7.2 40.7 %collective-permute-start = (bf16[3,128,1024]{2,1,0:T(8,128)(2,1)}, bf16[3,128,1024]{2,1,0:T(8,128)(2,1)S(1)}, u32[]{:S(2)}, u32[]{:S(2)}) collective-permute-start(bf16[3,128,1024]{2,1,0:T(8,128)(2,1)} %bitcast.272), channel_id=1, source_target_pairs={{0,0},{1,4},{2,8},{3,12},{4,1},{5,5},{6,9},{7,13},{8,2},{9,6},{10,... | collective-permute-start | bytes 2359304 | tf_op jit(solution)/shard_map/ppermute | solution.py:555
  48.8 77.7 %all-gather.15.cloned.1.call-start = ((), (), s32[]{:S(2)}) async-start(), calls=%async_computation.20 | async-start | bytes 2621440 | tf_op jit(solution)/shard_map/all_gather | solution.py:574
  49.6 127.5 %all-gather.17.cloned.1.call-start = ((), (), s32[]{:S(2)}) async-start(), calls=%async_computation.21 | async-start | bytes 10485760 | tf_op jit(solution)/shard_map/all_gather | solution.py:575
  50.3 186.5 %all-gather.19.cloned.1.call-start = ((), (), s32[]{:S(2)}) async-start(), calls=%async_computation.22 | async-start | bytes 10485760 | tf_op jit(solution)/shard_map/all_gather | solution.py:576
  53.9 37.4 %all-to-all-start = ((bf16[256,3,4,256]{0,3,1,2:T(8,128)(2,1)}), bf16[256,3,4,256]{0,3,1,2:T(8,128)(2,1)S(1)}, u32[]{:S(2)}, u32[]{:S(2)}) async-start(bf16[256,3,4,256]{0,3,1,2:T(8,128)(2,1)} %copy.116), calls=%async_computation | async-start | bytes 3145728 | tf_op jit(solution)/shard_map/all_to_all | solution.py:573
  106.9 15.9 %all-to-all-start.1 = ((bf16[3,4,128,256]{3,2,0,1:T(8,128)(2,1)}), bf16[3,4,128,256]{3,2,0,1:T(8,128)(2,1)S(1)}, u32[]{:S(2)}, u32[]{:S(2)}) async-start(bf16[3,4,128,256]{3,2,0,1:T(8,128)(2,1)} %copy.120), calls=%async_computation.1 | async-start | bytes 1572864 | tf_op jit(solution)/shard_map/all_to_all | solution.py:565
  112.0 197.5 %all-gather.13.cloned.1.call-start = ((), (), s32[]{:S(2)}) async-start(), calls=%async_computation.13 | async-start | bytes 3932160 | tf_op jit(solution)/shard_map/all_gather | solution.py:558
  256.9 21.1 %collective-permute-start.1 = (bf16[384,1024]{1,0:T(8,128)(2,1)}, bf16[384,1024]{1,0:T(8,128)(2,1)}, u32[]{:S(2)}, u32[]{:S(2)}) collective-permute-start(bf16[384,1024]{1,0:T(8,128)(2,1)} %add_convert_fusion), channel_id=1, source_target_pairs={{0,16},{1,17},{2,18},{3,19},{4,20},{5,21},{6,22},{7,23},{8,24},{9,... | collective-permute-start | bytes 2359304 | tf_op jit(solution)/shard_map/ppermute | solution.py:17
  321.2 6.8 copy-start.24
  322.2 38.8 %all-to-all-start.2 = ((bf16[3,4,128,256]{3,2,0,1:T(8,128)(2,1)}), bf16[3,4,128,256]{3,2,0,1:T(8,128)(2,1)}, u32[]{:S(2)}, u32[]{:S(2)}) async-start(bf16[3,4,128,256]{3,2,0,1:T(8,128)(2,1)} %copy.124), calls=%async_computation.2 | async-start | bytes 1572864 | tf_op jit(solution)/shard_map/all_to_all | solution.py:565
  328.0 154.5 %reduce-scatter.7.cloned.1.call-start = ((), (), s32[]{:S(2)}) async-start(), calls=%async_computation.14 | async-start | bytes 3932160 | tf_op jit(solution)/shard_map/reduce_scatter | solution.py:561
  363.1 13.9 %slice-start.2 = ((s8[8388608]{0:T(1024)(128)(4,1)}), s8[4194304]{0:T(1024)(128)(4,1)S(1)}, s32[]{:S(2)}) async-start(s8[8388608]{0:T(1024)(128)(4,1)} %bitcast.270), calls=%async_computation.26 | async-start | bytes 8388608
  364.2 12.8 %copy-start.10 = (f32[384,1024]{1,0:T(8,128)}, f32[384,1024]{1,0:T(8,128)S(1)}, u32[]{:S(2)}) copy-start(f32[384,1024]{1,0:T(8,128)S(1)} %get-tuple-element.84) | copy-start | bytes 4718596
  364.5 12.4 %slice-start.3 = ((s8[8388608]{0:T(1024)(128)(4,1)}), s8[4194304]{0:T(1024)(128)(4,1)S(1)}, s32[]{:S(2)}) async-start(s8[8388608]{0:T(1024)(128)(4,1)} %bitcast.270), calls=%async_computation.27 | async-start | bytes 8388608
  447.2 60.5 %copy-start.9 = (bf16[3,128,1024]{2,1,0:T(8,128)(2,1)S(1)}, bf16[3,128,1024]{2,1,0:T(8,128)(2,1)}, u32[]{:S(2)}) copy-start(bf16[3,128,1024]{2,1,0:T(8,128)(2,1)} %copy-done.7) | copy-start | bytes 2359300
  447.2 209.3 %reduce-scatter.11.cloned.1.call-start = ((), (), s32[]{:S(2)}) async-start(), calls=%async_computation.16 | async-start | bytes 2621440 | tf_op jit(solution)/shard_map/reduce_scatter | solution.py:667
  486.1 21.6 %collective-permute-start.2 = (bf16[384,1024]{1,0:T(8,128)(2,1)}, bf16[384,1024]{1,0:T(8,128)(2,1)}, u32[]{:S(2)}, u32[]{:S(2)}) collective-permute-start(bf16[384,1024]{1,0:T(8,128)(2,1)} %fusion.55), channel_id=1, source_target_pairs={{16,0},{17,1},{18,2},{19,3},{20,4},{21,5},{22,6},{23,7},{24,8},{25... | collective-permute-start | bytes 2359304 | tf_op jit(solution)/shard_map/ppermute | solution.py:17
  487.4 23.2 %copy-start.6 = (f32[384,1024]{1,0:T(8,128)S(1)}, f32[384,1024]{1,0:T(8,128)}, u32[]{:S(2)}) copy-start(f32[384,1024]{1,0:T(8,128)} %copy-done.5) | copy-start | bytes 4718596
  510.5 14.7 %slice-start = ((s8[8388608]{0:T(1024)(128)(4,1)}), s8[4194304]{0:T(1024)(128)(4,1)S(1)}, s32[]{:S(2)}) async-start(s8[8388608]{0:T(1024)(128)(4,1)} %bitcast.268), calls=%async_computation.24 | async-start | bytes 8388608
  512.7 12.5 %copy-start.20 = (f32[384,1024]{1,0:T(8,128)}, f32[384,1024]{1,0:T(8,128)S(1)}, u32[]{:S(2)}) copy-start(f32[384,1024]{1,0:T(8,128)S(1)} %get-tuple-element.66) | copy-start | bytes 4718596
  512.7 12.5 %copy-start.11 = (f32[384,1024]{1,0:T(8,128)S(1)}, f32[384,1024]{1,0:T(8,128)}, u32[]{:S(2)}) copy-start(f32[384,1024]{1,0:T(8,128)} %copy-done.10) | copy-start | bytes 4718596
  512.7 12.5 %slice-start.1 = ((s8[8388608]{0:T(1024)(128)(4,1)}), s8[4194304]{0:T(1024)(128)(4,1)S(1)}, s32[]{:S(2)}) async-start(s8[8388608]{0:T(1024)(128)(4,1)} %bitcast.268), calls=%async_computation.25 | async-start | bytes 8388608
  533.5 123.1 %reduce-scatter.15.cloned.1.call-start = ((), (), s32[]{:S(2)}) async-start(), calls=%async_computation.18 | async-start | bytes 10485760 | tf_op jit(solution)/shard_map/reduce_scatter | solution.py:667
  544.3 184.2 %reduce-scatter.13.cloned.1.call-start = ((), (), s32[]{:S(2)}) async-start(), calls=%async_computation.17 | async-start | bytes 10485760 | tf_op jit(solution)/shard_map/reduce_scatter | solution.py:667
  554.6 214.8 %reduce-scatter.9.cloned.1.call-start = ((), (), s32[]{:S(2)}) async-start(), calls=%async_computation.15 | async-start | bytes 3932160 | tf_op jit(solution)/shard_map/reduce_scatter | solution.py:561
  615.8 38.1 %all-to-all-start.5 = ((bf16[4,256,3,1,256]{1,4,2,3,0:T(8,128)(2,1)}), bf16[4,256,3,1,256]{1,4,2,3,0:T(8,128)(2,1)}, u32[]{:S(2)}, u32[]{:S(2)}) async-start(bf16[4,256,3,1,256]{1,4,2,3,0:T(8,128)(2,1)} %copy.138), calls=%async_computation.7 | async-start | bytes 3145728 | tf_op jit(solution)/shard_map/all_to_all | solution.py:665
  621.7 170.0 %reduce-scatter.17.cloned.1.call-start = ((), (), s32[]{:S(2)}) async-start(), calls=%async_computation.19 | async-start | bytes 40960 | tf_op jit(solution)/shard_map/reduce_scatter | solution.py:670
  622.5 408.0 %all-reduce.5.cloned.1.call-start = ((), (), s32[]{:S(2)}) async-start(), calls=%async_computation.23 | async-start | bytes 12582912 | tf_op jit(solution)/shard_map/psum | solution.py:672
  728.5 49.8 %copy-start.26 = (u32[32]{0:T(128)S(1)}, u32[32]{0:T(128)}, u32[]{:S(2)}) copy-start(u32[32]{0:T(128)} %constant.85) | copy-start | bytes 388
  772.8 80.8 %collective-permute-start.3 = (bf16[3,128,1024]{2,1,0:T(8,128)(2,1)}, bf16[3,128,1024]{2,1,0:T(8,128)(2,1)S(1)}, u32[]{:S(2)}, u32[]{:S(2)}) collective-permute-start(bf16[3,128,1024]{2,1,0:T(8,128)(2,1)} %bitcast.39), channel_id=1, source_target_pairs={{0,0},{1,4},{2,8},{3,12},{4,1},{5,5},{6,9},{7,13},{8,2},{9,6},{10,... | collective-permute-start | bytes 2359304 | tf_op jit(solution)/shard_map/ppermute | solution.py:555
  (21 other events, 48.8 us)
Sparse Core Ops, SparseCore 0:
  49.0 40.5 all-gather.10
  91.1 25.4 all-gather.14
  118.2 58.9 all-gather.16
  178.5 58.2 all-gather.18
  279.1 30.4 all-gather.12
  447.3 35.1 reduce-scatter.6
  533.6 30.3 reduce-scatter.10
  566.6 85.3 reduce-scatter.14
  654.8 73.6 reduce-scatter.12
  731.4 37.9 reduce-scatter.8
  772.5 19.1 reduce-scatter.16
  794.8 235.5 all-reduce.4

commit v2 on v1

--- a/solution.py
+++ b/solution.py
@@ -382,7 +382,7 @@
 
 PAIR = 128
 FAR = -1000000000.0
-VMEM = pltpu.VMEM
+MESH = pl.DeviceIdType.MESH
 
 
 def dot(left, right, dims=((1,), (0,))):
@@ -537,6 +537,296 @@
     return inverse * (inner - mean - normal * along)
 
 
+CHUNK = 128
+
+
+def sum_into(target, parts, rows):
+    step = 16
+
+    def one(index, carry):
+        at = pl.ds(pl.multiple_of(index * step, step), step)
+        total = parts[0][at, :].astype(jnp.float32)
+        for part in parts[1:]:
+            total = total + part[at, :].astype(jnp.float32)
+        target[at, :] = total.astype(jnp.bfloat16)
+        return carry
+
+    lax.fori_loop(0, rows // step, one, 0)
+
+
+def chunk_list(local, width, hidden):
+    down = [("down", index) for index in range(hidden // 4 // CHUNK)]
+    across = [
+        ("in", (half, column))
+        for column in range(hidden // width)
+        for half in range(local // CHUNK)
+    ]
+    out = [("out", half) for half in range(local // CHUNK)]
+    qkv = [("qkv", (half, part)) for part in range(3) for half in range(local // CHUNK)]
+    return down + across + out + [("rest", 0)] + qkv
+
+
+def reduce_kernel(chunks, local, width, hidden, grads, results, buffers, sems):
+    near, far, near_in, far_in, across_in, up_in, side_in, total = buffers
+    load, load_far, near_send, near_recv, far_send, far_recv = sems[:6]
+    across_send, across_recv, up_send, up_recv, side_recv = sems[6:11]
+    down_send, down_recv, keep, piece_send, piece_recv = sems[11:]
+    z = lax.axis_index("ctx")
+    w = lax.axis_index("wt")
+    core = lax.rem(w, 2)
+    sibling = w + 1 - 2 * core
+    across = lax.rem(w + 2, 4)
+    across_sibling = lax.rem(sibling + 2, 4)
+    partners = (sibling, across, across_sibling)
+
+    barrier = pltpu.get_barrier_semaphore()
+    for partner in partners:
+        pl.semaphore_signal(barrier, 1, device_id={"wt": partner}, device_id_type=MESH)
+
+    @pl.when(z > 0)
+    def _():
+        pl.semaphore_signal(barrier, 1, device_id={"ctx": z - 1}, device_id_type=MESH)
+
+    @pl.when(z < 3)
+    def _():
+        pl.semaphore_signal(barrier, 1, device_id={"ctx": z + 1}, device_id_type=MESH)
+
+    pl.semaphore_wait(barrier, 3 + (z > 0).astype(jnp.int32) + (z < 3).astype(jnp.int32))
+
+    def rows_of(k):
+        return 16 if chunks[k][0] == "rest" else CHUNK
+
+    def is_piece(k):
+        return chunks[k][0] == "qkv"
+
+    def source(k, j):
+        kind, at = chunks[k]
+        if kind == "down":
+            return grads["down"].at[pl.ds(j * (hidden // 4) + at * CHUNK, CHUNK), :]
+        if kind == "in":
+            half, column = at
+            return grads["in"].at[
+                pl.ds(j * local + half * CHUNK, CHUNK), pl.ds(column * width, width)
+            ]
+        if kind == "out":
+            return grads["out"].at[pl.ds(j * local + at * CHUNK, CHUNK), :]
+        if kind == "rest":
+            return grads["rest"].at[pl.ds(j * 16, 16), :]
+        half, part = at
+        return grads["qkv"].at[
+            pl.ds(j * local + half * CHUNK, CHUNK), pl.ds(part * local, local)
+        ]
+
+    def result(k):
+        kind, at = chunks[k]
+        if kind == "down":
+            return results["down"].at[pl.ds(at * CHUNK, CHUNK), :]
+        if kind == "out":
+            return results["out"].at[pl.ds(at * CHUNK, CHUNK), :]
+        if kind == "rest":
+            return results["rest"]
+        half, column = at
+        return results[kind].at[pl.ds(half * CHUNK, CHUNK), pl.ds(column * width, width)]
+
+    def slot(buffer, k):
+        return buffer.at[k, pl.ds(0, rows_of(k)), :]
+
+    def remote(source_ref, target_ref, send, recv, **where):
+        return pltpu.make_async_remote_copy(
+            source_ref, target_ref, send, recv, device_id=where, device_id_type=MESH
+        )
+
+    def near_load(k):
+        if is_piece(k):
+            place = near.at[k, :, pl.ds(w * local, local)]
+            return pltpu.make_async_copy(source(k, w), place, load.at[k])
+        return pltpu.make_async_copy(source(k, w), slot(near, k), load.at[k])
+
+    def far_load(k):
+        return pltpu.make_async_copy(source(k, across), slot(far, k), load_far.at[k])
+
+    def near_copy(k):
+        return remote(
+            source(k, sibling), slot(near_in, k), near_send.at[k], near_recv.at[k], wt=sibling
+        )
+
+    def far_copy(k):
+        return remote(
+            source(k, across_sibling), slot(far_in, k), far_send.at[k], far_recv.at[k], wt=sibling
+        )
+
+    def piece_copy(k, index):
+        place = near.at[k, :, pl.ds(w * local, local)]
+        at = piece_send.at[k, index], piece_recv.at[k, index]
+        return remote(source(k, partners[index]), place, *at, wt=partners[index])
+
+    def across_copy(k):
+        return remote(
+            slot(far, k), slot(across_in, k), across_send.at[k], across_recv.at[k], wt=across
+        )
+
+    def place_of(k, role):
+        return role if k % 2 == 0 else 3 - role
+
+    def up_copy(k, role):
+        target = place_of(k, 1 if role == 0 else 2)
+        return remote(slot(total, k), slot(up_in, k), up_send.at[k], up_recv.at[k], ctx=target)
+
+    def side_copy(k):
+        return remote(
+            slot(total, k), slot(side_in, k), up_send.at[k], side_recv.at[k], ctx=place_of(k, 1)
+        )
+
+    def down_copy(k, role):
+        origin = result(k) if role == 3 else slot(total, k)
+        at = down_send.at[k, 1 if role == 2 else 0]
+        return remote(origin, result(k), at, down_recv.at[k], ctx=place_of(k, role))
+
+    def keep_copy(k):
+        return pltpu.make_async_copy(slot(total, k), result(k), keep.at[k])
+
+    def on(k, role, step):
+        pl.when(z == place_of(k, role))(step)
+
+    def summands(k):
+        if is_piece(k):
+            return [slot(near, k)]
+        return [slot(near, k), slot(near_in, k), slot(across_in, k)]
+
+    count = len(chunks)
+    for k in range(count):
+        if not is_piece(k):
+            far_copy(k).start()
+            far_load(k).start()
+            near_copy(k).start()
+            near_load(k).start()
+
+    def begin(k):
+        if is_piece(k):
+            near_load(k).start()
+            for index in range(3):
+                piece_copy(k, index).start()
+            return
+        far_load(k).wait()
+        far_copy(k).wait_recv()
+        sum_into(slot(far, k), [slot(far, k), slot(far_in, k)], rows_of(k))
+        across_copy(k).start()
+
+    def settle(k):
+        near_load(k).wait()
+        if is_piece(k):
+            for index in range(3):
+                piece_copy(k, index).wait_recv()
+        else:
+            near_copy(k).wait_recv()
+            across_copy(k).wait_recv()
+        for role in (0, 3):
+
+            def step(role=role):
+                sum_into(slot(total, k), summands(k), rows_of(k))
+                up_copy(k, role).start()
+
+            on(k, role, step)
+
+    def aside(k):
+        def step():
+            up_copy(k, 3).wait_recv()
+            sum_into(slot(total, k), summands(k) + [slot(up_in, k)], rows_of(k))
+            side_copy(k).start()
+
+        on(k, 2, step)
+
+    def finish(k):
+        def step():
+            up_copy(k, 0).wait_recv()
+            side_copy(k).wait_recv()
+            parts = summands(k) + [slot(up_in, k), slot(side_in, k)]
+            sum_into(slot(total, k), parts, rows_of(k))
+            down_copy(k, 0).start()
+            down_copy(k, 2).start()
+            keep_copy(k).start()
+
+        on(k, 1, step)
+
+    def forward(k):
+        def step():
+            down_copy(k, 2).wait_recv()
+            down_copy(k, 3).start()
+
+        on(k, 2, step)
+
+    stages = (begin, settle, aside, finish, forward)
+    for tick in range(count + len(stages) - 1):
+        for lag, stage in enumerate(stages):
+            if 0 <= tick - lag < count:
+                stage(tick - lag)
+    for k in range(count):
+        if is_piece(k):
+            for index in range(3):
+                piece_copy(k, index).wait_send()
+        else:
+            far_copy(k).wait_send()
+            near_copy(k).wait_send()
+            across_copy(k).wait_send()
+
+        def ends(role):
+            up_copy(k, role).wait_send()
+            down_copy(k, role).wait_recv()
+
+        def middle():
+            side_copy(k).wait_send()
+            down_copy(k, 3).wait_send()
+
+        def owner():
+            down_copy(k, 0).wait_send()
+            down_copy(k, 2).wait_send()
+            keep_copy(k).wait()
+
+        on(k, 0, lambda: ends(0))
+        on(k, 3, lambda: ends(3))
+        on(k, 2, middle)
+        on(k, 1, owner)
+
+
+def reduce_grads(grad_qkv, grad_out, grad_in, grad_down, rest):
+    width = grad_out.shape[0]
+    hidden = grad_down.shape[0]
+    local = width // 4
+    chunks = chunk_list(local, width, hidden)
+    count = len(chunks)
+
+    def body(*refs):
+        grads = dict(zip(("qkv", "out", "in", "down", "rest"), refs[:5]))
+        results = dict(zip(("qkv", "out", "in", "down", "rest"), refs[5:10]))
+        reduce_kernel(chunks, local, width, hidden, grads, results, refs[10:18], refs[18:])
+
+    shapes = [
+        (local, 3 * width),
+        (local, width),
+        (local, hidden),
+        (hidden // 4, width),
+        (16, width),
+    ]
+    dma = pltpu.SemaphoreType.DMA
+    whole = [pltpu.VMEM((count, CHUNK, width), jnp.bfloat16)]
+    direct = [pltpu.VMEM((count - 6, CHUNK, width), jnp.bfloat16)]
+    return pl.pallas_call(
+        body,
+        in_specs=[pl.BlockSpec(memory_space=pl.ANY)] * 5,
+        out_specs=[pl.BlockSpec(memory_space=pl.ANY)] * 5,
+        out_shape=[jax.ShapeDtypeStruct(shape, jnp.bfloat16) for shape in shapes],
+        scratch_shapes=whole
+        + direct * 4
+        + whole * 3
+        + [dma((count,))] * 11
+        + [dma((count, 2)), dma((count,)), dma((count,)), dma((count, 3)), dma((count, 3))],
+        compiler_params=pltpu.CompilerParams(
+            collective_id=1, has_side_effects=True, vmem_limit_bytes=60 * 2**20
+        ),
+        name="reduce_grads",
+    )(grad_qkv, grad_out, grad_in, grad_down, rest)
+
+
 def relay(boundary, lengths, valid, w_qkv, w_out, w_in, w_down, bias_in, vectors):
     section_at = lax.axis_index("section")
     count_ctx = lax.axis_size("ctx")
@@ -661,17 +951,19 @@
     results = swapped(results.reshape(micro, rows, width))[None]
     grads = weight_grads()
     low = lambda part: part.astype(jnp.bfloat16)
-    qkv_back = low(grads[0]).reshape(count_ctx, local, 3, 1, local)
-    qkv_back = lax.all_to_all(qkv_back, "wt", 0, 3, tiled=True).reshape(local, 3 * width)
-    out_back, in_back, down_back = [
-        lax.psum_scatter(low(part), "wt", scatter_dimension=0, tiled=True) for part in grads[1:4]
-    ]
-    bias_back = lax.psum_scatter(grads[4], "wt", scatter_dimension=0, tiled=True)
-    whole_back = lax.psum_scatter(grads[6], "wt", scatter_dimension=1, tiled=True)
-    rows_back = jnp.concatenate([grads[5], whole_back])
-    shares = lax.psum((qkv_back, out_back, in_back, down_back, bias_back, rows_back), "ctx")
-    shares = tuple(part.astype(jnp.float32)[None] for part in shares)
-    return (results,) + shares
+    mine = (jnp.arange(4) == wt_at).astype(jnp.float32)[None, :, None]
+    rest = jnp.concatenate([grads[5][:, None, :] * mine, grads[6].reshape(6, 4, local)])
+    rest = jnp.concatenate([rest, jnp.zeros((8, 4, local), jnp.float32)])
+    rest = rest.transpose(1, 0, 2)
+    in_rows = jnp.zeros((4, 16, local), jnp.float32)
+    in_rows = in_rows.at[:, :4].set(grads[4].reshape(4, -1, local))
+    rest = jnp.concatenate([rest, in_rows, jnp.zeros((4, 16, 2 * local), jnp.float32)], axis=2)
+    rest = rest.reshape(64, width)
+    sums = reduce_grads(*[low(part) for part in grads[:4]], low(rest))
+    sums = [part.astype(jnp.float32)[None] for part in sums]
+    rest = sums[4]
+    bias_back = rest[:, :4, local : 2 * local].reshape(1, -1)
+    return (results, *sums[:4], bias_back, rest[:, :8, :local])
 
 
 def solution(mesh):

time: 1060 us -> 852 us (0.80)
  waiting for transfers between devices: 578 us -> 289 us
  Pallas kernels: 55.7 us -> 241 us
  blocking collectives: 170 us -> 98 us
  local copies, waits for them, and re-layouts: 49.5 us -> 34.1 us
    pallas_call x0 -> x1, Pallas kernels: none -> 186 us  [reduce_grads(): pl.pallas_call(body, in_specs=[pl.BlockSpec(memory_space=pl.ANY)] * 5, ou...]
    psum x1 -> x0, waiting for transfers between devices: 177 us -> none  [relay(): lax.psum((qkv_back, out_back, in_back, down_back, bias_back, rows_back),...]
    reduce_scatter x4 -> x0, waiting for transfers between devices: 72.5 us -> none  [the longest x3 71.9 us: relay(): lax.psum_scatter(low(part), 'wt', scatter_dimension=0, tiled=True)]
    psum x1 -> x0, blocking collectives: 61.2 us -> none  [relay(): lax.psum((qkv_back, out_back, in_back, down_back, bias_back, rows_back),...]
    reduce_scatter x2, waiting for transfers between devices: 76.1 us -> 35.3 us  [scatter_rows(): return lax.psum_scatter(block, 'wt', scatter_dimension=1, tiled=True)]
    ppermute x2, waiting for transfers between devices: 36.3 us -> 68.5 us  [swapped(): return lax.ppermute(block, ('ctx', 'wt'), swap)]
    all_to_all x1 -> x0, waiting for transfers between devices: 31.4 us -> none  [relay(): lax.all_to_all(qkv_back, 'wt', 0, 3, tiled=True).reshape(local, 3 * width)]
    unnamed x1 -> x0, blocking collectives: 11.1 us -> none
  transfers between devices with their start and end apart: 20 -> 14, of which waited for: 13 -> 9; matrix products, arithmetic and copies ran while one was open for 7% -> 7% of each run, Pallas kernels for 3% -> 23%
where the time goes in v2:
time: 852 us; the launch traced here: 846 us
  waiting for transfers between devices  289 us (34%)
  Pallas kernels  241 us (28%)
  matrix products  108 us (13%)
  blocking collectives  98 us (12%)
  local copies, waits for them, and re-layouts  34.1 us (4%)
  other arithmetic  30.8 us (4%)
  starting transfers between devices  29.8 us (3%)
  between operations  15.7 us (2%)
    pallas_call x1, Pallas kernels, reduce_grads(): pl.pallas_call(body, in_specs=[pl.BlockSpec(memory_space=pl.ANY)] * 5, ou...  186 us
    dot_general x14, matrix products, dot(): lax.dot_general(left, right, (dims, ((), ())), preferred_element_type=jnp...  108 us
    ppermute x2, waiting for transfers between devices, swapped(): return lax.ppermute(block, ('ctx', 'wt'), swap)  68.5 us
    all_gather x1, waiting for transfers between devices, relay(): weight_down = lax.all_gather(w_down[0], 'wt', axis=0, tiled=True)  59.7 us
    all_gather x1, waiting for transfers between devices, relay(): weight_in = lax.all_gather(w_in[0], 'wt', axis=0, tiled=True)  45.9 us
    ppermute x2, waiting for transfers between devices, shifted(): return lax.ppermute(block, axis, route)  36.7 us
    reduce_scatter x2, waiting for transfers between devices, scatter_rows(): return lax.psum_scatter(block, 'wt', scatter_dimension=1, tiled=True)  35.3 us
    pallas_call x2, Pallas kernels, attend_heads_back(): pl.pallas_call(functools.partial(attend_back_kernel, size), grid=(packs,)...  35.1 us
  transfers between devices with their start and end apart: 14, of which 9 were waited for; matrix products, arithmetic and copies ran while one was open for 7% of the time, Pallas kernels for 23%

profile of v2, /device:TPU:4, one launch (start us, length us, event | category | flops | bytes accessed | tf_op | source)
XLA Modules:
  0.0 846.2 jit_solution(5878352153672004030)
XLA Ops:
  7.2 4.4 collective-permute-start
  11.7 36.3 %collective-permute-done = bf16[3,128,1024]{2,1,0:T(8,128)(2,1)S(1)} collective-permute-done((bf16[3,128,1024]{2,1,0:T(8,128)(2,1)}, bf16[3,128,1024]{2,1,0:T(8,128)(2,1)S(1)}, u32[]{:S(2)}, u32[]{:S(2)}) %collective-permute-start) | collective-permute-done | bytes 786464 | tf_op jit(solution)/shard_map/ppermute | solution.py:845
  59.1 32.2 %all-gather.4 = bf16[4,12,256]{2,1,0:T(8,128)(2,1)S(1)} all-gather(bf16[1,12,256]{2,1,0:T(8,128)(2,1)S(1)} %maximum_bitcast_fusion), channel_id=3, replica_groups=mesh['section'=2,'ctx'=4,'wt'=4] {'wt'}, dimensions={0}, use_global_device_ids=true | all-gather | bytes 30720 | tf_op jit(solution)/shard_map/all_gather | solution.py:868
  95.8 10.2 %attend_heads.2 = (bf16[3,512,768]{2,1,0:T(8,128)(2,1)}, bf16[3,512,256]{2,1,0:T(8,128)(2,1)S(1)}) custom-call(s32[3,1,512]{2,1,0:T(1,128)S(1)} %bitcast.200, s32[3,512,1]{2,1,0:T(8,128)S(1)} %reshape.296.ids_col, bf16[3,512,1024]{2,1,0:T(8,128)(2,1)} %all-gather.11.cloned.1.call-done.states, bf16[1024,768]{1,0:T(8,128)(2,1)S(1)} %bitcast.192, ...), custom_call_target="tpu_custom_call" | custom-call | tf_op jit(solution)/shard_map/attend_heads/pallas_call | solution.py:428
  106.9 5.2 all-to-all-start.1
  112.3 10.5 %all-to-all-done.1 = bf16[3,4,128,256]{3,2,0,1:T(8,128)(2,1)S(1)} async-done(((bf16[3,4,128,256]{3,2,0,1:T(8,128)(2,1)}), bf16[3,4,128,256]{3,2,0,1:T(8,128)(2,1)S(1)}, u32[]{:S(2)}, u32[]{:S(2)}) %all-to-all-start.1) | async-done | bytes 786464 | tf_op jit(solution)/shard_map/all_to_all | solution.py:855
  131.3 45.9 %all-gather.17.cloned.1.call-done = bf16[1,1024,4096]{2,1,0:T(8,128)(2,1)} async-done(((bf16[1,256,4096]{2,1,0:T(8,128)(2,1)}), bf16[1,1024,4096]{2,1,0:T(8,128)(2,1)}) %all-gather.17.cloned.1.call-update) | async-done | bytes 8388624 | tf_op jit(solution)/shard_map/all_gather | solution.py:865
  177.1 59.7 %all-gather.19.cloned.1.call-done = bf16[1,4096,1024]{2,1,0:T(8,128)(2,1)} async-done(((bf16[1,1024,1024]{2,1,0:T(8,128)(2,1)}), bf16[1,4096,1024]{2,1,0:T(8,128)(2,1)}) %all-gather.19.cloned.1.call-update) | async-done | bytes 8388624 | tf_op jit(solution)/shard_map/all_gather | solution.py:866
  236.8 17.0 %fusion.133 = (f32[384]{0:T(512)S(1)}, f32[384,1024]{1,0:T(8,128)}) fusion(f32[1024]{0:T(1024)S(1)} %bitcast.254, bf16[1,4096,1024]{2,1,0:T(8,128)(2,1)} %all-gather.19.cloned.1.call-done, bf16[1,1024,4096]{2,1,0:T(8,128)(2,1)} %all-gather.17.cloned.1.call-done, f32[4096]{0:T(1024)S(1)} %bitcast.245, f32[384,1024]{1,0:T(8,128)} %copy-done.22, ...), kind=kOutput, calls=%fused_computation.174 | convolution fusion | flops 6483344896 | bytes 19956224 | tf_op jit(solution)/shard_map/dot_general | solution.py:389
  256.9 4.7 collective-permute-start.1
  261.6 16.4 %collective-permute-done.1 = bf16[384,1024]{1,0:T(8,128)(2,1)} collective-permute-done((bf16[384,1024]{1,0:T(8,128)(2,1)}, bf16[384,1024]{1,0:T(8,128)(2,1)}, u32[]{:S(2)}, u32[]{:S(2)}) %collective-permute-start.1) | collective-permute-done | bytes 786464 | tf_op jit(solution)/shard_map/ppermute | solution.py:17
  279.1 30.6 %all-gather.13.cloned.1.call-done.states = bf16[3,512,1024]{2,1,0:T(8,128)(2,1)} async-done(((bf16[3,128,1024]{2,1,0:T(8,128)(2,1)}), bf16[3,512,1024]{2,1,0:T(8,128)(2,1)}) %all-gather.13.cloned.1.call-update) | async-done | bytes 3145744 | tf_op jit(solution)/shard_map/all_gather | solution.py:848
  309.6 10.2 %attend_heads.3 = (bf16[3,512,768]{2,1,0:T(8,128)(2,1)S(1)}, bf16[3,512,256]{2,1,0:T(8,128)(2,1)S(1)}) custom-call(s32[3,1,512]{2,1,0:T(1,128)S(1)} %bitcast.201, s32[3,512,1]{2,1,0:T(8,128)S(1)} %reshape.296.ids_col, bf16[3,512,1024]{2,1,0:T(8,128)(2,1)} %all-gather.13.cloned.1.call-done.states, bf16[1024,768]{1,0:T(8,128)(2,1)S(1)} %bitcast.193, ...), custom_call_target="tpu_custom_call" | custom-call | tf_op jit(solution)/shard_map/attend_heads/pallas_call | solution.py:428
  322.2 5.9 all-to-all-start.2
  328.0 31.6 %all_gather.31 = s32[3,2048]{1,0:T(4,128)S(1)} all-gather(s32[3,128]{1,0:T(4,128)S(1)} %copy-done.28), channel_id=1, replica_groups=mesh['section'=2,'ctx'=4,'wt'=4] {'wt','ctx'}, dimensions={1}, use_global_device_ids=true | all-gather | bytes 26112 | tf_op jit(solution)/shard_map/all_gather | solution.py:875
  364.5 12.5 %multiply_convert_fusion.2 = (bf16[384,4096]{1,0:T(8,128)(2,1)S(1)}, f32[384,4096]{1,0:T(8,128)}) fusion(f32[4096]{0:T(1024)S(1)} %bitcast.246, bf16[1,1024,4096]{2,1,0:T(8,128)(2,1)} %all-gather.17.cloned.1.call-done, f32[1024]{0:T(1024)S(1)} %bitcast.251, f32[1024]{0:T(1024)S(1)} %bitcast.238, f32[384]{0:T(512)S(1)} %add_rsqrt_fusion.1, ...), kind=kOutput, calls=%fused_computation.33 | convolution fusion | flops 3259367424 | bytes 19426304 | tf_op jit(solution)/shard_map/dot_general | solution.py:389
  381.9 22.4 %fusion.128 = (f32[384]{0:T(512)S(1)}, f32[384]{0:T(512)S(1)}, f32[384,1024]{1,0:T(8,128)}) fusion(f32[384]{0:T(512)S(1)} %add_rsqrt_fusion.1, f32[384,1024]{1,0:T(8,128)} %copy-done.11, f32[384]{0:T(512)S(1)} %broadcast_multiply_fusion.9, f32[1024]{0:T(1024)S(1)} %bitcast.240, bf16[1,1024,4096]{2,1,0:T(8,128)(2,1)} %all-gather.17.cloned.1.call-done, ...), kind=kOutput, calls=%fused_computation.169 | convolution fusion | flops 6495927296 | bytes 28616192 | tf_op jit(solution)/shard_map/dot_general | solution.py:389
  404.3 4.6 fusion.71
  410.6 17.0 %all_to_all.75 = bf16[3,1,128,1024]{2,0,1,3:T(4,128)(2,1)S(1)} all-to-all(bf16[3,1,128,1024]{2,0,1,3:T(4,128)(2,1)S(1)} %copy.113), channel_id=1, replica_groups=mesh['section'=2,'ctx'=4,'wt'=4] {'wt'}, dimensions={3} | all-to-all | bytes 1572864 | tf_op jit(solution)/shard_map/all_to_all | solution.py:859
  430.0 17.5 %attend_heads_back.2 = (bf16[3,512,768]{2,1,0:T(8,128)(2,1)}, bf16[3,512,1024]{2,1,0:T(8,128)(2,1)}) custom-call(s32[3,1,512]{2,1,0:T(1,128)S(1)} %bitcast.202, s32[3,512,1]{2,1,0:T(8,128)S(1)} %reshape.296.ids_col, bf16[3,512,768]{2,1,0:T(8,128)(2,1)} %copy-done.2, bf16[3,512,256]{2,1,0:T(8,128)(2,1)S(1)} %bitcast.197, bf16[1024,768]{1,0:T(8,128)(2,1)S(1)} %bitcast.194), custom_call_target="tpu_custom_call" | custom-call | tf_op jit(solution)/shard_map/attend_heads_back/pallas_call | solution.py:488
  447.6 35.3 %reduce-scatter.3.cloned.1.call-done = bf16[3,128,1024]{2,1,0:T(8,128)(2,1)} async-done(((bf16[3,512,1024]{2,1,0:T(8,128)(2,1)}), bf16[3,128,1024]{2,1,0:T(8,128)(2,1)}) %reduce-scatter.3.cloned.1.call-update) | async-done | bytes 786448 | tf_op jit(solution)/shard_map/reduce_scatter | solution.py:851
  487.7 20.3 %collective-permute-done.2 = bf16[384,1024]{1,0:T(8,128)(2,1)} collective-permute-done((bf16[384,1024]{1,0:T(8,128)(2,1)}, bf16[384,1024]{1,0:T(8,128)(2,1)}, u32[]{:S(2)}, u32[]{:S(2)}) %collective-permute-start.2) | collective-permute-done | bytes 786464 | tf_op jit(solution)/shard_map/ppermute | solution.py:17
  513.1 12.4 %fusion.144 = (bf16[4096]{0:T(1024)(128)(2,1)S(1)}, bf16[384,4096]{1,0:T(8,128)(2,1)S(1)}) fusion(f32[384,4096]{1,0:T(8,128)} %get-tuple-element.74, f32[4096]{0:T(1024)S(1)} %bitcast.248, bf16[1,4096,1024]{2,1,0:T(8,128)(2,1)} %all-gather.19.cloned.1.call-done, f32[384,1024]{1,0:T(8,128)S(1)} %get-tuple-element.54), kind=kOutput, calls=%fused_computation.177 | convolution fusion | flops 3264081920 | bytes 19423232 | tf_op jit(solution)/shard_map/dot_general | solution.py:389
  535.0 17.2 %all_to_all.76 = bf16[3,1,128,1024]{2,0,1,3:T(4,128)(2,1)S(1)} all-to-all(bf16[3,1,128,1024]{2,0,1,3:T(4,128)(2,1)S(1)} %copy.118), channel_id=1, replica_groups=mesh['section'=2,'ctx'=4,'wt'=4] {'wt'}, dimensions={3} | all-to-all | bytes 1572864 | tf_op jit(solution)/shard_map/all_to_all | solution.py:859
  554.5 17.5 %attend_heads_back.3 = (bf16[3,512,768]{2,1,0:T(8,128)(2,1)S(1)}, bf16[3,512,1024]{2,1,0:T(8,128)(2,1)}) custom-call(s32[3,1,512]{2,1,0:T(1,128)S(1)} %bitcast.203, s32[3,512,1]{2,1,0:T(8,128)S(1)} %reshape.296.ids_col, bf16[3,512,768]{2,1,0:T(8,128)(2,1)} %copy-done.2, bf16[3,512,256]{2,1,0:T(8,128)(2,1)S(1)} %bitcast.196, bf16[1024,768]{1,0:T(8,128)(2,1)S(1)} %bitcast.195), custom_call_target="tpu_custom_call" | custom-call | tf_op jit(solution)/shard_map/attend_heads_back/pallas_call | solution.py:488
  577.7 9.1 %convolution_convert_fusion.refs_3_ = bf16[4096,1024]{1,0:T(8,128)(2,1)} fusion(bf16[384,4096]{1,0:T(8,128)(2,1)} %copy-done.31, f32[384,1024]{1,0:T(8,128)S(1)} %copy-done.24), kind=kOutput, calls=%fused_computation.20 | convolution fusion | flops 3225812992 | bytes 13107200 | tf_op jit(solution)/shard_map/dot_general | solution.py:389
  586.8 7.3 convolution_convert_fusion.1.refs_2_
  595.4 5.7 bitcast_convert_fusion.refs_0_
  601.2 185.6 %reduce_grads.1 = (bf16[256,3072]{1,0:T(8,128)(2,1)}, bf16[256,1024]{1,0:T(8,128)(2,1)}, bf16[256,4096]{1,0:T(8,128)(2,1)}, bf16[1024,1024]{1,0:T(8,128)(2,1)}, bf16[16,1024]{1,0:T(8,128)(2,1)}) custom-call(bf16[1024,768]{1,0:T(8,128)(2,1)} %bitcast_convert_fusion.refs_0_, bf16[1024,1024]{1,0:T(8,128)(2,1)} %convolution_convert_fusion.2.refs_1_, ...), custom_call_target="tpu_custom_call" | custom-call | tf_op jit(solution)/shard_map/reduce_grads/pallas_call | solution.py:813
  790.8 4.2 bitcast_convert_fusion.1
  799.8 4.2 collective-permute-start.3
  806.0 32.3 %collective-permute-done.3 = bf16[3,128,1024]{2,1,0:T(8,128)(2,1)S(1)} collective-permute-done((bf16[3,128,1024]{2,1,0:T(8,128)(2,1)S(1)}, bf16[3,128,1024]{2,1,0:T(8,128)(2,1)S(1)}, u32[]{:S(2)}, u32[]{:S(2)}) %collective-permute-start.3) | collective-permute-done | bytes 786464 | tf_op jit(solution)/shard_map/ppermute | solution.py:845
  (194 shorter events, 84.7 us)
Async XLA Ops:
  7.2 50.5 %copy-start = (s32[3,4,4]{2,1,0:T(4,128)S(1)}, s32[3,4,4]{2,1,0:T(4,128)}, u32[]{:S(2)}) copy-start(s32[3,4,4]{2,1,0:T(4,128)} %param.12) | copy-start | bytes 580
  7.2 88.6 %all-gather.11.cloned.1.call-start = ((), (), s32[]{:S(2)}) async-start(), calls=%async_computation.7 | async-start | bytes 3932160 | tf_op jit(solution)/shard_map/all_gather | solution.py:848
  7.2 40.7 %collective-permute-start = (bf16[3,128,1024]{2,1,0:T(8,128)(2,1)}, bf16[3,128,1024]{2,1,0:T(8,128)(2,1)S(1)}, u32[]{:S(2)}, u32[]{:S(2)}) collective-permute-start(bf16[3,128,1024]{2,1,0:T(8,128)(2,1)} %bitcast.267), channel_id=1, source_target_pairs={{0,0},{1,4},{2,8},{3,12},{4,1},{5,5},{6,9},{7,13},{8,2},{9,6},{10,... | collective-permute-start | bytes 2359304 | tf_op jit(solution)/shard_map/ppermute | solution.py:845
  48.8 77.7 %all-gather.15.cloned.1.call-start = ((), (), s32[]{:S(2)}) async-start(), calls=%async_computation.11 | async-start | bytes 2621440 | tf_op jit(solution)/shard_map/all_gather | solution.py:864
  49.6 127.5 %all-gather.17.cloned.1.call-start = ((), (), s32[]{:S(2)}) async-start(), calls=%async_computation.12 | async-start | bytes 10485760 | tf_op jit(solution)/shard_map/all_gather | solution.py:865
  50.3 186.5 %all-gather.19.cloned.1.call-start = ((), (), s32[]{:S(2)}) async-start(), calls=%async_computation.13 | async-start | bytes 10485760 | tf_op jit(solution)/shard_map/all_gather | solution.py:866
  53.9 5.1 copy-start.26
  53.9 5.2 copy-start.27
  53.9 37.4 %all-to-all-start = ((bf16[256,3,4,256]{0,3,1,2:T(8,128)(2,1)}), bf16[256,3,4,256]{0,3,1,2:T(8,128)(2,1)S(1)}, u32[]{:S(2)}, u32[]{:S(2)}) async-start(bf16[256,3,4,256]{0,3,1,2:T(8,128)(2,1)} %copy.103), calls=%async_computation | async-start | bytes 3145728 | tf_op jit(solution)/shard_map/all_to_all | solution.py:863
  106.9 15.9 %all-to-all-start.1 = ((bf16[3,4,128,256]{3,2,0,1:T(8,128)(2,1)}), bf16[3,4,128,256]{3,2,0,1:T(8,128)(2,1)S(1)}, u32[]{:S(2)}, u32[]{:S(2)}) async-start(bf16[3,4,128,256]{3,2,0,1:T(8,128)(2,1)} %copy.107), calls=%async_computation.1 | async-start | bytes 1572864 | tf_op jit(solution)/shard_map/all_to_all | solution.py:855
  112.0 197.6 %all-gather.13.cloned.1.call-start = ((), (), s32[]{:S(2)}) async-start(), calls=%async_computation.8 | async-start | bytes 3932160 | tf_op jit(solution)/shard_map/all_gather | solution.py:848
  256.9 21.1 %collective-permute-start.1 = (bf16[384,1024]{1,0:T(8,128)(2,1)}, bf16[384,1024]{1,0:T(8,128)(2,1)}, u32[]{:S(2)}, u32[]{:S(2)}) collective-permute-start(bf16[384,1024]{1,0:T(8,128)(2,1)} %add_convert_fusion), channel_id=1, source_target_pairs={{0,16},{1,17},{2,18},{3,19},{4,20},{5,21},{6,22},{7,23},{8,24},{9,... | collective-permute-start | bytes 2359304 | tf_op jit(solution)/shard_map/ppermute | solution.py:17
  321.2 6.8 copy-start.28
  322.2 38.8 %all-to-all-start.2 = ((bf16[3,4,128,256]{3,2,0,1:T(8,128)(2,1)}), bf16[3,4,128,256]{3,2,0,1:T(8,128)(2,1)}, u32[]{:S(2)}, u32[]{:S(2)}) async-start(bf16[3,4,128,256]{3,2,0,1:T(8,128)(2,1)} %copy.111), calls=%async_computation.2 | async-start | bytes 1572864 | tf_op jit(solution)/shard_map/all_to_all | solution.py:855
  328.0 154.9 %reduce-scatter.3.cloned.1.call-start = ((), (), s32[]{:S(2)}) async-start(), calls=%async_computation.9 | async-start | bytes 3932160 | tf_op jit(solution)/shard_map/reduce_scatter | solution.py:851
  363.1 13.9 %slice-start.2 = ((s8[8388608]{0:T(1024)(128)(4,1)}), s8[4194304]{0:T(1024)(128)(4,1)S(1)}, s32[]{:S(2)}) async-start(s8[8388608]{0:T(1024)(128)(4,1)} %bitcast.265), calls=%async_computation.16 | async-start | bytes 8388608
  364.2 12.8 %copy-start.11 = (f32[384,1024]{1,0:T(8,128)}, f32[384,1024]{1,0:T(8,128)S(1)}, u32[]{:S(2)}) copy-start(f32[384,1024]{1,0:T(8,128)S(1)} %get-tuple-element.72) | copy-start | bytes 4718596
  364.5 12.5 %slice-start.3 = ((s8[8388608]{0:T(1024)(128)(4,1)}), s8[4194304]{0:T(1024)(128)(4,1)S(1)}, s32[]{:S(2)}) async-start(s8[8388608]{0:T(1024)(128)(4,1)} %bitcast.265), calls=%async_computation.17 | async-start | bytes 8388608
  447.6 60.5 %copy-start.10 = (bf16[3,128,1024]{2,1,0:T(8,128)(2,1)S(1)}, bf16[3,128,1024]{2,1,0:T(8,128)(2,1)}, u32[]{:S(2)}) copy-start(bf16[3,128,1024]{2,1,0:T(8,128)(2,1)} %copy-done.8) | copy-start | bytes 2359300
  447.6 350.0 %reduce-scatter.5.cloned.1.call-start = ((), (), s32[]{:S(2)}) async-start(), calls=%async_computation.10 | async-start | bytes 3932160 | tf_op jit(solution)/shard_map/reduce_scatter | solution.py:851
  486.4 21.6 %collective-permute-start.2 = (bf16[384,1024]{1,0:T(8,128)(2,1)}, bf16[384,1024]{1,0:T(8,128)(2,1)}, u32[]{:S(2)}, u32[]{:S(2)}) collective-permute-start(bf16[384,1024]{1,0:T(8,128)(2,1)} %fusion.55), channel_id=1, source_target_pairs={{16,0},{17,1},{18,2},{19,3},{20,4},{21,5},{22,6},{23,7},{24,8},{25... | collective-permute-start | bytes 2359304 | tf_op jit(solution)/shard_map/ppermute | solution.py:17
  487.7 23.2 %copy-start.6 = (f32[384,1024]{1,0:T(8,128)S(1)}, f32[384,1024]{1,0:T(8,128)}, u32[]{:S(2)}) copy-start(f32[384,1024]{1,0:T(8,128)} %copy-done.5) | copy-start | bytes 4718596
  510.9 14.6 %slice-start = ((s8[8388608]{0:T(1024)(128)(4,1)}), s8[4194304]{0:T(1024)(128)(4,1)S(1)}, s32[]{:S(2)}) async-start(s8[8388608]{0:T(1024)(128)(4,1)} %bitcast.263), calls=%async_computation.14 | async-start | bytes 8388608
  513.1 12.4 %copy-start.23 = (f32[384,1024]{1,0:T(8,128)}, f32[384,1024]{1,0:T(8,128)S(1)}, u32[]{:S(2)}) copy-start(f32[384,1024]{1,0:T(8,128)S(1)} %get-tuple-element.54) | copy-start | bytes 4718596
  513.1 12.4 %copy-start.12 = (f32[384,1024]{1,0:T(8,128)S(1)}, f32[384,1024]{1,0:T(8,128)}, u32[]{:S(2)}) copy-start(f32[384,1024]{1,0:T(8,128)} %copy-done.11) | copy-start | bytes 4718596
  513.1 12.4 %slice-start.1 = ((s8[8388608]{0:T(1024)(128)(4,1)}), s8[4194304]{0:T(1024)(128)(4,1)S(1)}, s32[]{:S(2)}) async-start(s8[8388608]{0:T(1024)(128)(4,1)} %bitcast.263), calls=%async_computation.15 | async-start | bytes 8388608
  577.7 9.1 %copy-start.13 = (f32[384,1024]{1,0:T(8,128)S(1)}, f32[384,1024]{1,0:T(8,128)}, u32[]{:S(2)}) copy-start(f32[384,1024]{1,0:T(8,128)} %copy-done.11) | copy-start | bytes 4718596
  577.7 9.1 %copy-start.33 = (bf16[384,4096]{1,0:T(8,128)(2,1)S(1)}, bf16[384,4096]{1,0:T(8,128)(2,1)}, u32[]{:S(2)}) copy-start(bf16[384,4096]{1,0:T(8,128)(2,1)} %copy-done.32) | copy-start | bytes 9437188
  586.8 7.4 copy-start.4
  797.6 6.4 copy-start.25
  799.8 38.5 %collective-permute-start.3 = (bf16[3,128,1024]{2,1,0:T(8,128)(2,1)S(1)}, bf16[3,128,1024]{2,1,0:T(8,128)(2,1)S(1)}, u32[]{:S(2)}, u32[]{:S(2)}) collective-permute-start(bf16[3,128,1024]{2,1,0:T(8,128)(2,1)S(1)} %bitcast.222), channel_id=1, source_target_pairs={{0,0},{1,4},{2,8},{3,12},{4,1},{5,5},{6,9},{7,13},{8,2},{9,6},{10,... | collective-permute-start | bytes 2359304 | tf_op jit(solution)/shard_map/ppermute | solution.py:845
  803.9 35.2 %copy-start.1 = (s32[3,4,4]{2,1,0:T(4,128)S(1)}, s32[3,4,4]{2,1,0:T(4,128)}, u32[]{:S(2)}) copy-start(s32[3,4,4]{2,1,0:T(4,128)} %param.12) | copy-start | bytes 580
  (20 other events, 42.1 us)
Sparse Core Ops, SparseCore 0:
  49.0 40.5 all-gather.10
  91.1 25.4 all-gather.14
  118.2 58.9 all-gather.16
  178.5 58.2 all-gather.18
  279.2 30.3 all-gather.12
  447.7 35.1 reduce-scatter.2
  573.6 39.3 reduce-scatter.4

commit v3 on v2

--- a/solution.py
+++ b/solution.py
@@ -398,17 +398,91 @@
     return jnp.where(mask, values, jnp.zeros_like(values))
 
 
-def attend_kernel(size, ids_row, ids_col, states, weight, bias, qkv, mixed):
-    local = mixed.shape[2]
-    projected = dot(states[0], weight[...]) + bias[...]
-    qkv[0] = projected.astype(jnp.bfloat16)
-    same = ids_col[0] == ids_row[0]
+def normal_tail(values):
+    size = jnp.abs(values)
+    bell = jnp.exp(-0.5 * values * values)
+    t = 1.0 / (1.0 + 0.3275911 * (2.0**-0.5) * size)
+    poly = t * (
+        0.254829592
+        + t * (-0.284496736 + t * (1.421413741 + t * (-1.453152027 + t * 1.061405429)))
+    )
+    tail = 0.5 * poly * bell
+    return (jnp.where(values >= 0, 1.0 - tail, tail), bell)
+
+
+def gelu_both(values):
+    below, bell = normal_tail(values)
+    return (values * below, below + values * bell * 0.3989422804014327)
+
+
+def norm_parts(values):
+    center = jnp.mean(values, axis=-1, keepdims=True)
+    offset = values - center
+    spread = jnp.mean(offset * offset, axis=-1, keepdims=True)
+    inverse = lax.rsqrt(spread + 1e-05)
+    return (offset * inverse, inverse)
+
+
+def norm_back(grad, gain, normal, inverse):
+    inner = grad * gain
+    mean = jnp.mean(inner, axis=-1, keepdims=True)
+    along = jnp.mean(inner * normal, axis=-1, keepdims=True)
+    return inverse * (inner - mean - normal * along)
+
+
+class Wires:
+    def __init__(self, sems):
+        self.sems = sems
+        self.places = {}
+
+    def at(self, *key):
+        return self.sems.at[self.places.setdefault(key, len(self.places))]
+
+    def remote(self, key, source, target, **where):
+        return pltpu.make_async_remote_copy(
+            source,
+            target,
+            self.at(key, "send"),
+            self.at(key, "recv"),
+            device_id=where,
+            device_id_type=MESH,
+        )
+
+    def local(self, key, source, target):
+        return pltpu.make_async_copy(source, target, self.at(key, "local"))
+
+
+def wt_places():
+    w = lax.axis_index("wt")
+    core = lax.rem(w, 2)
+    sibling = w + 1 - 2 * core
+    across = lax.rem(w + 2, 4)
+    return w, sibling, across, lax.rem(sibling + 2, 4)
+
+
+def greet(partners, extra):
+    barrier = pltpu.get_barrier_semaphore()
+    for partner in partners:
+        pl.semaphore_signal(barrier, 1, device_id=partner, device_id_type=MESH)
+    waits = len(partners)
+    for here, partner in extra:
+
+        @pl.when(here)
+        def _():
+            pl.semaphore_signal(barrier, 1, device_id=partner, device_id_type=MESH)
+
+        waits = waits + here.astype(jnp.int32)
+    pl.semaphore_wait(barrier, waits)
+
+
+def attend_pack(size, same, qkv, mixed):
+    local = mixed.shape[1]
     masks = head_lanes(size)
     for pair in range(local // PAIR):
         at = pair * PAIR
-        q = qkv[0, :, at : at + PAIR] * jnp.bfloat16(size**-0.5)
-        k = qkv[0, :, local + at : local + at + PAIR]
-        v = qkv[0, :, 2 * local + at : 2 * local + at + PAIR]
+        q = qkv[:, at : at + PAIR] * jnp.bfloat16(size**-0.5)
+        k = qkv[:, local + at : local + at + PAIR]
+        v = qkv[:, 2 * local + at : 2 * local + at + PAIR]
         total = None
         for mask in masks:
             scores = jnp.where(same, dot(only(mask, k), q, ((1,), (1,))), FAR)
@@ -417,45 +491,18 @@
             low = (probs * scale).astype(jnp.bfloat16)
             term = dot(only(mask, v), low, ((0,), (0,)))
             total = term if total is None else total + term
-        mixed[0, :, at : at + PAIR] = total.T.astype(jnp.bfloat16)
-
-
-def attend_heads(states, weight, bias, ids, size):
-    packs, rows, width = states.shape
-    local = weight.shape[1] // 3
-    whole = lambda *shape: pl.BlockSpec(shape, lambda m: (0,) * len(shape))
-    block = lambda *shape: pl.BlockSpec((1,) + shape, lambda m: (m, 0, 0))
-    return pl.pallas_call(
-        functools.partial(attend_kernel, size),
-        grid=(packs,),
-        in_specs=[
-            block(1, rows),
-            block(rows, 1),
-            block(rows, width),
-            whole(width, 3 * local),
-            whole(1, 3 * local),
-        ],
-        out_specs=[block(rows, 3 * local), block(rows, local)],
-        out_shape=[
-            jax.ShapeDtypeStruct((packs, rows, 3 * local), jnp.bfloat16),
-            jax.ShapeDtypeStruct((packs, rows, local), jnp.bfloat16),
-        ],
-        compiler_params=pltpu.CompilerParams(vmem_limit_bytes=48 * 2**20),
-        name="attend_heads",
-    )(ids[:, None, :], ids[:, :, None], states, weight, bias)
-
-
-def attend_back_kernel(size, ids_row, ids_col, qkv, mixed_grad, weight, projected_grad, part):
-    local = mixed_grad.shape[2]
-    same = ids_col[0] == ids_row[0]
+        mixed[:, at : at + PAIR] = total.T.astype(jnp.bfloat16)
+
+
+def attend_pack_back(size, same, qkv, grad_heads, projected_grad):
+    local = grad_heads.shape[1]
     masks = head_lanes(size)
-    scale = jnp.bfloat16(size**-0.5)
     for pair in range(local // PAIR):
         at = pair * PAIR
-        q = qkv[0, :, at : at + PAIR] * scale
-        k = qkv[0, :, local + at : local + at + PAIR]
-        v = qkv[0, :, 2 * local + at : 2 * local + at + PAIR]
-        grad = mixed_grad[0, :, at : at + PAIR]
+        q = qkv[:, at : at + PAIR] * jnp.bfloat16(size**-0.5)
+        k = qkv[:, local + at : local + at + PAIR]
+        v = qkv[:, 2 * local + at : 2 * local + at + PAIR]
+        grad = grad_heads[:, at : at + PAIR]
         totals = [None] * 3
         for mask in masks:
             own_k = only(mask, k)
@@ -472,69 +519,546 @@
             )
             totals = [t if o is None else o + t for o, t in zip(totals, terms)]
         query_grad = totals[0].T * size**-0.5
-        projected_grad[0, :, at : at + PAIR] = query_grad.astype(jnp.bfloat16)
-        projected_grad[0, :, local + at : local + at + PAIR] = totals[1].astype(jnp.bfloat16)
-        projected_grad[0, :, 2 * local + at : 2 * local + at + PAIR] = totals[2].astype(
-            jnp.bfloat16
-        )
-    part[0] = dot(projected_grad[0], weight[...], ((1,), (1,))).astype(jnp.bfloat16)
-
-
-def attend_heads_back(qkv, mixed_grad, weight, ids, size):
-    packs, rows, local = mixed_grad.shape
-    width = weight.shape[0]
-    whole = lambda *shape: pl.BlockSpec(shape, lambda m: (0,) * len(shape))
-    block = lambda *shape: pl.BlockSpec((1,) + shape, lambda m: (m, 0, 0))
+        projected_grad[:, at : at + PAIR] = query_grad.astype(jnp.bfloat16)
+        projected_grad[:, local + at : local + at + PAIR] = totals[1].astype(jnp.bfloat16)
+        projected_grad[:, 2 * local + at : 2 * local + at + PAIR] = totals[2].astype(jnp.bfloat16)
+
+
+class Spread:
+    def __init__(self, wires, full, mixed, mixed_rows, rows, local):
+        self.wires, self.full, self.mixed, self.mixed_rows = wires, full, mixed, mixed_rows
+        self.rows, self.local = rows, local
+        self.w, self.sibling, self.across, self.across_sibling = wt_places()
+
+    def stripe(self, m, j):
+        return self.full.at[m, pl.ds(j * self.rows, self.rows), :]
+
+    def to_sibling(self, m):
+        own = self.stripe(m, self.w)
+        return self.wires.remote(("sibling", m), own, own, wt=self.sibling)
+
+    def to_across(self, m):
+        own = self.stripe(m, self.w)
+        return self.wires.remote(("across", m), own, own, wt=self.across)
+
+    def passed(self, m):
+        block = self.stripe(m, self.across)
+        return self.wires.remote(("passed", m), block, block, wt=self.sibling)
+
+    def send(self, m):
+        self.to_across(m).start()
+        self.to_sibling(m).start()
+
+    def hand_on(self, m):
+        self.to_across(m).wait_recv()
+        self.passed(m).start()
+
+    def settle(self, m):
+        self.to_sibling(m).wait_recv()
+        self.passed(m).wait_recv()
+
+    def back(self, m):
+        heads = pl.ds(self.w * self.local, self.local)
+        target = self.mixed_rows.at[pl.ds(m * self.rows, self.rows), heads]
+        for index, partner in enumerate((self.across, self.across_sibling, self.sibling)):
+            block = self.mixed.at[m, pl.ds(partner * self.rows, self.rows), :]
+            yield self.wires.remote(("back", m, index), block, target, wt=partner)
+
+    def send_back(self, m):
+        for copy in self.back(m):
+            copy.start()
+        self.own_back(m).start()
+
+    def own_back(self, m):
+        heads = pl.ds(self.w * self.local, self.local)
+        return self.wires.local(
+            ("back", m),
+            self.mixed.at[m, pl.ds(self.w * self.rows, self.rows), :],
+            self.mixed_rows.at[pl.ds(m * self.rows, self.rows), heads],
+        )
+
+    def finish(self, m):
+        for copy in (self.to_sibling(m), self.to_across(m), self.passed(m)):
+            copy.wait_send()
+        for copy in self.back(m):
+            copy.wait()
+        self.own_back(m).wait()
+
+
+def project(full, weight, bias, qkv):
+    qkv[...] = (dot(full[...], weight[...]) + bias[...]).astype(jnp.bfloat16)
+
+
+def first_kernel(size, *refs):
+    block, shard_qkv, shard_out, shard_in, shard_down, small, marks, bias = refs[:8]
+    ids_row, ids_col = refs[8:10]
+    own, weight, whole_out, whole_in, whole_down, smalls, own_marks, count = refs[10:18]
+    mixed_rows, full, qkv, mixed, marks_wt, marks_ctx, sems = refs[18:]
+    micro, rows, width = block.shape
+    local = small.shape[1]
+    hidden = shard_in.shape[1]
+    half = local // 2
+    deep = shard_down.shape[0] // 8
+    wires = Wires(sems)
+    z = lax.axis_index("ctx")
+    spread = Spread(wires, full, mixed, mixed_rows, rows, local)
+    w, sibling, across, across_sibling = wt_places()
+    partners = (across, across_sibling, sibling)
+    level = lax.rem(z, 2)
+    neighbor = z + 1 - 2 * level
+    moves = w != z
+    others = [lax.rem(z + step, 4) for step in (1, 2, 3)]
+    greet(
+        [{"wt": partner} for partner in partners] + [{"ctx": other} for other in others],
+        [(moves, {"ctx": w, "wt": z})],
+    )
+
+    def swap(m):
+        return wires.remote(("swap", m), block.at[m], spread.stripe(m, z), ctx=w, wt=z)
+
+    def stay(m):
+        return wires.local(("stay", m), block.at[m], spread.stripe(m, z))
+
+    def swap_marks():
+        return wires.remote("swap marks", marks, own_marks, ctx=w, wt=z)
+
+    def head_copy(part, index):
+        column = part * width + partners[index] * local
+        return wires.remote(
+            ("heads", part, index),
+            shard_qkv.at[:, pl.ds(column, local)],
+            weight.at[pl.ds(w * local, local), pl.ds(part * local, local)],
+            wt=partners[index],
+        )
+
+    def head_own(part):
+        return wires.local(
+            ("heads", part),
+            shard_qkv.at[:, pl.ds(part * width + w * local, local)],
+            weight.at[pl.ds(w * local, local), pl.ds(part * local, local)],
+        )
+
+    def small_copy(index):
+        return wires.remote(("small", index), small, smalls.at[w], wt=partners[index])
+
+    def marks_copy(index):
+        return wires.remote(("marks", index), marks, marks_wt.at[index], wt=partners[index])
+
+    def count_copy(index):
+        return wires.remote(("count", index), count, marks_ctx.at[index], ctx=others[index])
+
+    columns = hidden // width
+    chunks = 1 + columns + 4
+
+    def piece(k, level):
+        if k == 0:
+            return shard_out, whole_out, local, level * half, half, 0
+        if k <= columns:
+            return shard_in, whole_in, local, level * half, half, (k - 1) * width
+        at = (level * 4 + k - 1 - columns) * deep
+        return shard_down, whole_down, 4 * deep * 2, at, deep, 0
+
+    def from_shard(k, level):
+        shard, _, _, at, size, column = piece(k, level)
+        return shard.at[pl.ds(at, size), pl.ds(column, width)]
+
+    def in_whole(k, level, j):
+        _, whole, stride, at, size, column = piece(k, level)
+        return whole.at[pl.ds(j * stride + at, size), pl.ds(column, width)]
+
+    def y_copy(k):
+        return wires.remote(
+            ("y", k), from_shard(k, level), in_whole(k, level, w), wt=across
+        )
+
+    def z_copy(k):
+        block = in_whole(k, level, across)
+        return wires.remote(("z", k), block, block, ctx=neighbor)
+
+    def core_copy(k, side):
+        block = in_whole(k, level if side == 0 else 1 - level, across)
+        return wires.remote(("core", k, side), block, block, wt=sibling)
+
+    def shard_sibling(index):
+        shard, whole = ((shard_out, whole_out), (shard_in, whole_in), (shard_down, whole_down))[
+            index
+        ]
+        size = shard.shape[0]
+        return wires.remote(
+            ("shard", index), shard, whole.at[pl.ds(w * size, size), :], wt=sibling
+        )
+
+    def shard_own(index):
+        shard, whole = ((shard_out, whole_out), (shard_in, whole_in), (shard_down, whole_down))[
+            index
+        ]
+        size = shard.shape[0]
+        return wires.local(("shard", index), shard, whole.at[pl.ds(w * size, size), :])
+
+    @pl.when(moves)
+    def _():
+        for m in range(micro):
+            swap(m).start()
+        swap_marks().start()
+
+    @pl.when(w == z)
+    def _():
+        for m in range(micro):
+            stay(m).start()
+        own_marks[...] = marks[...]
+
+    for part in range(3):
+        for index in range(3):
+            head_copy(part, index).start()
+        head_own(part).start()
+    for index in range(3):
+        small_copy(index).start()
+        marks_copy(index).start()
+    smalls[w] = small[...]
+
+    def arrive(m):
+        @pl.when(moves)
+        def _():
+            swap(m).wait_recv()
+
+        @pl.when(w == z)
+        def _():
+            stay(m).wait()
+
+    def own_copy(m):
+        return wires.local(("own", m), spread.stripe(m, w), own.at[m])
+
+    for m in range(micro):
+        arrive(m)
+        spread.send(m)
+        own_copy(m).start()
+    for k in range(chunks):
+        y_copy(k).start()
+    for index in range(3):
+        shard_sibling(index).start()
+        shard_own(index).start()
+    for index in range(3):
+        marks_copy(index).wait_recv()
+    count[...] = marks[...] + marks_wt[0] + marks_wt[1] + marks_wt[2]
+    for index in range(3):
+        count_copy(index).start()
+    for part in range(3):
+        for index in range(3):
+            head_copy(part, index).wait_recv()
+        head_own(part).wait()
+    for m in range(micro):
+        spread.hand_on(m)
+        spread.settle(m)
+        project(full.at[m], weight, bias, qkv.at[0])
+        attend_pack(size, ids_col[m] == ids_row[m], qkv.at[0], mixed.at[m])
+        spread.send_back(m)
+        y_copy(m).wait_recv()
+        z_copy(m).start()
+        core_copy(m, 0).start()
+    for k in range(micro, chunks):
+        y_copy(k).wait_recv()
+        z_copy(k).start()
+        core_copy(k, 0).start()
+        z_copy(k - micro).wait_recv()
+        core_copy(k - micro, 1).start()
+    for k in range(chunks - micro, chunks):
+        z_copy(k).wait_recv()
+        core_copy(k, 1).start()
+    for index in range(3):
+        count_copy(index).wait()
+    count[...] = count[...] + marks_ctx[0] + marks_ctx[1] + marks_ctx[2]
+    for m in range(micro):
+        spread.finish(m)
+        own_copy(m).wait()
+    for part in range(3):
+        for index in range(3):
+            head_copy(part, index).wait_send()
+    for index in range(3):
+        small_copy(index).wait()
+        marks_copy(index).wait_send()
+        shard_sibling(index).wait()
+        shard_own(index).wait()
+    for k in range(chunks):
+        y_copy(k).wait_send()
+        z_copy(k).wait_send()
+        for side in range(2):
+            core_copy(k, side).wait()
+
+    @pl.when(moves)
+    def _():
+        for m in range(micro):
+            swap(m).wait_send()
+        swap_marks().wait()
+
+
+def first_pass(block, shards, small, marks, bias, ids, size):
+    micro, rows, width = block.shape
+    local = small.shape[1]
+    pack = ids.shape[1]
+    anywhere = pl.BlockSpec(memory_space=pl.ANY)
+    inside = pl.BlockSpec(memory_space=pltpu.VMEM)
+    low = lambda *shape: jax.ShapeDtypeStruct(shape, jnp.bfloat16)
+    word = jax.ShapeDtypeStruct(marks.shape, jnp.float32)
     return pl.pallas_call(
-        functools.partial(attend_back_kernel, size),
-        grid=(packs,),
-        in_specs=[
-            block(1, rows),
-            block(rows, 1),
-            block(rows, 3 * local),
-            block(rows, local),
-            whole(width, 3 * local),
+        functools.partial(first_kernel, size),
+        in_specs=[anywhere] * 5 + [inside] * 5,
+        out_specs=[anywhere, inside] + [anywhere] * 3 + [inside] * 4,
+        out_shape=[
+            low(micro, rows, width),
+            low(width, 3 * local),
+            low(4 * shards[1].shape[0], shards[1].shape[1]),
+            low(4 * shards[2].shape[0], shards[2].shape[1]),
+            low(4 * shards[3].shape[0], shards[3].shape[1]),
+            low(4, *small.shape),
+            word,
+            word,
+            low(micro * rows, width),
         ],
-        out_specs=[block(rows, 3 * local), block(rows, width)],
+        scratch_shapes=[
+            pltpu.VMEM((micro, pack, width), jnp.bfloat16),
+            pltpu.VMEM((1, pack, 3 * local), jnp.bfloat16),
+            pltpu.VMEM((micro, pack, local), jnp.bfloat16),
+            pltpu.VMEM((3,) + marks.shape, jnp.float32),
+            pltpu.VMEM((3,) + marks.shape, jnp.float32),
+            pltpu.SemaphoreType.DMA((256,)),
+        ],
+        compiler_params=pltpu.CompilerParams(
+            collective_id=2, has_side_effects=True, vmem_limit_bytes=48 * 2**20
+        ),
+        name="first_pass",
+    )(block, *shards, small, marks, bias, ids[:, None, :], ids[:, :, None])
+
+
+def second_kernel(size, *refs):
+    states, leaving, weight, bias, ids_row, ids_col = refs[:6]
+    full, qkv, mixed_rows, mixed, sems = refs[6:]
+    micro, rows, width = states.shape
+    wires = Wires(sems)
+    section = lax.axis_index("section")
+    spread = Spread(wires, full, mixed, mixed_rows, rows, weight.shape[1] // 3)
+    w, sibling, across, across_sibling = wt_places()
+    greet(
+        [{"wt": partner} for partner in (across, across_sibling, sibling)]
+        + [{"section": 1 - section}],
+        [],
+    )
+
+    def relay_copy(m):
+        return wires.remote(("relay", m), leaving.at[m], spread.stripe(m, w), section=1 - section)
+
+    def stay(m):
+        return wires.local(("stay", m), states.at[m], spread.stripe(m, w))
+
+    @pl.when(section == 0)
+    def _():
+        for m in range(micro):
+            relay_copy(m).start()
+            stay(m).start()
+
+    def arrive(m):
+        @pl.when(section == 0)
+        def _():
+            stay(m).wait()
+
+        @pl.when(section == 1)
+        def _():
+            relay_copy(m).wait_recv()
+
+        spread.send(m)
+
+    def work(m):
+        spread.settle(m)
+        project(full.at[m], weight, bias, qkv.at[m])
+        attend_pack(size, ids_col[m] == ids_row[m], qkv.at[m], mixed.at[m])
+        spread.send_back(m)
+
+    arrive(0)
+    arrive(1)
+    spread.hand_on(0)
+    work(0)
+    arrive(2)
+    spread.hand_on(1)
+    work(1)
+    spread.hand_on(2)
+    work(2)
+    for m in range(micro):
+        spread.finish(m)
+
+    @pl.when(section == 0)
+    def _():
+        for m in range(micro):
+            relay_copy(m).wait_send()
+
+
+def second_pass(states, leaving, weight, bias, ids, size):
+    micro, rows, width = states.shape
+    local = weight.shape[1] // 3
+    pack = ids.shape[1]
+    anywhere = pl.BlockSpec(memory_space=pl.ANY)
+    inside = pl.BlockSpec(memory_space=pltpu.VMEM)
+    low = lambda *shape: jax.ShapeDtypeStruct(shape, jnp.bfloat16)
+    return pl.pallas_call(
+        functools.partial(second_kernel, size),
+        in_specs=[anywhere] * 2 + [inside] * 4,
+        out_specs=[inside] * 3,
         out_shape=[
-            jax.ShapeDtypeStruct((packs, rows, 3 * local), jnp.bfloat16),
-            jax.ShapeDtypeStruct((packs, rows, width), jnp.bfloat16),
+            low(micro, pack, width),
+            low(micro, pack, 3 * local),
+            low(micro * rows, width),
         ],
-        compiler_params=pltpu.CompilerParams(vmem_limit_bytes=48 * 2**20),
-        name="attend_heads_back",
-    )(ids[:, None, :], ids[:, :, None], qkv, mixed_grad, weight)
-
-
-def normal_tail(values):
-    size = jnp.abs(values)
-    bell = jnp.exp(-0.5 * values * values)
-    t = 1.0 / (1.0 + 0.3275911 * (2.0**-0.5) * size)
-    poly = t * (
-        0.254829592
-        + t * (-0.284496736 + t * (1.421413741 + t * (-1.453152027 + t * 1.061405429)))
+        scratch_shapes=[
+            pltpu.VMEM((micro, pack, local), jnp.bfloat16),
+            pltpu.SemaphoreType.DMA((80,)),
+        ],
+        compiler_params=pltpu.CompilerParams(
+            collective_id=3, has_side_effects=True, vmem_limit_bytes=48 * 2**20
+        ),
+        name="second_pass",
+    )(states, leaving, weight, bias, ids[:, None, :], ids[:, :, None])
+
+
+def back_kernel(size, returns, *refs):
+    rows_grad, skip, qkv, weight, ids_row, ids_col = refs[:6]
+    grad_states, projected, returned = refs[6:9]
+    heads_grad, part, from_sibling, far, from_across, sems = refs[9:]
+    micro, pack, local = heads_grad.shape
+    rows = pack // 4
+    wires = Wires(sems)
+    section = lax.axis_index("section")
+    w, sibling, across, across_sibling = wt_places()
+    partners = (across, across_sibling, sibling)
+    greet(
+        [{"wt": partner} for partner in partners]
+        + ([{"section": 1 - section}] if returns else []),
+        [],
     )
-    tail = 0.5 * poly * bell
-    return (jnp.where(values >= 0, 1.0 - tail, tail), bell)
-
-
-def gelu_both(values):
-    below, bell = normal_tail(values)
-    return (values * below, below + values * bell * 0.3989422804014327)
-
-
-def norm_parts(values):
-    center = jnp.mean(values, axis=-1, keepdims=True)
-    offset = values - center
-    spread = jnp.mean(offset * offset, axis=-1, keepdims=True)
-    inverse = lax.rsqrt(spread + 1e-05)
-    return (offset * inverse, inverse)
-
-
-def norm_back(grad, gain, normal, inverse):
-    inner = grad * gain
-    mean = jnp.mean(inner, axis=-1, keepdims=True)
-    along = jnp.mean(inner * normal, axis=-1, keepdims=True)
-    return inverse * (inner - mean - normal * along)
+
+    def heads_copy(m, index):
+        return wires.remote(
+            ("heads", m, index),
+            rows_grad.at[pl.ds(m * rows, rows), pl.ds(partners[index] * local, local)],
+            heads_grad.at[m, pl.ds(w * rows, rows), :],
+            wt=partners[index],
+        )
+
+    def heads_own(m):
+        return wires.local(
+            ("heads", m),
+            rows_grad.at[pl.ds(m * rows, rows), pl.ds(w * local, local)],
+            heads_grad.at[m, pl.ds(w * rows, rows), :],
+        )
+
+    def stripe(m, j):
+        return part.at[m, pl.ds(j * rows, rows), :]
+
+    def sibling_copy(m, index):
+        j = (across_sibling, sibling)[index]
+        return wires.remote(
+            ("sibling", m, index), stripe(m, j), from_sibling.at[m, index], wt=sibling
+        )
+
+    def across_copy(m):
+        return wires.remote(("across", m), far.at[m], from_across.at[m], wt=across)
+
+    def back_copy(m):
+        place = pl.ds(m * rows, rows)
+        return wires.remote(
+            ("return", m), grad_states.at[place, :], returned.at[place, :], section=1 - section
+        )
+
+    for m in range(micro):
+        for index in range(3):
+            heads_copy(m, index).start()
+        heads_own(m).start()
+
+    def work(m):
+        for index in range(3):
+            heads_copy(m, index).wait_recv()
+        heads_own(m).wait()
+        same = ids_col[m] == ids_row[m]
+        attend_pack_back(size, same, qkv.at[m], heads_grad.at[m], projected.at[m])
+        part[m] = dot(projected[m], weight[...], ((1,), (1,))).astype(jnp.bfloat16)
+        for index in range(2):
+            sibling_copy(m, index).start()
+
+    def cross(m):
+        for index in range(2):
+            sibling_copy(m, index).wait_recv()
+        total = stripe(m, across)[...].astype(jnp.float32) + from_sibling[m, 0].astype(jnp.float32)
+        far[m] = total.astype(jnp.bfloat16)
+        across_copy(m).start()
+
+    def finish(m):
+        across_copy(m).wait_recv()
+        place = pl.ds(m * rows, rows)
+        total = skip[place, :] + stripe(m, w)[...].astype(jnp.float32)
+        total = total + from_sibling[m, 1].astype(jnp.float32)
+        total = total + from_across[m].astype(jnp.float32)
+        grad_states[place, :] = total.astype(jnp.bfloat16)
+        if returns:
+
+            @pl.when(section == 1)
+            def _():
+                back_copy(m).start()
+
+    work(0)
+    cross(0)
+    work(1)
+    cross(1)
+    finish(0)
+    work(2)
+    cross(2)
+    finish(1)
+    finish(2)
+    for m in range(micro):
+        for index in range(3):
+            heads_copy(m, index).wait_send()
+        for index in range(2):
+            sibling_copy(m, index).wait_send()
+        across_copy(m).wait_send()
+        if returns:
+
+            @pl.when(section == 1)
+            def _():
+                back_copy(m).wait_send()
+
+            @pl.when(section == 0)
+            def _():
+                back_copy(m).wait_recv()
+
+    if not returns:
+        returned[...] = jnp.zeros_like(returned)
+
+
+def back_pass(rows_grad, skip, qkv, weight, ids, size, returns):
+    micro, pack, local = qkv.shape
+    local = local // 3
+    tokens, width = rows_grad.shape
+    rows = pack // 4
+    inside = pl.BlockSpec(memory_space=pltpu.VMEM)
+    low = lambda *shape: jax.ShapeDtypeStruct(shape, jnp.bfloat16)
+    back = (tokens, width) if returns else (16, PAIR)
+    block = pltpu.VMEM((micro, rows, width), jnp.bfloat16)
+    return pl.pallas_call(
+        functools.partial(back_kernel, size, returns),
+        in_specs=[inside] * 6,
+        out_specs=[inside] * 3,
+        out_shape=[low(tokens, width), low(micro, pack, 3 * local), low(*back)],
+        scratch_shapes=[
+            pltpu.VMEM((micro, pack, local), jnp.bfloat16),
+            pltpu.VMEM((micro, pack, width), jnp.bfloat16),
+            pltpu.VMEM((micro, 2, rows, width), jnp.bfloat16),
+            block,
+            block,
+            pltpu.SemaphoreType.DMA((80,)),
+        ],
+        compiler_params=pltpu.CompilerParams(
+            collective_id=4 if returns else 5,
+            has_side_effects=True,
+            vmem_limit_bytes=48 * 2**20,
+        ),
+        name="back_pass",
+    )(rows_grad, skip, qkv, weight, ids[:, None, :], ids[:, :, None])
 
 
 CHUNK = 128
@@ -841,47 +1365,24 @@
         (c * count_ctx + w, w * count_ctx + c) for c in range(count_ctx) for w in range(count_ctx)
     ]
 
-    def swapped(block):
-        return lax.ppermute(block, ("ctx", "wt"), swap)
-
-    def gather_rows(block):
-        return lax.all_gather(block, "wt", axis=1, tiled=True)
-
-    def scatter_rows(block):
-        return lax.psum_scatter(block, "wt", scatter_dimension=1, tiled=True)
-
-    def rows_of_heads(block):
-        split = block.reshape(micro, count_ctx, rows, local)
-        return lax.all_to_all(split, "wt", 1, 3, tiled=True).reshape(tokens, width)
-
-    def heads_of_rows(block):
-        split = block.reshape(micro, 1, rows, width)
-        return lax.all_to_all(split, "wt", 3, 1, tiled=True).reshape(micro, pack, local)
-
-    own = swapped(boundary[0])
-    shard = w_qkv[0].reshape(local, 3, count_ctx, local)
-    weight_qkv = lax.all_to_all(shard, "wt", 2, 0, tiled=True).reshape(width, 3 * local)
-    weight_out = lax.all_gather(w_out[0], "wt", axis=0, tiled=True)
-    weight_in = lax.all_gather(w_in[0], "wt", axis=0, tiled=True)
-    weight_down = lax.all_gather(w_down[0], "wt", axis=0, tiled=True)
-    small = jnp.concatenate([vectors[0], bias_in[0].reshape(-1, local)], axis=0)
-    small = lax.all_gather(small, "wt", axis=0)
-    vector_rows = small[:, :8].transpose(1, 0, 2).reshape(8, width).astype(jnp.float32)
-    in_bias = small[:, 8:].reshape(-1).astype(jnp.float32)
     own_rows = vectors[0].astype(jnp.float32)
     qkv_bias = jnp.concatenate([own_rows[0], jnp.zeros((local,), jnp.float32), own_rows[1]])[None]
     my_lengths = lax.dynamic_index_in_dim(lengths, ctx_at, 1, keepdims=False)
     ids = jax.vmap(lambda row: dealt_ids(row, pack, count_ctx))(my_lengths)
-    marks = lax.all_gather(valid, ("wt", "ctx"), axis=1, tiled=True)
-    count = jnp.sum(marks.astype(jnp.float32))
-    at = (ctx_at * count_ctx + wt_at) * rows
-    marks = lax.dynamic_slice_in_dim(marks, at, rows, 1).reshape(tokens, 1).astype(jnp.float32)
-    factor = LOSS_SCALE / count
-
-    def forward(states):
-        full = gather_rows(states.reshape(micro, rows, width))
-        qkv, mixed = attend_heads(full, weight_qkv, qkv_bias, ids, size)
-        mixed = rows_of_heads(mixed)
+    small = jnp.concatenate([vectors[0], bias_in[0].reshape(-1, local)], axis=0)
+    small = jnp.pad(small, ((0, 16 - small.shape[0]), (0, 0)))
+    marks = jnp.pad(valid.astype(jnp.float32), ((0, 8 - micro), (0, 0)))
+    shards = (w_qkv[0], w_out[0], w_in[0], w_down[0])
+    own, weight_qkv, weight_out, weight_in, weight_down, smalls, marks, counts, mixed = first_pass(
+        boundary[0], shards, small, marks, qkv_bias, ids, size
+    )
+    vector_rows = smalls[:, :8].transpose(1, 0, 2).reshape(8, width).astype(jnp.float32)
+    in_bias = smalls[:, 8 : 8 + w_in.shape[2] // width].reshape(-1).astype(jnp.float32)
+    marks = marks[:micro].reshape(tokens, 1)
+    factor = LOSS_SCALE / jnp.sum(counts)
+    flat = own.reshape(tokens, width)
+
+    def forward(states, mixed):
         summed = states.astype(jnp.float32) + (dot(mixed, weight_out) + vector_rows[2])
         normal_one, inverse_one = norm_parts(summed)
         first = normal_one * vector_rows[3] + vector_rows[4]
@@ -891,12 +1392,14 @@
         second = first + (dot(hidden, weight_down) + vector_rows[5])
         normal_two, inverse_two = norm_parts(second)
         output = normal_two * vector_rows[6] + vector_rows[7]
-        kept = (full, qkv, mixed, normal_one, inverse_one, first_low, hidden, slope)
-        return (output, kept + (normal_two, inverse_two))
+        slope = slope.astype(jnp.bfloat16)
+        return (
+            output,
+            (normal_one, inverse_one, first_low, hidden, slope, normal_two, inverse_two),
+        )
 
     def backward(grad, kept):
-        full, qkv, mixed, normal_one, inverse_one, first_low, hidden, slope = kept[:8]
-        normal_two, inverse_two = kept[8:]
+        normal_one, inverse_one, first_low, hidden, slope, normal_two, inverse_two = kept
         grad_second = norm_back(grad, vector_rows[6], normal_two, inverse_two)
         down_low = grad_second.astype(jnp.bfloat16)
         pre_low = (dot(down_low, weight_down, ((1,), (1,))) * slope).astype(jnp.bfloat16)
@@ -904,65 +1407,58 @@
         grad_summed = norm_back(grad_first, vector_rows[3], normal_one, inverse_one)
         branch_low = grad_summed.astype(jnp.bfloat16)
         mixed_grad = dot(branch_low, weight_out, ((1,), (1,))).astype(jnp.bfloat16)
-        mixed_grad = heads_of_rows(mixed_grad)
-        projected_grad, part = attend_heads_back(qkv, mixed_grad, weight_qkv, ids, size)
-        grad_states = grad_summed + scatter_rows(part).reshape(tokens, width)
-
-        def weight_grads():
-            along = ((0,), (0,))
-            flat = projected_grad.reshape(-1, 3 * local)
-            total = lambda values: jnp.sum(values.astype(jnp.float32), axis=0)
-            bias_qkv = total(flat)
-            rows_local = jnp.stack([bias_qkv[:local], bias_qkv[2 * local :]])
-            rows_whole = jnp.stack(
-                [
-                    total(branch_low),
-                    total(grad_first * normal_one),
-                    total(grad_first),
-                    total(down_low),
-                    total(grad * normal_two),
-                    total(grad),
-                ]
-            )
-            return (
-                dot(full.reshape(-1, width), flat, along),
-                dot(mixed, branch_low, along),
-                dot(first_low, pre_low, along),
-                dot(hidden, down_low, along),
-                total(pre_low),
-                rows_local,
-                rows_whole,
-            )
-
-        return (grad_states, weight_grads)
-
-    states = own.reshape(tokens, width)
-    output, _ = forward(states)
-    arrived = shifted(output.astype(jnp.bfloat16), "section", 1)
-    states = jnp.where(section_at == 0, states, arrived)
-    output, kept = forward(states)
-    distance = output - own.reshape(tokens, width).astype(jnp.float32)
-    cotangent = factor * marks * distance
-    grad_states, _ = backward(cotangent, kept)
-    returned = shifted(grad_states.astype(jnp.bfloat16), "section", -1)
+        return (mixed_grad, grad_summed, (down_low, pre_low, grad_first, branch_low))
+
+    output, _ = forward(flat, mixed)
+    leaving = output.astype(jnp.bfloat16).reshape(micro, rows, width)
+    full, qkv, mixed = second_pass(own, leaving, weight_qkv, qkv_bias, ids, size)
+    states = lax.dynamic_slice_in_dim(full, wt_at * rows, rows, 1).reshape(tokens, width)
+    output, kept = forward(states, mixed)
+    cotangent = factor * marks * (output - flat.astype(jnp.float32))
+    mixed_grad, skip, _ = backward(cotangent, kept)
+    _, _, returned = back_pass(mixed_grad, skip, qkv, weight_qkv, ids, size, True)
     cotangent = jnp.where(section_at == 1, cotangent, returned.astype(jnp.float32))
-    grad_states, weight_grads = backward(cotangent, kept)
-    results = jnp.where(section_at == 0, grad_states, output).astype(jnp.bfloat16)
-    results = swapped(results.reshape(micro, rows, width))[None]
-    grads = weight_grads()
+    mixed_grad, skip, grads = backward(cotangent, kept)
+    grad_states, projected, _ = back_pass(mixed_grad, skip, qkv, weight_qkv, ids, size, False)
+    results = jnp.where(section_at == 0, grad_states, output.astype(jnp.bfloat16))
+    results = results.reshape(micro, rows, width)
+    results = lax.ppermute(results, ("ctx", "wt"), swap)[None]
+
+    normal_one, _, first_low, hidden, _, normal_two, _ = kept
+    down_low, pre_low, grad_first, branch_low = grads
+    along = ((0,), (0,))
+    total = lambda values: jnp.sum(values.astype(jnp.float32), axis=0)
+    projected = projected.reshape(-1, 3 * local)
+    bias_qkv = total(projected)
+    rows_local = jnp.stack([bias_qkv[:local], bias_qkv[2 * local :]])
+    rows_whole = jnp.stack(
+        [
+            total(branch_low),
+            total(grad_first * normal_one),
+            total(grad_first),
+            total(down_low),
+            total(cotangent * normal_two),
+            total(cotangent),
+        ]
+    )
+    mine = (jnp.arange(4) == wt_at).astype(jnp.float32)[None, :, None]
+    rest = jnp.concatenate([rows_local[:, None, :] * mine, rows_whole.reshape(6, 4, local)])
+    rest = jnp.concatenate([rest, jnp.zeros((8, 4, local), jnp.float32)]).transpose(1, 0, 2)
+    in_rows = total(pre_low).reshape(4, -1, local)
+    in_rows = jnp.pad(in_rows, ((0, 0), (0, 16 - in_rows.shape[1]), (0, 2 * local)))
+    rest = jnp.concatenate([rest, in_rows], axis=2).reshape(64, width)
     low = lambda part: part.astype(jnp.bfloat16)
-    mine = (jnp.arange(4) == wt_at).astype(jnp.float32)[None, :, None]
-    rest = jnp.concatenate([grads[5][:, None, :] * mine, grads[6].reshape(6, 4, local)])
-    rest = jnp.concatenate([rest, jnp.zeros((8, 4, local), jnp.float32)])
-    rest = rest.transpose(1, 0, 2)
-    in_rows = jnp.zeros((4, 16, local), jnp.float32)
-    in_rows = in_rows.at[:, :4].set(grads[4].reshape(4, -1, local))
-    rest = jnp.concatenate([rest, in_rows, jnp.zeros((4, 16, 2 * local), jnp.float32)], axis=2)
-    rest = rest.reshape(64, width)
-    sums = reduce_grads(*[low(part) for part in grads[:4]], low(rest))
+    sums = reduce_grads(
+        low(dot(full.reshape(-1, width), projected, along)),
+        low(dot(mixed, branch_low, along)),
+        low(dot(first_low, pre_low, along)),
+        low(dot(hidden, down_low, along)),
+        low(rest),
+    )
     sums = [part.astype(jnp.float32)[None] for part in sums]
     rest = sums[4]
-    bias_back = rest[:, :4, local : 2 * local].reshape(1, -1)
+    in_rows = w_in.shape[2] // width
+    bias_back = rest[:, :in_rows, local : 2 * local].reshape(1, -1)
     return (results, *sums[:4], bias_back, rest[:, :8, :local])
 
 

time: 852 us -> 636 us (0.75)
  waiting for transfers between devices: 289 us -> 0.01 us
  Pallas kernels: 241 us -> 479 us
  blocking collectives: 98 us -> 0 us
  starting transfers between devices: 29.8 us -> 5.01 us
  local copies, waits for them, and re-layouts: 34.1 us -> 13.5 us
  between operations: 15.7 us -> 2.25 us
    pallas_call x4, Pallas kernels: 55.4 us -> 296 us  [the longest x1 170 us: first_pass(): pl.pallas_call(functools.partial(first_kernel, size), in_specs=[anywhere]...]
    all_gather x5 -> x0, waiting for transfers between devices: 136 us -> none  [the longest x1 59.7 us: relay(): weight_down = lax.all_gather(w_down[0], 'wt', axis=0, tiled=True)]
    ppermute x4 -> x1, waiting for transfers between devices: 105 us -> 0.01 us  [relay(): results = lax.ppermute(results, ('ctx', 'wt'), swap)[None]]
    all_gather x2 -> x0, blocking collectives: 63.8 us -> none  [the longest x1 32.2 us: relay(): small = lax.all_gather(small, 'wt', axis=0)]
    reduce_scatter x2 -> x0, waiting for transfers between devices: 35.3 us -> none  [scatter_rows(): return lax.psum_scatter(block, 'wt', scatter_dimension=1, tiled=True)]
    all_to_all x2 -> x0, blocking collectives: 34.2 us -> none  [heads_of_rows(): lax.all_to_all(split, 'wt', 3, 1, tiled=True).reshape(micro, pack, local)]
    all_to_all x3 -> x0, starting transfers between devices: 14.9 us -> none  [the longest x2 11 us: rows_of_heads(): return lax.all_to_all(split, 'wt', 1, 3, tiled=True).reshape(tokens, width)]
    all_to_all x3 -> x0, waiting for transfers between devices: 10.5 us -> none  [the longest x2 10.5 us: rows_of_heads(): return lax.all_to_all(split, 'wt', 1, 3, tiled=True).reshape(tokens, width)]
  transfers between devices with their start and end apart: 14 -> 1, of which waited for: 9 -> 0; matrix products, arithmetic and copies ran while one was open for 7% -> 5% of each run, Pallas kernels for 23% -> 29%
where the time goes in v3:
time: 636 us; the launch traced here: 626 us
  Pallas kernels  479 us (75%)
  matrix products  100 us (16%)
  other arithmetic  26.3 us (4%)
  local copies, waits for them, and re-layouts  13.5 us (2%)
    pallas_call x1, Pallas kernels, reduce_grads(): pl.pallas_call(body, in_specs=[pl.BlockSpec(memory_space=pl.ANY)] * 5, ou...  183 us
    pallas_call x1, Pallas kernels, first_pass(): pl.pallas_call(functools.partial(first_kernel, size), in_specs=[anywhere]...  170 us
    dot_general x14, matrix products, dot(): lax.dot_general(left, right, (dims, ((), ())), preferred_element_type=jnp...  100 us
    pallas_call x2, Pallas kernels, back_pass(): pl.pallas_call(functools.partial(back_kernel, size, returns), in_specs=[i...  91.7 us
    pallas_call x1, Pallas kernels, second_pass(): pl.pallas_call(functools.partial(second_kernel, size), in_specs=[anywhere...  34.9 us
  transfers between devices with their start and end apart: 1, of which 0 were waited for; matrix products, arithmetic and copies ran while one was open for 5% of the time, Pallas kernels for 29%

profile of v3, /device:TPU:4, one launch (start us, length us, event | category | flops | bytes accessed | tf_op | source)
XLA Modules:
  0.0 626.1 jit_solution(15697096349864847405)
XLA Ops:
  5.4 1.1 copy-done.8
  7.6 169.6 %first_pass.1 = (bf16[3,128,1024]{2,1,0:T(8,128)(2,1)S(1)}, bf16[1024,768]{1,0:T(8,128)(2,1)S(1)}, bf16[1024,1024]{1,0:T(8,128)(2,1)}, bf16[1024,4096]{1,0:T(8,1...) custom-call(bf16[3,128,1024]{2,1,0:T(8,128)(2,1)S(1)} %bitcast.96, ...), custom_call_target="tpu_custom_call" | custom-call | tf_op jit(solution)/shard_map/first_pass/pallas_call | solution.py:802
  178.1 3.4 fusion.71
  181.6 1.1 copy-done.17
  183.0 17.0 %fusion.72 = (f32[384]{0:T(512)S(1)}, f32[384,1024]{1,0:T(8,128)}) fusion(f32[1024]{0:T(1024)S(1)} %bitcast.140, bf16[4096,1024]{1,0:T(8,128)(2,1)} %get-tuple-element.32, bf16[1024,4096]{1,0:T(8,128)(2,1)} %get-tuple-element.31, f32[4096]{0:T(1024)S(1)} %bitcast.131, f32[384,1024]{1,0:T(8,128)} %copy-done.17, f32[1024]{0:T(1024)S(1)} %bitcast.136, ...), kind=kOutput, calls=%fused_computation.140 | convolution fusion | flops 6483344896 | bytes 19956224 | tf_op jit(solution)/shard_map/dot_general | solution.py:389
  200.0 1.7 multiply_reduce_fusion.8
  201.7 1.7 add_convert_fusion
  203.5 34.9 %second_pass.1 = (bf16[3,512,1024]{2,1,0:T(8,128)(2,1)}, bf16[3,512,768]{2,1,0:T(8,128)(2,1)}, bf16[384,1024]{1,0:T(8,128)(2,1)S(1)}) custom-call(bf16[3,128,1024]{2,1,0:T(8,128)(2,1)S(1)} %get-tuple-element.27.refs_0_, bf16[3,128,1024]{2,1,0:T(8,128)(2,1)S(1)} %bitcast.95, bf16[1024,768]{1,0:T(8,128)(2,1)S(1)} %get-tuple-element.33.refs_2_.refs_3_, ...), custom_call_target="tpu_custom_call" | custom-call | tf_op jit(solution)/shard_map/second_pass/pallas_call | solution.py:900
  239.2 1.3 constant_dynamic-slice_fusion
  240.6 2.8 fusion.75
  243.8 12.1 %multiply_convert_fusion = (bf16[384,4096]{1,0:T(8,128)(2,1)S(1)}, f32[384,4096]{1,0:T(8,128)}) fusion(f32[4096]{0:T(1024)S(1)} %bitcast.132, bf16[1024,4096]{1,0:T(8,128)(2,1)} %get-tuple-element.31, f32[1024]{0:T(1024)S(1)} %bitcast.137, f32[1024]{0:T(1024)S(1)} %bitcast.124, f32[384]{0:T(512)S(1)} %add_rsqrt_fusion.1, ...), kind=kOutput, calls=%fused_computation.20 | convolution fusion | flops 3259367424 | bytes 19426304 | tf_op jit(solution)/shard_map/dot_general | solution.py:389
  255.9 3.6 fusion.76
  262.1 18.8 %fusion.67 = (f32[384]{0:T(512)S(1)}, f32[384]{0:T(512)S(1)}, f32[384,1024]{1,0:T(8,128)}) fusion(f32[384]{0:T(512)S(1)} %add_rsqrt_fusion.1, f32[384,1024]{1,0:T(8,128)} %copy-done.13, f32[384]{0:T(512)S(1)} %broadcast_multiply_fusion.9, f32[1024]{0:T(1024)S(1)} %bitcast.126, bf16[1024,4096]{1,0:T(8,128)(2,1)} %get-tuple-element.31, ...), kind=kOutput, calls=%fused_computation.135 | convolution fusion | flops 6499073024 | bytes 28616192 | tf_op jit(solution)/shard_map/dot_general | solution.py:389
  280.9 2.4 subtract_multiply_fusion.2.refs_1_
  283.4 1.9 convolution_convert_fusion.4.refs_0_
  285.3 1.1 copy-done.4
  286.5 52.7 %back_pass.2 = (bf16[384,1024]{1,0:T(8,128)(2,1)}, bf16[3,512,768]{2,1,0:T(8,128)(2,1)}, bf16[384,1024]{1,0:T(8,128)(2,1)S(1)}) custom-call(bf16[384,1024]{1,0:T(8,128)(2,1)S(1)} %copy-done.4, f32[384,1024]{1,0:T(8,128)S(1)} %subtract_multiply_fusion.2.refs_1_, bf16[3,512,768]{2,1,0:T(8,128)(2,1)} %get-tuple-element.38.refs_2_, bf16[1024,768]{1,0:T(8,128)(2,1)} %copy-done.2, ...), custom_call_target="tpu_custom_call" | custom-call | tf_op jit(solution)/shard_map/back_pass/pallas_call | solution.py:1042
  339.2 1.2 fusion.65
  341.3 11.6 %fusion.79 = (bf16[4096]{0:T(1024)(128)(2,1)S(1)}, bf16[384,4096]{1,0:T(8,128)(2,1)S(1)}) fusion(f32[384,4096]{1,0:T(8,128)} %get-tuple-element.80, f32[4096]{0:T(1024)S(1)} %bitcast.134, bf16[4096,1024]{1,0:T(8,128)(2,1)} %get-tuple-element.32, f32[384,1024]{1,0:T(8,128)S(1)} %get-tuple-element.60), kind=kOutput, calls=%fused_computation.143 | convolution fusion | flops 3267227648 | bytes 19423232 | tf_op jit(solution)/shard_map/dot_general | solution.py:389
  353.0 7.6 %multiply_reduce_fusion.1 = (bf16[1024]{0:T(1024)(128)(2,1)S(1)}, f32[384]{0:T(512)S(1)}, f32[384]{0:T(512)S(1)}, bf16[1024]{0:T(1024)(128)(2,1)S(1)}, f32[384,1024]{1,0:T(8,128)S(1)}) fusion(f32[384]{0:T(512)S(1)} %add_rsqrt_fusion.1, f32[384,1024]{1,0:T(8,128)S(1)} %copy-done.14, f32[384]{0:T(512)S(1)} %broadcast_multiply_fusion.9, ...), kind=kOutput, calls=%fused_computation.33 | convolution fusion | flops 3225154560 | bytes 16267264 | tf_op jit(solution)/shard_map/dot_general | solution.py:389
  361.1 1.1 copy-done.22
  363.6 39.0 %back_pass.3 = (bf16[384,1024]{1,0:T(8,128)(2,1)S(1)}, bf16[3,512,768]{2,1,0:T(8,128)(2,1)}, bf16[16,128]{1,0:T(8,128)(2,1)}) custom-call(bf16[384,1024]{1,0:T(8,128)(2,1)S(1)} %convolution_convert_fusion.3.refs_0_, f32[384,1024]{1,0:T(8,128)S(1)} %get-tuple-element.62.refs_1_, bf16[3,512,768]{2,1,0:T(8,128)(2,1)} %get-tuple-element.38.refs_2_, ...), custom_call_target="tpu_custom_call" | custom-call | tf_op jit(solution)/shard_map/back_pass/pallas_call | solution.py:1042
  403.1 5.0 collective-permute-start
  408.1 6.8 %convolution_convert_fusion.refs_3_ = bf16[4096,1024]{1,0:T(8,128)(2,1)} fusion(bf16[384,4096]{1,0:T(8,128)(2,1)S(1)} %copy-done.24, f32[384,1024]{1,0:T(8,128)S(1)} %get-tuple-element.60), kind=kOutput, calls=%fused_computation.6 | convolution fusion | flops 3225812992 | bytes 13107200 | tf_op jit(solution)/shard_map/dot_general | solution.py:389
  414.9 7.1 %convolution_convert_fusion.1.refs_2_ = bf16[1024,4096]{1,0:T(8,128)(2,1)} fusion(bf16[384,4096]{1,0:T(8,128)(2,1)S(1)} %copy-done.26, f32[1024]{0:T(1024)S(1)} %bitcast.139, f32[1024]{0:T(1024)S(1)} %bitcast.129, f32[384,1024]{1,0:T(8,128)S(1)} %copy-done.14, f32[384]{0:T(512)S(1)} %add_rsqrt_fusion.1, f32[384]{0:T(512)S(1)} %broadcast_multiply_fusion.9), kind=kOutput, calls=%fused_computation.7 | convolution fusion | flops 3227385856 | bytes 13118464 | tf_op jit(solution)/shard_map/dot_general | solution.py:389
  422.1 2.6 convolution_convert_fusion.2.refs_1_
  425.4 3.8 bitcast_convert_fusion.refs_0_
  430.1 182.7 %reduce_grads.1 = (bf16[256,3072]{1,0:T(8,128)(2,1)}, bf16[256,1024]{1,0:T(8,128)(2,1)}, bf16[256,4096]{1,0:T(8,128)(2,1)}, bf16[1024,1024]{1,0:T(8,128)(2,1)}, bf16[16,1024]{1,0:T(8,128)(2,1)}) custom-call(bf16[1024,768]{1,0:T(8,128)(2,1)} %bitcast_convert_fusion.refs_0_, bf16[1024,1024]{1,0:T(8,128)(2,1)} %convolution_convert_fusion.2.refs_1_, ...), custom_call_target="tpu_custom_call" | custom-call | tf_op jit(solution)/shard_map/reduce_grads/pallas_call | solution.py:1337
  614.2 4.2 bitcast_convert_fusion.1
  618.5 2.5 bitcast_convert_fusion.2
  621.0 1.1 bitcast_convert_fusion.4
  622.8 2.0 bitcast_convert_fusion.3
  (122 shorter events, 18.2 us)
Async XLA Ops:
  0.6 0.7 copy-start
  5.4 1.1 copy-start.8
  6.5 1.0 copy-start.9
  177.2 0.9 copy-start.10
  178.1 25.4 %copy-start.2 = (bf16[1024,768]{1,0:T(8,128)(2,1)}, bf16[1024,768]{1,0:T(8,128)(2,1)S(1)}, u32[]{:S(2)}) copy-start(bf16[1024,768]{1,0:T(8,128)(2,1)S(1)} %get-tuple-element.33.refs_2_.refs_3_) | copy-start | bytes 4718596
  181.6 1.1 copy-start.17
  238.3 0.9 copy-start.5
  239.2 1.4 copy-start.6
  240.6 15.3 %slice-start = ((s8[8388608]{0:T(1024)(128)(4,1)}), s8[4194304]{0:T(1024)(128)(4,1)S(1)}, s32[]{:S(2)}) async-start(s8[8388608]{0:T(1024)(128)(4,1)} %bitcast.149), calls=%async_computation | async-start | bytes 8388608
  243.4 12.5 %copy-start.13 = (f32[384,1024]{1,0:T(8,128)}, f32[384,1024]{1,0:T(8,128)S(1)}, u32[]{:S(2)}) copy-start(f32[384,1024]{1,0:T(8,128)S(1)} %get-tuple-element.78) | copy-start | bytes 4718596
  243.8 12.2 %slice-start.1 = ((s8[8388608]{0:T(1024)(128)(4,1)}), s8[4194304]{0:T(1024)(128)(4,1)S(1)}, s32[]{:S(2)}) async-start(s8[8388608]{0:T(1024)(128)(4,1)} %bitcast.149), calls=%async_computation.1 | async-start | bytes 8388608
  255.9 3.6 copy-start.23
  259.5 2.6 copy-start.11
  280.9 2.5 copy-start.21
  285.3 1.1 copy-start.4
  286.5 52.7 %copy-start.12 = (f32[384,1024]{1,0:T(8,128)S(1)}, f32[384,1024]{1,0:T(8,128)}, u32[]{:S(2)}) copy-start(f32[384,1024]{1,0:T(8,128)} %copy-done.11) | copy-start | bytes 4718596
  341.3 11.6 %copy-start.14 = (f32[384,1024]{1,0:T(8,128)S(1)}, f32[384,1024]{1,0:T(8,128)}, u32[]{:S(2)}) copy-start(f32[384,1024]{1,0:T(8,128)} %copy-done.13) | copy-start | bytes 4718596
  352.9 7.6 %copy-start.25 = (bf16[384,4096]{1,0:T(8,128)(2,1)}, bf16[384,4096]{1,0:T(8,128)(2,1)S(1)}, u32[]{:S(2)}) copy-start(bf16[384,4096]{1,0:T(8,128)(2,1)S(1)} %get-tuple-element.86) | copy-start | bytes 9437188
  360.6 1.6 copy-start.22
  362.2 1.4 copy-start.3
  402.6 5.5 copy-start.24
  403.1 221.7 %collective-permute-start = (bf16[3,128,1024]{2,1,0:T(8,128)(2,1)S(1)}, bf16[3,128,1024]{2,1,0:T(8,128)(2,1)S(1)}, u32[]{:S(2)}, u32[]{:S(2)}) collective-permute-start(bf16[3,128,1024]{2,1,0:T(8,128)(2,1)S(1)} %bitcast.108), channel_id=1, source_target_pairs={{0,0},{1,4},{2,8},{3,12},{4,1},{5,5},{6,9},{7,13},{8,2},{9,6},{10,... | collective-permute-start | bytes 2359304 | tf_op jit(solution)/shard_map/ppermute | solution.py:1425
  408.1 6.8 %copy-start.26 = (bf16[384,4096]{1,0:T(8,128)(2,1)S(1)}, bf16[384,4096]{1,0:T(8,128)(2,1)}, u32[]{:S(2)}) copy-start(bf16[384,4096]{1,0:T(8,128)(2,1)} %copy-done.25) | copy-start | bytes 9437188
  414.9 7.1 %copy-start.7 = (bf16[384,1024]{1,0:T(8,128)(2,1)S(1)}, bf16[384,1024]{1,0:T(8,128)(2,1)}, u32[]{:S(2)}) copy-start(bf16[384,1024]{1,0:T(8,128)(2,1)} %copy-done.5) | copy-start | bytes 2359300
  422.0 2.6 copy-start.15
  422.1 3.4 copy-start.20
  614.2 4.2 copy-start.16
  618.5 2.5 copy-start.19
  621.0 1.8 copy-start.18
  622.8 2.9 copy-start.1

commit v4 on v3

--- a/solution.py
+++ b/solution.py
@@ -460,6 +460,10 @@
     return w, sibling, across, lax.rem(sibling + 2, 4)
 
 
+def turned(place):
+    return 2 * lax.rem(place, 2) + place // 2
+
+
 def greet(partners, extra):
     barrier = pltpu.get_barrier_semaphore()
     for partner in partners:
@@ -593,7 +597,8 @@
     block, shard_qkv, shard_out, shard_in, shard_down, small, marks, bias = refs[:8]
     ids_row, ids_col = refs[8:10]
     own, weight, whole_out, whole_in, whole_down, smalls, own_marks, count = refs[10:18]
-    mixed_rows, full, qkv, mixed, marks_wt, marks_ctx, sems = refs[18:]
+    mixed_rows, full, qkv, mixed, marks_wt, marks_ctx = refs[18:24]
+    held_out, held_in, held_down, sems = refs[24:]
     micro, rows, width = block.shape
     local = small.shape[1]
     hidden = shard_in.shape[1]
@@ -606,21 +611,23 @@
     partners = (across, across_sibling, sibling)
     level = lax.rem(z, 2)
     neighbor = z + 1 - 2 * level
-    moves = w != z
+    moves = w != turned(z)
     others = [lax.rem(z + step, 4) for step in (1, 2, 3)]
     greet(
         [{"wt": partner} for partner in partners] + [{"ctx": other} for other in others],
-        [(moves, {"ctx": w, "wt": z})],
+        [(moves, {"ctx": turned(w), "wt": turned(z)})],
     )
 
     def swap(m):
-        return wires.remote(("swap", m), block.at[m], spread.stripe(m, z), ctx=w, wt=z)
+        return wires.remote(
+            ("swap", m), block.at[m], spread.stripe(m, turned(z)), ctx=turned(w), wt=turned(z)
+        )
 
     def stay(m):
-        return wires.local(("stay", m), block.at[m], spread.stripe(m, z))
+        return wires.local(("stay", m), block.at[m], spread.stripe(m, w))
 
     def swap_marks():
-        return wires.remote("swap marks", marks, own_marks, ctx=w, wt=z)
+        return wires.remote("swap marks", marks, own_marks, ctx=turned(w), wt=turned(z))
 
     def head_copy(part, index):
         column = part * width + partners[index] * local
@@ -693,7 +700,12 @@
             index
         ]
         size = shard.shape[0]
-        return wires.local(("shard", index), shard, whole.at[pl.ds(w * size, size), :])
+        held = (held_out, held_in, held_down)[index]
+        place = whole.at[pl.ds(w * size, size), :]
+        return (
+            wires.local(("shard in", index), shard, held),
+            wires.local(("shard own", index), held, place),
+        )
 
     @pl.when(moves)
     def _():
@@ -701,7 +713,7 @@
             swap(m).start()
         swap_marks().start()
 
-    @pl.when(w == z)
+    @pl.when(w == turned(z))
     def _():
         for m in range(micro):
             stay(m).start()
@@ -721,7 +733,7 @@
         def _():
             swap(m).wait_recv()
 
-        @pl.when(w == z)
+        @pl.when(w == turned(z))
         def _():
             stay(m).wait()
 
@@ -736,7 +748,10 @@
         y_copy(k).start()
     for index in range(3):
         shard_sibling(index).start()
-        shard_own(index).start()
+        shard_own(index)[0].start()
+    for index in range(3):
+        shard_own(index)[0].wait()
+        shard_own(index)[1].start()
     for index in range(3):
         marks_copy(index).wait_recv()
     count[...] = marks[...] + marks_wt[0] + marks_wt[1] + marks_wt[2]
@@ -777,7 +792,7 @@
         small_copy(index).wait()
         marks_copy(index).wait_send()
         shard_sibling(index).wait()
-        shard_own(index).wait()
+        shard_own(index)[1].wait()
     for k in range(chunks):
         y_copy(k).wait_send()
         z_copy(k).wait_send()
@@ -820,6 +835,9 @@
             pltpu.VMEM((micro, pack, local), jnp.bfloat16),
             pltpu.VMEM((3,) + marks.shape, jnp.float32),
             pltpu.VMEM((3,) + marks.shape, jnp.float32),
+        ]
+        + [pltpu.VMEM(shard.shape, jnp.bfloat16) for shard in shards[1:]]
+        + [
             pltpu.SemaphoreType.DMA((256,)),
         ],
         compiler_params=pltpu.CompilerParams(
@@ -917,151 +935,188 @@
     )(states, leaving, weight, bias, ids[:, None, :], ids[:, :, None])
 
 
-def back_kernel(size, returns, *refs):
-    rows_grad, skip, qkv, weight, ids_row, ids_col = refs[:6]
-    grad_states, projected, returned = refs[6:9]
-    heads_grad, part, from_sibling, far, from_across, sems = refs[9:]
-    micro, pack, local = heads_grad.shape
-    rows = pack // 4
-    wires = Wires(sems)
+class Back:
+    def __init__(self, wires, size, refs):
+        self.wires, self.size = wires, size
+        self.rows_grad, self.skip, self.qkv, self.weight, self.ids = refs[:5]
+        self.projected, self.grad_states = refs[5:7]
+        self.heads_grad, self.part, self.from_sibling, self.far, self.from_across = refs[7:]
+        self.micro, self.pack, self.local = self.heads_grad.shape
+        self.rows = self.pack // 4
+        self.w, self.sibling, self.across, self.across_sibling = wt_places()
+        self.partners = (self.across, self.across_sibling, self.sibling)
+
+    def place(self, m):
+        return pl.ds(m * self.rows, self.rows)
+
+    def heads_copy(self, m, index):
+        column = pl.ds(self.partners[index] * self.local, self.local)
+        return self.wires.remote(
+            ("heads", m, index),
+            self.rows_grad.at[self.place(m), column],
+            self.heads_grad.at[m, pl.ds(self.w * self.rows, self.rows), :],
+            wt=self.partners[index],
+        )
+
+    def heads_own(self, m):
+        return self.wires.local(
+            ("heads", m),
+            self.rows_grad.at[self.place(m), pl.ds(self.w * self.local, self.local)],
+            self.heads_grad.at[m, pl.ds(self.w * self.rows, self.rows), :],
+        )
+
+    def stripe(self, m, j):
+        return self.part.at[m, pl.ds(j * self.rows, self.rows), :]
+
+    def sibling_copy(self, m, index):
+        j = (self.across_sibling, self.sibling)[index]
+        return self.wires.remote(
+            ("to sibling", m, index),
+            self.stripe(m, j),
+            self.from_sibling.at[m, index],
+            wt=self.sibling,
+        )
+
+    def across_copy(self, m):
+        return self.wires.remote(
+            ("to across", m), self.far.at[m], self.from_across.at[m], wt=self.across
+        )
+
+    def begin(self, m):
+        for index in range(3):
+            self.heads_copy(m, index).start()
+        self.heads_own(m).start()
+
+    def arrive(self, m):
+        for index in range(3):
+            self.heads_copy(m, index).wait_recv()
+        self.heads_own(m).wait()
+
+    def work(self, m, following=None):
+        self.arrive(m)
+        if following is not None:
+            self.begin(following)
+        ids_row, ids_col = self.ids
+        whole = pl.ds(m * self.pack, self.pack)
+        projected = self.projected.at[whole, :]
+        same = ids_col[m] == ids_row[m]
+        attend_pack_back(self.size, same, self.qkv.at[m], self.heads_grad.at[m], projected)
+        product = dot(projected[...], self.weight[...], ((1,), (1,)))
+        self.part[m] = product.astype(jnp.bfloat16)
+        for index in range(2):
+            self.sibling_copy(m, index).start()
+
+    def cross(self, m):
+        for index in range(2):
+            self.sibling_copy(m, index).wait_recv()
+        total = self.stripe(m, self.across)[...].astype(jnp.float32)
+        total = total + self.from_sibling[m, 0].astype(jnp.float32)
+        self.far[m] = total.astype(jnp.bfloat16)
+        self.across_copy(m).start()
+
+    def finish(self, m):
+        self.across_copy(m).wait_recv()
+        total = self.skip[self.place(m), :] + self.stripe(m, self.w)[...].astype(jnp.float32)
+        total = total + self.from_sibling[m, 1].astype(jnp.float32)
+        total = total + self.from_across[m].astype(jnp.float32)
+        self.grad_states[self.place(m), :] = total.astype(jnp.bfloat16)
+
+    def end(self, m):
+        for index in range(3):
+            self.heads_copy(m, index).wait_send()
+        for index in range(2):
+            self.sibling_copy(m, index).wait_send()
+        self.across_copy(m).wait_send()
+
+
+def back_scratch(micro, pack, local, width):
+    block = pltpu.VMEM((micro, pack // 4, width), jnp.bfloat16)
+    return [
+        pltpu.VMEM((micro, pack, local), jnp.bfloat16),
+        pltpu.VMEM((micro, pack, width), jnp.bfloat16),
+        pltpu.VMEM((micro, 2, pack // 4, width), jnp.bfloat16),
+        block,
+        block,
+    ]
+
+
+def swap_back(wires, rows, source, target, m, moves):
+    z, w = lax.axis_index("ctx"), lax.axis_index("wt")
+    block = source.at[pl.ds(m * rows, rows), :]
+    if moves:
+        return wires.remote(("home", m), block, target.at[m], ctx=turned(w), wt=turned(z))
+    return wires.local(("home", m), block, target.at[m])
+
+
+def back_kernel(size, *refs):
+    returned, grad_states, projected = refs[6:9]
+    wires = Wires(refs[-1])
     section = lax.axis_index("section")
-    w, sibling, across, across_sibling = wt_places()
-    partners = (across, across_sibling, sibling)
-    greet(
-        [{"wt": partner} for partner in partners]
-        + ([{"section": 1 - section}] if returns else []),
-        [],
-    )
-
-    def heads_copy(m, index):
-        return wires.remote(
-            ("heads", m, index),
-            rows_grad.at[pl.ds(m * rows, rows), pl.ds(partners[index] * local, local)],
-            heads_grad.at[m, pl.ds(w * rows, rows), :],
-            wt=partners[index],
-        )
-
-    def heads_own(m):
-        return wires.local(
-            ("heads", m),
-            rows_grad.at[pl.ds(m * rows, rows), pl.ds(w * local, local)],
-            heads_grad.at[m, pl.ds(w * rows, rows), :],
-        )
-
-    def stripe(m, j):
-        return part.at[m, pl.ds(j * rows, rows), :]
-
-    def sibling_copy(m, index):
-        j = (across_sibling, sibling)[index]
-        return wires.remote(
-            ("sibling", m, index), stripe(m, j), from_sibling.at[m, index], wt=sibling
-        )
-
-    def across_copy(m):
-        return wires.remote(("across", m), far.at[m], from_across.at[m], wt=across)
+    back = Back(wires, size, refs[:4] + (refs[4:6], projected, grad_states) + refs[9:-1])
+    greet([{"wt": partner} for partner in back.partners] + [{"section": 1 - section}], [])
+    back.begin(0)
 
     def back_copy(m):
-        place = pl.ds(m * rows, rows)
+        place = back.place(m)
         return wires.remote(
             ("return", m), grad_states.at[place, :], returned.at[place, :], section=1 - section
         )
 
-    for m in range(micro):
-        for index in range(3):
-            heads_copy(m, index).start()
-        heads_own(m).start()
-
-    def work(m):
-        for index in range(3):
-            heads_copy(m, index).wait_recv()
-        heads_own(m).wait()
-        same = ids_col[m] == ids_row[m]
-        attend_pack_back(size, same, qkv.at[m], heads_grad.at[m], projected.at[m])
-        part[m] = dot(projected[m], weight[...], ((1,), (1,))).astype(jnp.bfloat16)
-        for index in range(2):
-            sibling_copy(m, index).start()
-
-    def cross(m):
-        for index in range(2):
-            sibling_copy(m, index).wait_recv()
-        total = stripe(m, across)[...].astype(jnp.float32) + from_sibling[m, 0].astype(jnp.float32)
-        far[m] = total.astype(jnp.bfloat16)
-        across_copy(m).start()
-
     def finish(m):
-        across_copy(m).wait_recv()
-        place = pl.ds(m * rows, rows)
-        total = skip[place, :] + stripe(m, w)[...].astype(jnp.float32)
-        total = total + from_sibling[m, 1].astype(jnp.float32)
-        total = total + from_across[m].astype(jnp.float32)
-        grad_states[place, :] = total.astype(jnp.bfloat16)
-        if returns:
-
-            @pl.when(section == 1)
-            def _():
-                back_copy(m).start()
-
-    work(0)
-    cross(0)
-    work(1)
-    cross(1)
+        back.finish(m)
+
+        @pl.when(section == 1)
+        def _():
+            back_copy(m).start()
+
+    back.work(0, 1)
+    back.cross(0)
+    back.work(1, 2)
+    back.cross(1)
     finish(0)
-    work(2)
-    cross(2)
+    back.work(2)
+    back.cross(2)
     finish(1)
     finish(2)
-    for m in range(micro):
-        for index in range(3):
-            heads_copy(m, index).wait_send()
-        for index in range(2):
-            sibling_copy(m, index).wait_send()
-        across_copy(m).wait_send()
-        if returns:
-
-            @pl.when(section == 1)
-            def _():
-                back_copy(m).wait_send()
-
-            @pl.when(section == 0)
-            def _():
-                back_copy(m).wait_recv()
-
-    if not returns:
-        returned[...] = jnp.zeros_like(returned)
-
-
-def back_pass(rows_grad, skip, qkv, weight, ids, size, returns):
+    for m in range(back.micro):
+        back.end(m)
+
+        @pl.when(section == 1)
+        def _():
+            back_copy(m).wait_send()
+
+        @pl.when(section == 0)
+        def _():
+            back_copy(m).wait_recv()
+
+
+def back_pass(rows_grad, skip, qkv, weight, ids, size):
     micro, pack, local = qkv.shape
     local = local // 3
     tokens, width = rows_grad.shape
-    rows = pack // 4
     inside = pl.BlockSpec(memory_space=pltpu.VMEM)
     low = lambda *shape: jax.ShapeDtypeStruct(shape, jnp.bfloat16)
-    back = (tokens, width) if returns else (16, PAIR)
-    block = pltpu.VMEM((micro, rows, width), jnp.bfloat16)
     return pl.pallas_call(
-        functools.partial(back_kernel, size, returns),
+        functools.partial(back_kernel, size),
         in_specs=[inside] * 6,
-        out_specs=[inside] * 3,
-        out_shape=[low(tokens, width), low(micro, pack, 3 * local), low(*back)],
+        out_specs=inside,
+        out_shape=low(tokens, width),
         scratch_shapes=[
-            pltpu.VMEM((micro, pack, local), jnp.bfloat16),
-            pltpu.VMEM((micro, pack, width), jnp.bfloat16),
-            pltpu.VMEM((micro, 2, rows, width), jnp.bfloat16),
-            block,
-            block,
-            pltpu.SemaphoreType.DMA((80,)),
-        ],
+            pltpu.VMEM((tokens, width), jnp.bfloat16),
+            pltpu.VMEM((micro * pack, 3 * local), jnp.bfloat16),
+        ]
+        + back_scratch(micro, pack, local, width)
+        + [pltpu.SemaphoreType.DMA((96,))],
         compiler_params=pltpu.CompilerParams(
-            collective_id=4 if returns else 5,
-            has_side_effects=True,
-            vmem_limit_bytes=48 * 2**20,
+            collective_id=4, has_side_effects=True, vmem_limit_bytes=48 * 2**20
         ),
         name="back_pass",
     )(rows_grad, skip, qkv, weight, ids[:, None, :], ids[:, :, None])
 
 
 CHUNK = 128
+RING = 6
+LAGS = (0, 3, 5, 7, 9)
 
 
 def sum_into(target, parts, rows):
@@ -1079,135 +1134,189 @@
 
 
 def chunk_list(local, width, hidden):
-    down = [("down", index) for index in range(hidden // 4 // CHUNK)]
+    down = [("down", row, CHUNK, 0) for row in range(0, hidden // 4, CHUNK)]
     across = [
-        ("in", (half, column))
+        ("in", row, CHUNK, column)
         for column in range(hidden // width)
-        for half in range(local // CHUNK)
+        for row in range(0, local, CHUNK)
     ]
-    out = [("out", half) for half in range(local // CHUNK)]
-    qkv = [("qkv", (half, part)) for part in range(3) for half in range(local // CHUNK)]
-    return down + across + out + [("rest", 0)] + qkv
-
-
-def reduce_kernel(chunks, local, width, hidden, grads, results, buffers, sems):
-    near, far, near_in, far_in, across_in, up_in, side_in, total = buffers
-    load, load_far, near_send, near_recv, far_send, far_recv = sems[:6]
-    across_send, across_recv, up_send, up_recv, side_recv = sems[6:11]
-    down_send, down_recv, keep, piece_send, piece_recv = sems[11:]
-    z = lax.axis_index("ctx")
-    w = lax.axis_index("wt")
-    core = lax.rem(w, 2)
-    sibling = w + 1 - 2 * core
-    across = lax.rem(w + 2, 4)
-    across_sibling = lax.rem(sibling + 2, 4)
+    out = [("out", row, CHUNK, 0) for row in range(0, local, CHUNK)]
+    qkv = [("qkv", row, CHUNK, part) for part in range(2) for row in range(0, local, CHUNK)]
+    qkv += [("qkv", row, CHUNK // 2, 2) for row in range(0, local - CHUNK // 2, CHUNK // 2)]
+    qkv += [("qkv", row, CHUNK // 4, 2) for row in range(local - CHUNK // 2, local, CHUNK // 4)]
+    return down + across + out + [("rest", 0, 16, 0)] + qkv
+
+
+def starts_of(chunks):
+    rows = [chunk[2] for chunk in chunks]
+    starts = [sum(rows[:k]) for k in range(len(rows) + 1)]
+    return starts, [sum(rows[k % 2 : k : 2]) for k in range(len(rows) + 2)]
+
+
+def last_kernel(chunks, size, *refs):
+    rows_grad, skip, qkv_all, weight, ids_row, ids_col, full_all, rest = refs[:8]
+    hidden, pre, first, mixed, down, branch, final = refs[8:15]
+    home = refs[15]
+    results = dict(zip(("qkv", "out", "in", "down", "rest"), refs[16:21]))
+    grad_states, projected, full, product = refs[21:25]
+    downs, ins, outs, down_both, pre_both, branch_both, rest_in = refs[25:32]
+    near, far, across_in, up_in, side_in = refs[32:37]
+    wires = Wires(refs[-1])
+    z, section = lax.axis_index("ctx"), lax.axis_index("section")
+    given = (rows_grad, skip, qkv_all, weight, (ids_row, ids_col))
+    back = Back(wires, size, given + (projected, grad_states) + refs[37:-1])
+    w, sibling, across, across_sibling = wt_places()
     partners = (sibling, across, across_sibling)
-
-    barrier = pltpu.get_barrier_semaphore()
-    for partner in partners:
-        pl.semaphore_signal(barrier, 1, device_id={"wt": partner}, device_id_type=MESH)
-
-    @pl.when(z > 0)
-    def _():
-        pl.semaphore_signal(barrier, 1, device_id={"ctx": z - 1}, device_id_type=MESH)
-
-    @pl.when(z < 3)
-    def _():
-        pl.semaphore_signal(barrier, 1, device_id={"ctx": z + 1}, device_id_type=MESH)
-
-    pl.semaphore_wait(barrier, 3 + (z > 0).astype(jnp.int32) + (z < 3).astype(jnp.int32))
-
-    def rows_of(k):
-        return 16 if chunks[k][0] == "rest" else CHUNK
+    tokens, width = down.shape
+    count = len(chunks)
+    local = back.local
+    deep = hidden.shape[1] // 4
+    starts, sides_at = starts_of(chunks)
+    moves = w != turned(z)
+    greet(
+        [{"wt": partner} for partner in partners],
+        [
+            (moves, {"ctx": turned(w), "wt": turned(z)}),
+            (z > 0, {"ctx": z - 1}),
+            (z < 3, {"ctx": z + 1}),
+        ],
+    )
+
+    def both(key, source, target, at, columns, theirs):
+        mine = (pl.ds(0, tokens), at)
+        other = (pl.ds(tokens, tokens), at)
+        return (
+            wires.local(key, source.at[:, columns], target.at[mine]),
+            wires.remote(key, source.at[:, theirs], target.at[other], wt=sibling),
+        )
+
+    def sides(key, source, block, target):
+        for side, (j, k) in enumerate(((w, sibling), (across, across_sibling))):
+            yield from both(
+                key + (side,),
+                source,
+                target,
+                pl.ds(side * CHUNK, CHUNK),
+                pl.ds(block(j), CHUNK),
+                pl.ds(block(k), CHUNK),
+            )
+
+    def down_block(index):
+        return sides(
+            ("down", index), hidden, lambda j: j * deep + index * CHUNK, downs.at[index]
+        )
+
+    def in_block(half):
+        return sides(("in", half), first, lambda j: j * local + half * CHUNK, ins.at[half])
+
+    def out_block(half):
+        return sides(("out", half), mixed, lambda j: j * local + half * CHUNK, outs.at[half])
+
+    def whole(key, source, target, column):
+        at = pl.ds(column * width, width)
+        return both((key, column), source, target, at, at, at)
+
+    def rest_copies():
+        for side, k in enumerate((sibling, across_sibling)):
+            yield wires.remote(
+                ("rest", side), rest.at[pl.ds(k * 16, 16), :], rest_in.at[side], wt=sibling
+            )
+
+    halves = local // CHUNK
+    columns = hidden.shape[1] // width
+    loads = [lambda: whole("down", down, down_both, 0)]
+    loads += [lambda index=index: down_block(index) for index in range(deep // CHUNK)]
+    loads += [lambda half=half: in_block(half) for half in range(halves)]
+    loads += [lambda at=at: whole("pre", pre, pre_both, at) for at in range(columns)]
+    loads += [lambda: whole("branch", branch, branch_both, 0)]
+    loads += [lambda half=half: out_block(half) for half in range(halves)]
+
+    def full_copy():
+        return wires.local("full", full_all, full)
+
+    def needs(k):
+        kind, row, _, column = chunks[k]
+        index = row // CHUNK
+        if kind == "down":
+            return ([whole("down", down, down_both, 0)] if index == 0 else []) + [
+                down_block(index)
+            ]
+        if kind == "in":
+            return [whole("pre", pre, pre_both, column)] * (index == 0) + [
+                in_block(index)
+            ] * (column == 0)
+        return [whole("branch", branch, branch_both, 0)] * (index == 0) + [out_block(index)]
+
+    def operands(k):
+        kind, row, _, column = chunks[k]
+        index = row // CHUNK
+        if kind == "down":
+            return downs[index], down_both[...]
+        if kind == "in":
+            return ins[index], pre_both[:, column * width : (column + 1) * width]
+        return outs[index], branch_both[...]
 
     def is_piece(k):
         return chunks[k][0] == "qkv"
 
-    def source(k, j):
-        kind, at = chunks[k]
-        if kind == "down":
-            return grads["down"].at[pl.ds(j * (hidden // 4) + at * CHUNK, CHUNK), :]
-        if kind == "in":
-            half, column = at
-            return grads["in"].at[
-                pl.ds(j * local + half * CHUNK, CHUNK), pl.ds(column * width, width)
-            ]
-        if kind == "out":
-            return grads["out"].at[pl.ds(j * local + at * CHUNK, CHUNK), :]
-        if kind == "rest":
-            return grads["rest"].at[pl.ds(j * 16, 16), :]
-        half, part = at
-        return grads["qkv"].at[
-            pl.ds(j * local + half * CHUNK, CHUNK), pl.ds(part * local, local)
-        ]
+    def rows_of(k):
+        return chunks[k][2]
+
+    def slot(buffer, k):
+        return buffer.at[pl.ds(starts[k], rows_of(k)), :]
+
+    def beside_slot(k):
+        return side_in.at[pl.ds(sides_at[k], rows_of(k)), :]
 
     def result(k):
-        kind, at = chunks[k]
-        if kind == "down":
-            return results["down"].at[pl.ds(at * CHUNK, CHUNK), :]
-        if kind == "out":
-            return results["out"].at[pl.ds(at * CHUNK, CHUNK), :]
+        kind, row, rows, column = chunks[k]
         if kind == "rest":
             return results["rest"]
-        half, column = at
-        return results[kind].at[pl.ds(half * CHUNK, CHUNK), pl.ds(column * width, width)]
-
-    def slot(buffer, k):
-        return buffer.at[k, pl.ds(0, rows_of(k)), :]
-
-    def remote(source_ref, target_ref, send, recv, **where):
-        return pltpu.make_async_remote_copy(
-            source_ref, target_ref, send, recv, device_id=where, device_id_type=MESH
-        )
-
-    def near_load(k):
-        if is_piece(k):
-            place = near.at[k, :, pl.ds(w * local, local)]
-            return pltpu.make_async_copy(source(k, w), place, load.at[k])
-        return pltpu.make_async_copy(source(k, w), slot(near, k), load.at[k])
-
-    def far_load(k):
-        return pltpu.make_async_copy(source(k, across), slot(far, k), load_far.at[k])
-
-    def near_copy(k):
-        return remote(
-            source(k, sibling), slot(near_in, k), near_send.at[k], near_recv.at[k], wt=sibling
-        )
-
-    def far_copy(k):
-        return remote(
-            source(k, across_sibling), slot(far_in, k), far_send.at[k], far_recv.at[k], wt=sibling
-        )
+        return results[kind].at[pl.ds(row, rows), pl.ds(column * width, width)]
+
+    def piece(k, j):
+        _, row, rows, part = chunks[k]
+        return product.at[part, pl.ds(j * local + row, rows), :]
+
+    def piece_place(k):
+        return near.at[pl.ds(starts[k], rows_of(k)), pl.ds(w * local, local)]
 
     def piece_copy(k, index):
-        place = near.at[k, :, pl.ds(w * local, local)]
-        at = piece_send.at[k, index], piece_recv.at[k, index]
-        return remote(source(k, partners[index]), place, *at, wt=partners[index])
+        place = piece_place(k)
+        return wires.remote(
+            ("piece", k, index), piece(k, partners[index]), place, wt=partners[index]
+        )
+
+    def piece_own(k):
+        return wires.local(("piece", k), piece(k, w), piece_place(k))
 
     def across_copy(k):
-        return remote(
-            slot(far, k), slot(across_in, k), across_send.at[k], across_recv.at[k], wt=across
-        )
+        source = far.at[k % RING, pl.ds(0, rows_of(k)), :]
+        return wires.remote(("chunk", k), source, slot(across_in, k), wt=across)
 
     def place_of(k, role):
         return role if k % 2 == 0 else 3 - role
 
     def up_copy(k, role):
         target = place_of(k, 1 if role == 0 else 2)
-        return remote(slot(total, k), slot(up_in, k), up_send.at[k], up_recv.at[k], ctx=target)
+        return wires.remote(("up", k), slot(near, k), slot(up_in, k), ctx=target)
 
     def side_copy(k):
-        return remote(
-            slot(total, k), slot(side_in, k), up_send.at[k], side_recv.at[k], ctx=place_of(k, 1)
-        )
+        return wires.remote(("side", k), slot(near, k), beside_slot(k), ctx=place_of(k, 1))
 
     def down_copy(k, role):
-        origin = result(k) if role == 3 else slot(total, k)
-        at = down_send.at[k, 1 if role == 2 else 0]
-        return remote(origin, result(k), at, down_recv.at[k], ctx=place_of(k, role))
+        origin = result(k) if role == 3 else slot(near, k)
+        return pltpu.make_async_remote_copy(
+            origin,
+            result(k),
+            wires.at("down send", k, 1 if role == 2 else 0),
+            wires.at("down recv", k),
+            device_id={"ctx": place_of(k, role)},
+            device_id_type=MESH,
+        )
 
     def keep_copy(k):
-        return pltpu.make_async_copy(slot(total, k), result(k), keep.at[k])
+        return wires.local(("keep", k), slot(near, k), result(k))
 
     def on(k, role, step):
         pl.when(z == place_of(k, role))(step)
@@ -1215,39 +1324,56 @@
     def summands(k):
         if is_piece(k):
             return [slot(near, k)]
-        return [slot(near, k), slot(near_in, k), slot(across_in, k)]
-
-    count = len(chunks)
-    for k in range(count):
-        if not is_piece(k):
-            far_copy(k).start()
-            far_load(k).start()
-            near_copy(k).start()
-            near_load(k).start()
+        return [slot(near, k), slot(across_in, k)]
 
     def begin(k):
+        kind, row, _, column = chunks[k]
         if is_piece(k):
-            near_load(k).start()
-            for index in range(3):
-                piece_copy(k, index).start()
+            if row == 0:
+                at = pl.ds(column * local, local)
+                grad = dot(full[...], projected[:, at], ((0,), (0,)))
+                product[column] = grad.astype(jnp.bfloat16)
+            for partner in range(3):
+                piece_copy(k, partner).start()
+            piece_own(k).start()
             return
-        far_load(k).wait()
-        far_copy(k).wait_recv()
-        sum_into(slot(far, k), [slot(far, k), slot(far_in, k)], rows_of(k))
+        if k >= RING:
+            across_copy(k - RING).wait_send()
+        if kind == "rest":
+            for copy in rest_copies():
+                copy.wait_recv()
+            ones = jnp.ones((16, projected.shape[0]), jnp.bfloat16)
+            sums = dot(ones, projected[...])
+            row = lax.broadcasted_iota(jnp.int32, (16, local), 0)
+            own = jnp.where(row == 0, sums[:, :local], 0.0)
+            own = own + jnp.where(row == 1, sums[:, 2 * local :], 0.0)
+            own = jnp.concatenate([own, jnp.zeros((16, width - local), jnp.float32)], axis=1)
+            own = own + rest[pl.ds(w * 16, 16), :] + rest_in[0]
+            other = rest[pl.ds(across * 16, 16), :] + rest_in[1]
+            slot(near, k)[...] = own.astype(jnp.bfloat16)
+            far[k % RING, pl.ds(0, 16), :] = other.astype(jnp.bfloat16)
+        else:
+            for copies in needs(k):
+                for index, copy in enumerate(copies):
+                    (copy.wait if index % 2 == 0 else copy.wait_recv)()
+            left, right = operands(k)
+            grad = dot(left, right, ((0,), (0,))).astype(jnp.bfloat16)
+            slot(near, k)[...] = grad[:CHUNK]
+            far[k % RING] = grad[CHUNK:]
         across_copy(k).start()
 
     def settle(k):
-        near_load(k).wait()
         if is_piece(k):
             for index in range(3):
                 piece_copy(k, index).wait_recv()
+            piece_own(k).wait()
         else:
-            near_copy(k).wait_recv()
             across_copy(k).wait_recv()
         for role in (0, 3):
 
             def step(role=role):
-                sum_into(slot(total, k), summands(k), rows_of(k))
+                if not is_piece(k):
+                    sum_into(slot(near, k), summands(k), rows_of(k))
                 up_copy(k, role).start()
 
             on(k, role, step)
@@ -1255,7 +1381,7 @@
     def aside(k):
         def step():
             up_copy(k, 3).wait_recv()
-            sum_into(slot(total, k), summands(k) + [slot(up_in, k)], rows_of(k))
+            sum_into(slot(near, k), summands(k) + [slot(up_in, k)], rows_of(k))
             side_copy(k).start()
 
         on(k, 2, step)
@@ -1264,8 +1390,8 @@
         def step():
             up_copy(k, 0).wait_recv()
             side_copy(k).wait_recv()
-            parts = summands(k) + [slot(up_in, k), slot(side_in, k)]
-            sum_into(slot(total, k), parts, rows_of(k))
+            parts = summands(k) + [slot(up_in, k), beside_slot(k)]
+            sum_into(slot(near, k), parts, rows_of(k))
             down_copy(k, 0).start()
             down_copy(k, 2).start()
             keep_copy(k).start()
@@ -1279,19 +1405,70 @@
 
         on(k, 2, step)
 
+    def go_home(m, source, here, do):
+        @pl.when(moves & here)
+        def _():
+            do(swap_back(wires, back.rows, source, home, m, True))
+
+        @pl.when((w == turned(z)) & here)
+        def _():
+            do(swap_back(wires, back.rows, source, home, m, False))
+
+    def done(m):
+        back.finish(m)
+        go_home(m, grad_states, section == 0, lambda copy: copy.start())
+
+    def final_home(m):
+        go_home(m, final, section == 1, lambda copy: copy.start())
+
+    tail = count - 9
+    beside = {
+        1: [lambda: back.work(0)],
+        3: [lambda: back.work(1)],
+        5: [lambda: back.work(2)],
+        8: [lambda: final_home(0)],
+        12: [lambda: final_home(1)],
+        16: [lambda: final_home(2)],
+        tail: [lambda: back.cross(0)],
+        tail + 1: [lambda: back.cross(1)],
+        tail + 3: [lambda: back.cross(2), lambda: done(0)],
+        tail + 5: [lambda: done(1)],
+        tail + 7: [lambda: done(2)],
+    }
+
+    for m in range(back.micro):
+        back.begin(m)
+    for copy in rest_copies():
+        copy.start()
+    for load in loads:
+        for copy in load():
+            copy.start()
+    full_copy().start()
     stages = (begin, settle, aside, finish, forward)
-    for tick in range(count + len(stages) - 1):
-        for lag, stage in enumerate(stages):
+    for tick in range(count + LAGS[-1]):
+        if tick < count and chunks[tick][0] == "qkv" and chunks[tick - 1][0] != "qkv":
+            full_copy().wait()
+        for lag, stage in zip(LAGS, stages):
             if 0 <= tick - lag < count:
                 stage(tick - lag)
+        for step in beside.get(tick, []):
+            step()
+    for m in range(back.micro):
+        back.end(m)
+        go_home(m, grad_states, z >= 0, lambda copy: copy.wait())
+    for copy in rest_copies():
+        copy.wait_send()
+    for load in loads:
+        for index, copy in enumerate(load()):
+            if index % 2 == 1:
+                copy.wait_send()
+    direct = [k for k in range(count) if not is_piece(k)]
+    for k in direct[-RING:]:
+        across_copy(k).wait_send()
     for k in range(count):
         if is_piece(k):
             for index in range(3):
                 piece_copy(k, index).wait_send()
-        else:
-            far_copy(k).wait_send()
-            near_copy(k).wait_send()
-            across_copy(k).wait_send()
 
         def ends(role):
             up_copy(k, role).wait_send()
@@ -1312,43 +1489,68 @@
         on(k, 1, owner)
 
 
-def reduce_grads(grad_qkv, grad_out, grad_in, grad_down, rest):
-    width = grad_out.shape[0]
-    hidden = grad_down.shape[0]
-    local = width // 4
+def last_pass(rows_grad, skip, qkv, weight, ids, full, rest, operands, final, size):
+    micro, pack, local = qkv.shape
+    local = local // 3
+    tokens, width = rows_grad.shape
+    hidden = operands[0].shape[1]
     chunks = chunk_list(local, width, hidden)
     count = len(chunks)
-
-    def body(*refs):
-        grads = dict(zip(("qkv", "out", "in", "down", "rest"), refs[:5]))
-        results = dict(zip(("qkv", "out", "in", "down", "rest"), refs[5:10]))
-        reduce_kernel(chunks, local, width, hidden, grads, results, refs[10:18], refs[18:])
-
-    shapes = [
-        (local, 3 * width),
-        (local, width),
-        (local, hidden),
-        (hidden // 4, width),
-        (16, width),
-    ]
-    dma = pltpu.SemaphoreType.DMA
-    whole = [pltpu.VMEM((count, CHUNK, width), jnp.bfloat16)]
-    direct = [pltpu.VMEM((count - 6, CHUNK, width), jnp.bfloat16)]
+    direct = sum(chunk[0] != "qkv" for chunk in chunks)
+    starts, sides_at = starts_of(chunks)
+    inside = pl.BlockSpec(memory_space=pltpu.VMEM)
+    anywhere = pl.BlockSpec(memory_space=pl.ANY)
+    low = lambda *shape: jax.ShapeDtypeStruct(shape, jnp.bfloat16)
+    room = lambda *shape: pltpu.VMEM(shape, jnp.bfloat16)
+    halves = local // CHUNK
     return pl.pallas_call(
-        body,
-        in_specs=[pl.BlockSpec(memory_space=pl.ANY)] * 5,
-        out_specs=[pl.BlockSpec(memory_space=pl.ANY)] * 5,
-        out_shape=[jax.ShapeDtypeStruct(shape, jnp.bfloat16) for shape in shapes],
-        scratch_shapes=whole
-        + direct * 4
-        + whole * 3
-        + [dma((count,))] * 11
-        + [dma((count, 2)), dma((count,)), dma((count,)), dma((count, 3)), dma((count, 3))],
+        functools.partial(last_kernel, chunks, size),
+        in_specs=[inside] * 6 + [anywhere, inside] + [anywhere] * 7,
+        out_specs=[anywhere] * 6,
+        out_shape=[
+            low(micro, pack // 4, width),
+            low(local, 3 * width),
+            low(local, width),
+            low(local, hidden),
+            low(hidden // 4, width),
+            low(16, width),
+        ],
+        scratch_shapes=[
+            room(tokens, width),
+            room(micro * pack, 3 * local),
+            room(micro * pack, width),
+            room(3, width, local),
+            room(hidden // 4 // CHUNK, 2 * tokens, 2 * CHUNK),
+            room(halves, 2 * tokens, 2 * CHUNK),
+            room(halves, 2 * tokens, 2 * CHUNK),
+            room(2 * tokens, width),
+            room(2 * tokens, hidden),
+            room(2 * tokens, width),
+            pltpu.VMEM((2, 16, width), jnp.float32),
+            room(starts[count], width),
+            room(RING, CHUNK, width),
+            room(starts[direct], width),
+            room(starts[count], width),
+            room(max(sides_at[count:]), width),
+        ]
+        + back_scratch(micro, pack, local, width)
+        + [pltpu.SemaphoreType.DMA((720,))],
         compiler_params=pltpu.CompilerParams(
-            collective_id=1, has_side_effects=True, vmem_limit_bytes=60 * 2**20
+            collective_id=1, has_side_effects=True, vmem_limit_bytes=62 * 2**20
         ),
-        name="reduce_grads",
-    )(grad_qkv, grad_out, grad_in, grad_down, rest)
+        name="last_pass",
+    )(
+        rows_grad,
+        skip,
+        qkv,
+        weight,
+        ids[:, None, :],
+        ids[:, :, None],
+        full.reshape(micro * pack, width),
+        rest,
+        *operands,
+        final,
+    )
 
 
 def relay(boundary, lengths, valid, w_qkv, w_out, w_in, w_down, bias_in, vectors):
@@ -1361,14 +1563,11 @@
     size = width // HEADS
     local = width // lax.axis_size("wt")
     tokens = micro * rows
-    swap = [
-        (c * count_ctx + w, w * count_ctx + c) for c in range(count_ctx) for w in range(count_ctx)
-    ]
-
     own_rows = vectors[0].astype(jnp.float32)
     qkv_bias = jnp.concatenate([own_rows[0], jnp.zeros((local,), jnp.float32), own_rows[1]])[None]
-    my_lengths = lax.dynamic_index_in_dim(lengths, ctx_at, 1, keepdims=False)
+    my_lengths = lax.dynamic_index_in_dim(lengths, turned(ctx_at), 1, keepdims=False)
     ids = jax.vmap(lambda row: dealt_ids(row, pack, count_ctx))(my_lengths)
+    ids = ids.reshape(micro, 2, 2, rows).swapaxes(1, 2).reshape(micro, pack)
     small = jnp.concatenate([vectors[0], bias_in[0].reshape(-1, local)], axis=0)
     small = jnp.pad(small, ((0, 16 - small.shape[0]), (0, 0)))
     marks = jnp.pad(valid.astype(jnp.float32), ((0, 8 - micro), (0, 0)))
@@ -1388,7 +1587,7 @@
         first = normal_one * vector_rows[3] + vector_rows[4]
         first_low = first.astype(jnp.bfloat16)
         hidden, slope = gelu_both(dot(first_low, weight_in) + in_bias)
-        hidden = hidden.astype(jnp.bfloat16)
+        hidden = lax.optimization_barrier(hidden.astype(jnp.bfloat16))
         second = first + (dot(hidden, weight_down) + vector_rows[5])
         normal_two, inverse_two = norm_parts(second)
         output = normal_two * vector_rows[6] + vector_rows[7]
@@ -1403,6 +1602,7 @@
         grad_second = norm_back(grad, vector_rows[6], normal_two, inverse_two)
         down_low = grad_second.astype(jnp.bfloat16)
         pre_low = (dot(down_low, weight_down, ((1,), (1,))) * slope).astype(jnp.bfloat16)
+        pre_low = lax.optimization_barrier(pre_low)
         grad_first = grad_second + dot(pre_low, weight_in, ((1,), (1,)))
         grad_summed = norm_back(grad_first, vector_rows[3], normal_one, inverse_one)
         branch_low = grad_summed.astype(jnp.bfloat16)
@@ -1416,21 +1616,13 @@
     output, kept = forward(states, mixed)
     cotangent = factor * marks * (output - flat.astype(jnp.float32))
     mixed_grad, skip, _ = backward(cotangent, kept)
-    _, _, returned = back_pass(mixed_grad, skip, qkv, weight_qkv, ids, size, True)
+    returned = back_pass(mixed_grad, skip, qkv, weight_qkv, ids, size)
     cotangent = jnp.where(section_at == 1, cotangent, returned.astype(jnp.float32))
     mixed_grad, skip, grads = backward(cotangent, kept)
-    grad_states, projected, _ = back_pass(mixed_grad, skip, qkv, weight_qkv, ids, size, False)
-    results = jnp.where(section_at == 0, grad_states, output.astype(jnp.bfloat16))
-    results = results.reshape(micro, rows, width)
-    results = lax.ppermute(results, ("ctx", "wt"), swap)[None]
-
     normal_one, _, first_low, hidden, _, normal_two, _ = kept
     down_low, pre_low, grad_first, branch_low = grads
     along = ((0,), (0,))
     total = lambda values: jnp.sum(values.astype(jnp.float32), axis=0)
-    projected = projected.reshape(-1, 3 * local)
-    bias_qkv = total(projected)
-    rows_local = jnp.stack([bias_qkv[:local], bias_qkv[2 * local :]])
     rows_whole = jnp.stack(
         [
             total(branch_low),
@@ -1441,25 +1633,21 @@
             total(cotangent),
         ]
     )
-    mine = (jnp.arange(4) == wt_at).astype(jnp.float32)[None, :, None]
-    rest = jnp.concatenate([rows_local[:, None, :] * mine, rows_whole.reshape(6, 4, local)])
-    rest = jnp.concatenate([rest, jnp.zeros((8, 4, local), jnp.float32)]).transpose(1, 0, 2)
+    rest = rows_whole.reshape(6, 4, local)
+    rest = jnp.pad(rest, ((2, 8), (0, 0), (0, 0))).transpose(1, 0, 2)
     in_rows = total(pre_low).reshape(4, -1, local)
     in_rows = jnp.pad(in_rows, ((0, 0), (0, 16 - in_rows.shape[1]), (0, 2 * local)))
     rest = jnp.concatenate([rest, in_rows], axis=2).reshape(64, width)
-    low = lambda part: part.astype(jnp.bfloat16)
-    sums = reduce_grads(
-        low(dot(full.reshape(-1, width), projected, along)),
-        low(dot(mixed, branch_low, along)),
-        low(dot(first_low, pre_low, along)),
-        low(dot(hidden, down_low, along)),
-        low(rest),
+    operands = (hidden, pre_low, first_low, mixed, down_low, branch_low)
+    final = output.astype(jnp.bfloat16)
+    home, *sums = last_pass(
+        mixed_grad, skip, qkv, weight_qkv, ids, full, rest, operands, final, size
     )
     sums = [part.astype(jnp.float32)[None] for part in sums]
     rest = sums[4]
     in_rows = w_in.shape[2] // width
     bias_back = rest[:, :in_rows, local : 2 * local].reshape(1, -1)
-    return (results, *sums[:4], bias_back, rest[:, :8, :local])
+    return (home[None], *sums[:4], bias_back, rest[:, :8, :local])
 
 
 def solution(mesh):
@@ -1483,5 +1671,5 @@
         P("section", "wt"),
         P("section", None, "wt"),
     )
-    square = mesh.shape["ctx"] == mesh.shape["wt"]
+    square = mesh.shape["ctx"] == mesh.shape["wt"] == 4
     return jax.shard_map(relay if square else shards, mesh=mesh, in_specs=in_specs, out_specs=out_specs, check_vma=False)

time: 636 us -> 544 us (0.86)
  the two profiles are of different devices: /device:TPU:4 before, /device:TPU:0 now
where the time goes in v4:
time: 544 us; the launch traced here: 535 us
  Pallas kernels  425 us (78%)
  matrix products  71.5 us (13%)
  other arithmetic  23.3 us (4%)
  local copies, waits for them, and re-layouts  12.5 us (2%)
    pallas_call x1, Pallas kernels, last_pass(): pl.pallas_call(functools.partial(last_kernel, chunks, size), in_specs=[in...  217 us
    pallas_call x1, Pallas kernels, first_pass(): pl.pallas_call(functools.partial(first_kernel, size), in_specs=[anywhere]...  121 us
    dot_general x12, matrix products, dot(): lax.dot_general(left, right, (dims, ((), ())), preferred_element_type=jnp...  71.5 us
    pallas_call x1, Pallas kernels, back_pass(): pl.pallas_call(functools.partial(back_kernel, size), in_specs=[inside] *...  52.9 us
    pallas_call x1, Pallas kernels, second_pass(): pl.pallas_call(functools.partial(second_kernel, size), in_specs=[anywhere...  34.4 us

profile of v4, /device:TPU:0, one launch (start us, length us, event | category | flops | bytes accessed | tf_op | source)
XLA Modules:
  0.0 534.8 jit_solution(12110924593752040243)
XLA Ops:
  5.5 120.6 %first_pass.1 = (bf16[3,128,1024]{2,1,0:T(8,128)(2,1)S(1)}, bf16[1024,768]{1,0:T(8,128)(2,1)S(1)}, bf16[1024,1024]{1,0:T(8,128)(2,1)}, bf16[1024,4096]{1,0:T(8,1...) custom-call(bf16[3,128,1024]{2,1,0:T(8,128)(2,1)S(1)} %bitcast.92, ...), custom_call_target="tpu_custom_call" | custom-call | tf_op jit(solution)/shard_map/first_pass/pallas_call | solution.py:817
  126.1 1.2 copy-done.3
  127.4 0.9 copy-done.9
  129.6 3.1 fusion.31
  133.8 8.9 %fusion.5 = bf16[384,4096]{1,0:T(8,128)(2,1)S(1)} fusion(bf16[1024,4096]{1,0:T(8,128)(2,1)S(1)} %copy-done.19, f32[4096]{0:T(1024)S(1)} %bitcast.131, f32[384,1024]{1,0:T(8,128)S(1)} %get-tuple-element.74, f32[1024]{0:T(1024)S(1)} %bitcast.126, f32[1024]{0:T(1024)S(1)} %bitcast.116, f32[384]{0:T(512)S(1)} %add_rsqrt_fusion.3, ...), kind=kOutput, calls=%fused_computation.11 | convolution fusion | flops 3259367424 | bytes 13134848 | tf_op jit(solution)/shard_map/dot_general | solution.py:389
  142.8 3.6 fusion.32
  147.0 1.1 copy-done.4
  148.1 34.4 %second_pass.1 = (bf16[3,512,1024]{2,1,0:T(8,128)(2,1)}, bf16[3,512,768]{2,1,0:T(8,128)(2,1)}, bf16[384,1024]{1,0:T(8,128)(2,1)S(1)}) custom-call(bf16[3,128,1024]{2,1,0:T(8,128)(2,1)S(1)} %get-tuple-element.25.refs_0_, bf16[3,128,1024]{2,1,0:T(8,128)(2,1)S(1)} %bitcast.91, bf16[1024,768]{1,0:T(8,128)(2,1)S(1)} %copy-done.4, ...), custom_call_target="tpu_custom_call" | custom-call | tf_op jit(solution)/shard_map/second_pass/pallas_call | solution.py:918
  182.5 1.5 constant_dynamic-slice_fusion
  184.0 1.1 fusion.33
  185.8 12.7 %multiply_convert_fusion = (bf16[384,4096]{1,0:T(8,128)(2,1)S(1)}, bf16[384,4096]{1,0:T(8,128)(2,1)}) fusion(f32[4096]{0:T(1024)S(1)} %bitcast.132, bf16[384,1024]{1,0:T(8,128)(2,1)S(1)} %fusion.13.refs_10_, bf16[1024,4096]{1,0:T(8,128)(2,1)} %get-tuple-element.29), kind=kOutput, calls=%fused_computation.19 | convolution fusion | flops 3263692800 | bytes 15482880 | tf_op jit(solution)/shard_map/dot_general | solution.py:389
  198.5 3.7 fusion.34
  202.5 0.8 multiply_reduce_fusion.12
  203.4 1.6 fusion.14
  205.0 10.9 %fusion = bf16[384,4096]{1,0:T(8,128)(2,1)} fusion(bf16[384,4096]{1,0:T(8,128)(2,1)} %get-tuple-element.62, bf16[4096,1024]{1,0:T(8,128)(2,1)} %get-tuple-element.30, f32[384,1024]{1,0:T(8,128)S(1)} %get-tuple-element.64), kind=kOutput, calls=%fused_computation.6 | convolution fusion | flops 3226337280 | bytes 16252928 | tf_op jit(solution)/shard_map/dot_general | solution.py:389
  215.9 7.2 %fusion.27 = (f32[384]{0:T(512)S(1)}, f32[384]{0:T(512)S(1)}, f32[384,1024]{1,0:T(8,128)S(1)}) fusion(f32[384]{0:T(512)S(1)} %add_rsqrt_fusion.1, f32[384,1024]{1,0:T(8,128)S(1)} %get-tuple-element.78, f32[384]{0:T(512)S(1)} %broadcast_multiply_fusion.9, f32[1024]{0:T(1024)S(1)} %bitcast.120, f32[384,1024]{1,0:T(8,128)S(1)} %get-tuple-element.64, ...), kind=kOutput, calls=%fused_computation.105 | convolution fusion | flops 3223976960 | bytes 16263168 | tf_op jit(solution)/shard_map/dot_general | solution.py:389
  223.6 1.2 copy-done.21
  224.7 1.0 convolution_convert_fusion.1.refs_0_
  225.8 52.9 %back_pass.1 = bf16[384,1024]{1,0:T(8,128)(2,1)S(1)} custom-call(bf16[384,1024]{1,0:T(8,128)(2,1)S(1)} %convolution_convert_fusion.1.refs_0_, f32[384,1024]{1,0:T(8,128)S(1)} %subtract_multiply_fusion.2.refs_1_, bf16[3,512,768]{2,1,0:T(8,128)(2,1)} %get-tuple-element.36.refs_2_, bf16[1024,768]{1,0:T(8,128)(2,1)S(1)} %copy-done.4, s32[3,1,512]{2,1,0:T(1,128)S(1)} %bitcast.96, ...), custom_call_target="tpu_custom_call" | custom-call | tf_op jit(solution)/shard_map/back_pass/pallas_call | solution.py:1099
  278.7 1.3 multiply_reduce_fusion
  280.6 1.6 copy-done.23
  282.2 9.6 %fusion.1.refs_9_ = bf16[384,4096]{1,0:T(8,128)(2,1)S(1)} fusion(bf16[384,4096]{1,0:T(8,128)(2,1)S(1)} %copy-done.23, bf16[384,1024]{1,0:T(8,128)(2,1)S(1)} %get-tuple-element.56.refs_12_, bf16[4096,1024]{1,0:T(8,128)(2,1)} %get-tuple-element.30), kind=kOutput, calls=%fused_computation.7 | convolution fusion | flops 3225944064 | bytes 15466496 | tf_op jit(solution)/shard_map/dot_general | solution.py:389
  291.9 7.8 %multiply_reduce_fusion.1 = (f32[1024]{0:T(1024)S(1)}, f32[384]{0:T(512)S(1)}, f32[384]{0:T(512)S(1)}, f32[1024]{0:T(1024)S(1)}, f32[384,1024]{1,0:T(8,128)S(1)}) fusion(f32[384]{0:T(512)S(1)} %add_rsqrt_fusion.1, f32[384,1024]{1,0:T(8,128)S(1)} %get-tuple-element.78, f32[384]{0:T(512)S(1)} %broadcast_multiply_fusion.9, f32[1024]{0:T(1024)S(1)} %bitcast.121, ...), kind=kOutput, calls=%fused_computation.29 | convolution fusion | flops 3227907072 | bytes 17854464 | tf_op jit(solution)/shard_map/dot_general | solution.py:389
  299.8 1.7 convert_reduce_fusion.2
  301.5 1.9 convolution_convert_fusion.refs_0_
  304.9 217.4 %last_pass.1 = (bf16[3,128,1024]{2,1,0:T(8,128)(2,1)}, bf16[256,3072]{1,0:T(8,128)(2,1)}, bf16[256,1024]{1,0:T(8,128)(2,1)}, bf16[256,4096]{1,0:T(8,128)(2,1)}, ...) custom-call(bf16[384,1024]{1,0:T(8,128)(2,1)} %convolution_convert_fusion.refs_0_, ...), custom_call_target="tpu_custom_call" | custom-call | tf_op jit(solution)/shard_map/last_pass/pallas_call | solution.py:1506
  522.3 0.9 bitcast_convert_fusion.4
  524.4 2.1 bitcast_convert_fusion.3
  526.5 2.0 bitcast_convert_fusion.2
  528.7 2.5 bitcast_convert_fusion.1
  531.2 2.5 bitcast_convert_fusion
  533.7 0.9 copy.36
  (108 shorter events, 12.0 us)
Async XLA Ops:
  0.6 0.7 copy-start
  0.6 4.8 copy-start.7
  0.7 4.8 copy-start.6
  4.7 221.0 %copy-start.8 = (s32[3,2,2,128]{3,2,1,0:T(2,128)}, s32[3,2,2,128]{3,2,1,0:T(2,128)S(1)}, u32[]{:S(2)}) copy-start(s32[3,2,2,128]{3,2,1,0:T(2,128)S(1)} %copy.24) | copy-start | bytes 18436
  5.5 220.3 %copy-start.2 = (s32[3,512,1]{2,1,0:T(8,128)}, s32[3,512,1]{2,1,0:T(8,128)S(1)}, u32[]{:S(2)}) copy-start(s32[3,512,1]{2,1,0:T(8,128)S(1)} %broadcast_in_dim_reshape.6.refs_9_.refs_5_) | copy-start | bytes 18436
  126.1 1.2 copy-start.3
  127.4 0.9 copy-start.9
  129.5 4.2 copy-start.19
  132.7 10.1 %slice-start = ((s8[8388608]{0:T(1024)(128)(4,1)}), s8[4194304]{0:T(1024)(128)(4,1)S(1)}, s32[]{:S(2)}) async-start(s8[8388608]{0:T(1024)(128)(4,1)} %bitcast.145), calls=%async_computation | async-start | bytes 8388608
  133.8 9.0 %slice-start.1 = ((s8[8388608]{0:T(1024)(128)(4,1)}), s8[4194304]{0:T(1024)(128)(4,1)S(1)}, s32[]{:S(2)}) async-start(s8[8388608]{0:T(1024)(128)(4,1)} %bitcast.145), calls=%async_computation.1 | async-start | bytes 8388608
  146.7 1.4 copy-start.4
  148.1 35.9 %copy-start.20 = (bf16[1024,1024]{1,0:T(8,128)(2,1)S(1)}, bf16[1024,1024]{1,0:T(8,128)(2,1)}, u32[]{:S(2)}) copy-start(bf16[1024,1024]{1,0:T(8,128)(2,1)} %get-tuple-element.27) | copy-start | bytes 6291460
  182.5 2.6 copy-start.5
  185.4 13.1 %slice-start.2 = ((s8[8388608]{0:T(1024)(128)(4,1)}), s8[4194304]{0:T(1024)(128)(4,1)S(1)}, s32[]{:S(2)}) async-start(s8[8388608]{0:T(1024)(128)(4,1)} %bitcast.147), calls=%async_computation.2 | async-start | bytes 8388608
  185.8 12.7 %copy-start.11 = (bf16[384,1024]{1,0:T(8,128)(2,1)}, bf16[384,1024]{1,0:T(8,128)(2,1)S(1)}, u32[]{:S(2)}) copy-start(bf16[384,1024]{1,0:T(8,128)(2,1)S(1)} %fusion.13.refs_10_) | copy-start | bytes 2359300
  185.8 12.7 %slice-start.3 = ((s8[8388608]{0:T(1024)(128)(4,1)}), s8[4194304]{0:T(1024)(128)(4,1)S(1)}, s32[]{:S(2)}) async-start(s8[8388608]{0:T(1024)(128)(4,1)} %bitcast.147), calls=%async_computation.3 | async-start | bytes 8388608
  198.5 3.7 copy-start.14
  223.1 1.6 copy-start.21
  280.0 2.2 copy-start.23
  280.6 11.3 %copy-start.12 = (bf16[384,1024]{1,0:T(8,128)(2,1)}, bf16[384,1024]{1,0:T(8,128)(2,1)S(1)}, u32[]{:S(2)}) copy-start(bf16[384,1024]{1,0:T(8,128)(2,1)S(1)} %get-tuple-element.56.refs_12_) | copy-start | bytes 2359300
  291.9 11.6 %copy-start.10 = (bf16[384,4096]{1,0:T(8,128)(2,1)}, bf16[384,4096]{1,0:T(8,128)(2,1)S(1)}, u32[]{:S(2)}) copy-start(bf16[384,4096]{1,0:T(8,128)(2,1)S(1)} %fusion.1.refs_9_) | copy-start | bytes 9437188
  299.8 1.8 copy-start.22
  301.5 2.0 copy-start.13
  522.3 4.2 copy-start.17
  526.5 2.2 copy-start.16
  528.7 2.5 copy-start.15
  531.2 2.5 copy-start.18
  531.2 3.4 copy-start.1

commit v5 on v4

--- a/solution.py
+++ b/solution.py
@@ -464,7 +464,25 @@
     return 2 * lax.rem(place, 2) + place // 2
 
 
-def greet(partners, extra):
+def stripe_of(z, w):
+    return 2 * lax.rem(w, 2) + lax.rem(w // 2 + z, 2)
+
+
+def plane_place(z, w):
+    plane = turned(w)
+    return dict(ctx=plane, wt=2 * lax.rem(z + plane, 2) + z // 2)
+
+
+def home_place(z, w):
+    return dict(ctx=stripe_of(z, w), wt=turned(z))
+
+
+def is_moving(z, w):
+    place = home_place(z, w)
+    return (place["ctx"] != z) | (place["wt"] != w)
+
+
+def greet(partners, extra, meanwhile=lambda: None):
     barrier = pltpu.get_barrier_semaphore()
     for partner in partners:
         pl.semaphore_signal(barrier, 1, device_id=partner, device_id_type=MESH)
@@ -476,6 +494,7 @@
             pl.semaphore_signal(barrier, 1, device_id=partner, device_id_type=MESH)
 
         waits = waits + here.astype(jnp.int32)
+    meanwhile()
     pl.semaphore_wait(barrier, waits)
 
 
@@ -611,23 +630,23 @@
     partners = (across, across_sibling, sibling)
     level = lax.rem(z, 2)
     neighbor = z + 1 - 2 * level
-    moves = w != turned(z)
+    moves, place = is_moving(z, w), plane_place(z, w)
     others = [lax.rem(z + step, 4) for step in (1, 2, 3)]
     greet(
         [{"wt": partner} for partner in partners] + [{"ctx": other} for other in others],
-        [(moves, {"ctx": turned(w), "wt": turned(z)})],
+        [(moves, place), (moves, home_place(z, w))],
     )
 
     def swap(m):
         return wires.remote(
-            ("swap", m), block.at[m], spread.stripe(m, turned(z)), ctx=turned(w), wt=turned(z)
+            ("swap", m), block.at[m], spread.stripe(m, place["wt"]), **place
         )
 
     def stay(m):
         return wires.local(("stay", m), block.at[m], spread.stripe(m, w))
 
     def swap_marks():
-        return wires.remote("swap marks", marks, own_marks, ctx=turned(w), wt=turned(z))
+        return wires.remote("swap marks", marks, own_marks, **place)
 
     def head_copy(part, index):
         column = part * width + partners[index] * local
@@ -713,7 +732,7 @@
             swap(m).start()
         swap_marks().start()
 
-    @pl.when(w == turned(z))
+    @pl.when(jnp.logical_not(moves))
     def _():
         for m in range(micro):
             stay(m).start()
@@ -733,7 +752,7 @@
         def _():
             swap(m).wait_recv()
 
-        @pl.when(w == turned(z))
+        @pl.when(jnp.logical_not(moves))
         def _():
             stay(m).wait()
 
@@ -1000,7 +1019,8 @@
         whole = pl.ds(m * self.pack, self.pack)
         projected = self.projected.at[whole, :]
         same = ids_col[m] == ids_row[m]
-        attend_pack_back(self.size, same, self.qkv.at[m], self.heads_grad.at[m], projected)
+        qkv = self.qkv(m)
+        attend_pack_back(self.size, same, qkv, self.heads_grad.at[m], projected)
         product = dot(projected[...], self.weight[...], ((1,), (1,)))
         self.part[m] = product.astype(jnp.bfloat16)
         for index in range(2):
@@ -1044,7 +1064,7 @@
     z, w = lax.axis_index("ctx"), lax.axis_index("wt")
     block = source.at[pl.ds(m * rows, rows), :]
     if moves:
-        return wires.remote(("home", m), block, target.at[m], ctx=turned(w), wt=turned(z))
+        return wires.remote(("home", m), block, target.at[m], **home_place(z, w))
     return wires.local(("home", m), block, target.at[m])
 
 
@@ -1052,7 +1072,9 @@
     returned, grad_states, projected = refs[6:9]
     wires = Wires(refs[-1])
     section = lax.axis_index("section")
-    back = Back(wires, size, refs[:4] + (refs[4:6], projected, grad_states) + refs[9:-1])
+    qkv = lambda m: refs[2].at[m]
+    given = (refs[0], refs[1], qkv, refs[3], refs[4:6])
+    back = Back(wires, size, given + (projected, grad_states) + refs[9:-1])
     greet([{"wt": partner} for partner in back.partners] + [{"section": 1 - section}], [])
     back.begin(0)
 
@@ -1116,7 +1138,9 @@
 
 CHUNK = 128
 RING = 6
-LAGS = (0, 3, 5, 7, 9)
+TILE = 256
+LAGS = (2, 4, 6, 8)
+AHEAD = 4
 
 
 def sum_into(target, parts, rows):
@@ -1134,17 +1158,18 @@
 
 
 def chunk_list(local, width, hidden):
-    down = [("down", row, CHUNK, 0) for row in range(0, hidden // 4, CHUNK)]
+    down = [("down", 0, CHUNK // 4, 0), ("down", CHUNK // 4, CHUNK // 4, 0)]
+    down += [("down", CHUNK // 2, CHUNK // 2, 0)]
+    down += [("down", row, CHUNK, 0) for row in range(CHUNK, hidden // 4, CHUNK)]
     across = [
         ("in", row, CHUNK, column)
         for column in range(hidden // width)
         for row in range(0, local, CHUNK)
     ]
-    out = [("out", row, CHUNK, 0) for row in range(0, local, CHUNK)]
-    qkv = [("qkv", row, CHUNK, part) for part in range(2) for row in range(0, local, CHUNK)]
-    qkv += [("qkv", row, CHUNK // 2, 2) for row in range(0, local - CHUNK // 2, CHUNK // 2)]
-    qkv += [("qkv", row, CHUNK // 4, 2) for row in range(local - CHUNK // 2, local, CHUNK // 4)]
-    return down + across + out + [("rest", 0, 16, 0)] + qkv
+    out = [("out", row, CHUNK // 2, 0) for row in range(0, local - CHUNK // 2, CHUNK // 2)]
+    out += [("out", row, CHUNK // 4, 0) for row in range(local - CHUNK // 2, local, CHUNK // 4)]
+    qkv = [("qkv", row, CHUNK, part) for part in range(3) for row in range(0, local, CHUNK)]
+    return down + across[:3] + qkv + across[3:] + out + [("rest", 0, 16, 0)]
 
 
 def starts_of(chunks):
@@ -1154,33 +1179,141 @@
 
 
 def last_kernel(chunks, size, *refs):
-    rows_grad, skip, qkv_all, weight, ids_row, ids_col, full_all, rest = refs[:8]
-    hidden, pre, first, mixed, down, branch, final = refs[8:15]
-    home = refs[15]
-    results = dict(zip(("qkv", "out", "in", "down", "rest"), refs[16:21]))
-    grad_states, projected, full, product = refs[21:25]
-    downs, ins, outs, down_both, pre_both, branch_both, rest_in = refs[25:32]
-    near, far, across_in, up_in, side_in = refs[32:37]
+    weight, ids_row, ids_col, gain, inverse_one, rows_low = refs[:6]
+    grad_second, normal_one, qkv_all, full_all, slope = refs[6:11]
+    weight_out, weight_in, weight_down = refs[11:14]
+    hidden, first, mixed, down, final = refs[14:19]
+    home = refs[19]
+    results = dict(zip(("qkv", "out", "in", "down", "rest"), refs[20:25]))
+    grad_states, projected, full, product = refs[25:29]
+    downs, ins, outs, down_both, pre_both, branch_both, rest_in = refs[29:36]
+    near, far, across_in, up_in, side_in = refs[36:41]
+    skip, normal, slopes, qkv_one, rows_grad, rest = refs[41:47]
     wires = Wires(refs[-1])
     z, section = lax.axis_index("ctx"), lax.axis_index("section")
-    given = (rows_grad, skip, qkv_all, weight, (ids_row, ids_col))
-    back = Back(wires, size, given + (projected, grad_states) + refs[37:-1])
+    tokens, width = down.shape
+    count = len(chunks)
+    micro = qkv_all.shape[0]
+
+    def qkv_copy(m):
+        return wires.local(("pack", m), qkv_all.at[m], qkv_one)
+
+    def qkv_of(m):
+        qkv_copy(m).wait()
+        return qkv_one
+
+    given = (rows_grad, skip, qkv_of, weight, (ids_row, ids_col))
+    back = Back(wires, size, given + (projected, grad_states) + refs[47:-1])
     w, sibling, across, across_sibling = wt_places()
     partners = (sibling, across, across_sibling)
-    tokens, width = down.shape
-    count = len(chunks)
     local = back.local
     deep = hidden.shape[1] // 4
     starts, sides_at = starts_of(chunks)
-    moves = w != turned(z)
+    moves = is_moving(z, w)
+    own_rows = pl.ds(0, tokens)
+    blocks = hidden.shape[1] // TILE
+
+    def tile_copies(b):
+        low = full.at[pl.ds((b % 2) * TILE, TILE), :]
+        if b >= blocks:
+            source = weight_out.at[pl.ds((b - blocks) * TILE, TILE), :]
+            return [wires.local(("tile", b), source, low)]
+        columns = pl.ds(b * TILE, TILE)
+        wide = full.at[pl.ds(2 * TILE, width), pl.ds((b % 4) * TILE, TILE)]
+        return [
+            wires.local(("tile", b), weight_down.at[columns, :], low),
+            wires.local(("wide", b), weight_in.at[:, columns], wide),
+            wires.local(("slope", b), slope.at[:, columns], slopes.at[b % 2]),
+        ]
+
+    def start_tiles(b):
+        for copy in tile_copies(b):
+            copy.start()
+
+    def skip_copy():
+        return wires.local("skip", grad_second, skip)
+
+    def normal_copy():
+        return wires.local("normal", normal_one, normal)
+
+    def own_loads():
+        start_tiles(0)
+        start_tiles(1)
+        skip_copy().start()
+        normal_copy().start()
+        qkv_copy(0).start()
+
     greet(
         [{"wt": partner} for partner in partners],
         [
-            (moves, {"ctx": turned(w), "wt": turned(z)}),
+            (moves, home_place(z, w)),
+            (moves, plane_place(z, w)),
             (z > 0, {"ctx": z - 1}),
             (z < 3, {"ctx": z + 1}),
         ],
+        own_loads,
     )
+
+    def step_back(b):
+        if b == 0:
+            skip_copy().wait()
+        for copy in tile_copies(b):
+            copy.wait()
+        columns = pl.ds(b * TILE, TILE)
+        low = full[pl.ds((b % 2) * TILE, TILE), :]
+        wide = full[pl.ds(2 * TILE, width), pl.ds((b % 4) * TILE, TILE)]
+        grad = dot(down_both[own_rows, :], low, ((1,), (1,)))
+        grad = (grad * slopes[b % 2].astype(jnp.float32)).astype(jnp.bfloat16)
+        pre_both[own_rows, columns] = grad
+        skip[...] += dot(grad, wide, ((1,), (1,)))
+        start_tiles(b + 2)
+        if (b + 1) * TILE % width == 0:
+            to_sibling("pre", pre_both, (b + 1) * TILE // width - 1).start()
+
+    def to_sibling(key, array, column):
+        at = pl.ds(column * width, width)
+        target = array.at[pl.ds(tokens, tokens), at]
+        return wires.remote((key, column), array.at[own_rows, at], target, wt=sibling)
+
+    def step_norm():
+        normal_copy().wait()
+        ones = jnp.ones((16, tokens), jnp.bfloat16)
+        grad_first = skip[...]
+        rows = {r: rows_low[r : r + 1, :] for r in (5, 6, 7)}
+        rows[3] = jnp.sum(grad_first * normal[...], axis=0, keepdims=True)
+        rows[4] = jnp.sum(grad_first, axis=0, keepdims=True)
+        grad_summed = norm_back(grad_first, gain[...], normal[...], inverse_one[...])
+        skip[...] = grad_summed
+        branch = grad_summed.astype(jnp.bfloat16)
+        branch_both[own_rows, :] = branch
+        to_sibling("branch", branch_both, 0).start()
+        rows[2] = dot(ones, branch)[:1]
+        sums = dot(ones, pre_both[own_rows, :])[:1]
+        rest[...] = jnp.zeros_like(rest)
+        for j in range(4):
+            for r, row in rows.items():
+                rest[j * 16 + r : j * 16 + r + 1, :local] = row[:, j * local : (j + 1) * local]
+            for r in range(deep // local):
+                at = j * deep + r * local
+                rest[j * 16 + r : j * 16 + r + 1, local : 2 * local] = sums[:, at : at + local]
+        for copy in rest_copies():
+            copy.start()
+
+    def step_out(b):
+        for copy in tile_copies(b):
+            copy.wait()
+        tile = full[pl.ds((b % 2) * TILE, TILE), :]
+        grad = dot(branch_both[own_rows, :], tile, ((1,), (1,))).astype(jnp.bfloat16)
+        rows_grad[:, pl.ds((b - blocks) * TILE, TILE)] = grad
+        if b + 2 < blocks + width // TILE:
+            start_tiles(b + 2)
+
+    def last_out():
+        for b in range(blocks, blocks + width // TILE):
+            step_out(b)
+        full_copy().start()
+        for m in range(micro):
+            back.begin(m)
 
     def both(key, source, target, at, columns, theirs):
         mine = (pl.ds(0, tokens), at)
@@ -1227,8 +1360,6 @@
     loads = [lambda: whole("down", down, down_both, 0)]
     loads += [lambda index=index: down_block(index) for index in range(deep // CHUNK)]
     loads += [lambda half=half: in_block(half) for half in range(halves)]
-    loads += [lambda at=at: whole("pre", pre, pre_both, at) for at in range(columns)]
-    loads += [lambda: whole("branch", branch, branch_both, 0)]
     loads += [lambda half=half: out_block(half) for half in range(halves)]
 
     def full_copy():
@@ -1237,15 +1368,22 @@
     def needs(k):
         kind, row, _, column = chunks[k]
         index = row // CHUNK
+        copies = []
         if kind == "down":
-            return ([whole("down", down, down_both, 0)] if index == 0 else []) + [
-                down_block(index)
-            ]
-        if kind == "in":
-            return [whole("pre", pre, pre_both, column)] * (index == 0) + [
-                in_block(index)
-            ] * (column == 0)
-        return [whole("branch", branch, branch_both, 0)] * (index == 0) + [out_block(index)]
+            if index == 0:
+                copies += whole("down", down, down_both, 0)
+            copies += down_block(index)
+        elif kind == "in":
+            if column == 0:
+                copies += in_block(index)
+            if index == 0:
+                to_sibling("pre", pre_both, column).wait_recv()
+        else:
+            copies += out_block(index)
+            if index == 0:
+                to_sibling("branch", branch_both, 0).wait_recv()
+        for index, copy in enumerate(copies):
+            (copy.wait if index % 2 == 0 else copy.wait_recv)()
 
     def operands(k):
         kind, row, _, column = chunks[k]
@@ -1290,8 +1428,17 @@
     def piece_own(k):
         return wires.local(("piece", k), piece(k, w), piece_place(k))
 
+    direct = [k for k in range(count) if not is_piece(k)]
+    bases = [k for k in direct if chunks[k][1] % CHUNK == 0]
+
+    def base_of(k):
+        return max(base for base in bases if base <= k)
+
+    def far_slot(k, rows):
+        return far.at[bases.index(base_of(k)) % RING, pl.ds(chunks[k][1] % CHUNK, rows), :]
+
     def across_copy(k):
-        source = far.at[k % RING, pl.ds(0, rows_of(k)), :]
+        source = far_slot(k, rows_of(k))
         return wires.remote(("chunk", k), source, slot(across_in, k), wt=across)
 
     def place_of(k, role):
@@ -1337,8 +1484,11 @@
                 piece_copy(k, partner).start()
             piece_own(k).start()
             return
-        if k >= RING:
-            across_copy(k - RING).wait_send()
+        if k in bases:
+            order = bases.index(k)
+            for old in direct:
+                if order >= RING and base_of(old) == bases[order - RING]:
+                    across_copy(old).wait_send()
         if kind == "rest":
             for copy in rest_copies():
                 copy.wait_recv()
@@ -1351,15 +1501,13 @@
             own = own + rest[pl.ds(w * 16, 16), :] + rest_in[0]
             other = rest[pl.ds(across * 16, 16), :] + rest_in[1]
             slot(near, k)[...] = own.astype(jnp.bfloat16)
-            far[k % RING, pl.ds(0, 16), :] = other.astype(jnp.bfloat16)
-        else:
-            for copies in needs(k):
-                for index, copy in enumerate(copies):
-                    (copy.wait if index % 2 == 0 else copy.wait_recv)()
+            far_slot(k, 16)[...] = other.astype(jnp.bfloat16)
+        elif k in bases:
+            needs(k)
             left, right = operands(k)
             grad = dot(left, right, ((0,), (0,))).astype(jnp.bfloat16)
-            slot(near, k)[...] = grad[:CHUNK]
-            far[k % RING] = grad[CHUNK:]
+            near[pl.ds(starts[k], CHUNK), :] = grad[:CHUNK]
+            far_slot(k, CHUNK)[...] = grad[CHUNK:]
         across_copy(k).start()
 
     def settle(k):
@@ -1410,7 +1558,7 @@
         def _():
             do(swap_back(wires, back.rows, source, home, m, True))
 
-        @pl.when((w == turned(z)) & here)
+        @pl.when(jnp.logical_not(moves) & here)
         def _():
             do(swap_back(wires, back.rows, source, home, m, False))
 
@@ -1421,36 +1569,38 @@
     def final_home(m):
         go_home(m, final, section == 1, lambda copy: copy.start())
 
-    tail = count - 9
     beside = {
-        1: [lambda: back.work(0)],
-        3: [lambda: back.work(1)],
-        5: [lambda: back.work(2)],
-        8: [lambda: final_home(0)],
-        12: [lambda: final_home(1)],
-        16: [lambda: final_home(2)],
-        tail: [lambda: back.cross(0)],
-        tail + 1: [lambda: back.cross(1)],
-        tail + 3: [lambda: back.cross(2), lambda: done(0)],
-        tail + 5: [lambda: done(1)],
-        tail + 7: [lambda: done(2)],
+        9: [lambda: back.work(0), lambda: qkv_copy(1).start()],
+        10: [lambda: back.work(1), lambda: qkv_copy(2).start()],
+        11: [lambda: back.work(2)],
+        17: [lambda: final_home(0)],
+        18: [lambda: final_home(1)],
+        19: [lambda: final_home(2)],
+        20: [lambda: back.cross(0)],
+        22: [lambda: back.cross(1)],
+        24: [lambda: back.cross(2), lambda: done(0)],
+        26: [lambda: done(1)],
+        28: [lambda: done(2)],
+        7: [step_norm, last_out],
     }
-
-    for m in range(back.micro):
-        back.begin(m)
-    for copy in rest_copies():
-        copy.start()
+    steps = iter(range(blocks))
+    for tick, many in enumerate((0, 0, 2, 3, 3, 4, 4)):
+        beside[tick] = [functools.partial(step_back, next(steps)) for _ in range(many)]
+
     for load in loads:
         for copy in load():
             copy.start()
-    full_copy().start()
-    stages = (begin, settle, aside, finish, forward)
+    stages = (settle, aside, finish, forward)
+    begun, first_piece = 0, min(k for k in range(count) if is_piece(k))
     for tick in range(count + LAGS[-1]):
-        if tick < count and chunks[tick][0] == "qkv" and chunks[tick - 1][0] != "qkv":
-            full_copy().wait()
-        for lag, stage in zip(LAGS, stages):
+        for lag, stage in reversed(list(zip(LAGS, stages))):
             if 0 <= tick - lag < count:
                 stage(tick - lag)
+        while begun < min(count, tick + 1 + max(0, min(AHEAD, tick - 11))):
+            if begun == first_piece:
+                full_copy().wait()
+            begin(begun)
+            begun += 1
         for step in beside.get(tick, []):
             step()
     for m in range(back.micro):
@@ -1462,9 +1612,12 @@
         for index, copy in enumerate(load()):
             if index % 2 == 1:
                 copy.wait_send()
-    direct = [k for k in range(count) if not is_piece(k)]
-    for k in direct[-RING:]:
-        across_copy(k).wait_send()
+    for column in range(columns):
+        to_sibling("pre", pre_both, column).wait_send()
+    to_sibling("branch", branch_both, 0).wait_send()
+    for k in direct:
+        if base_of(k) in bases[-RING:]:
+            across_copy(k).wait_send()
     for k in range(count):
         if is_piece(k):
             for index in range(3):
@@ -1489,14 +1642,13 @@
         on(k, 1, owner)
 
 
-def last_pass(rows_grad, skip, qkv, weight, ids, full, rest, operands, final, size):
-    micro, pack, local = qkv.shape
+def last_pass(weight, ids, gain, inverse_one, rows_low, arrays, weights, operands, size):
+    micro, pack, local = arrays[2].shape
     local = local // 3
-    tokens, width = rows_grad.shape
+    tokens, width = operands[3].shape
     hidden = operands[0].shape[1]
     chunks = chunk_list(local, width, hidden)
     count = len(chunks)
-    direct = sum(chunk[0] != "qkv" for chunk in chunks)
     starts, sides_at = starts_of(chunks)
     inside = pl.BlockSpec(memory_space=pltpu.VMEM)
     anywhere = pl.BlockSpec(memory_space=pl.ANY)
@@ -1505,7 +1657,7 @@
     halves = local // CHUNK
     return pl.pallas_call(
         functools.partial(last_kernel, chunks, size),
-        in_specs=[inside] * 6 + [anywhere, inside] + [anywhere] * 7,
+        in_specs=[inside] * 6 + [anywhere] * 13,
         out_specs=[anywhere] * 6,
         out_shape=[
             low(micro, pack // 4, width),
@@ -1529,27 +1681,32 @@
             pltpu.VMEM((2, 16, width), jnp.float32),
             room(starts[count], width),
             room(RING, CHUNK, width),
-            room(starts[direct], width),
+            room(starts[count], width),
             room(starts[count], width),
             room(max(sides_at[count:]), width),
+            pltpu.VMEM((tokens, width), jnp.float32),
+            pltpu.VMEM((tokens, width), jnp.float32),
+            room(2, tokens, TILE),
+            room(pack, 3 * local),
+            room(tokens, width),
+            pltpu.VMEM((64, width), jnp.float32),
         ]
         + back_scratch(micro, pack, local, width)
-        + [pltpu.SemaphoreType.DMA((720,))],
+        + [pltpu.SemaphoreType.DMA((900,))],
         compiler_params=pltpu.CompilerParams(
-            collective_id=1, has_side_effects=True, vmem_limit_bytes=62 * 2**20
+            collective_id=1, has_side_effects=True, vmem_limit_bytes=63 * 2**20
         ),
         name="last_pass",
     )(
-        rows_grad,
-        skip,
-        qkv,
         weight,
         ids[:, None, :],
         ids[:, :, None],
-        full.reshape(micro * pack, width),
-        rest,
+        gain,
+        inverse_one,
+        rows_low,
+        *arrays,
+        *weights,
         *operands,
-        final,
     )
 
 
@@ -1566,8 +1723,10 @@
     own_rows = vectors[0].astype(jnp.float32)
     qkv_bias = jnp.concatenate([own_rows[0], jnp.zeros((local,), jnp.float32), own_rows[1]])[None]
     my_lengths = lax.dynamic_index_in_dim(lengths, turned(ctx_at), 1, keepdims=False)
-    ids = jax.vmap(lambda row: dealt_ids(row, pack, count_ctx))(my_lengths)
-    ids = ids.reshape(micro, 2, 2, rows).swapaxes(1, 2).reshape(micro, pack)
+    ends = jnp.cumsum(my_lengths, axis=1)
+    stripes = stripe_of(ctx_at, jnp.arange(count_ctx, dtype=jnp.int32))
+    places = jnp.arange(rows, dtype=jnp.int32)[None, :] * count_ctx + stripes[:, None]
+    ids = jnp.sum((places.reshape(1, pack, 1) >= ends[:, None, :]).astype(jnp.int32), axis=2)
     small = jnp.concatenate([vectors[0], bias_in[0].reshape(-1, local)], axis=0)
     small = jnp.pad(small, ((0, 16 - small.shape[0]), (0, 0)))
     marks = jnp.pad(valid.astype(jnp.float32), ((0, 8 - micro), (0, 0)))
@@ -1618,30 +1777,21 @@
     mixed_grad, skip, _ = backward(cotangent, kept)
     returned = back_pass(mixed_grad, skip, qkv, weight_qkv, ids, size)
     cotangent = jnp.where(section_at == 1, cotangent, returned.astype(jnp.float32))
-    mixed_grad, skip, grads = backward(cotangent, kept)
-    normal_one, _, first_low, hidden, _, normal_two, _ = kept
-    down_low, pre_low, grad_first, branch_low = grads
-    along = ((0,), (0,))
+    normal_one, inverse_one, first_low, hidden, slope, normal_two, inverse_two = kept
+    grad_second = norm_back(cotangent, vector_rows[6], normal_two, inverse_two)
+    down_low = grad_second.astype(jnp.bfloat16)
     total = lambda values: jnp.sum(values.astype(jnp.float32), axis=0)
-    rows_whole = jnp.stack(
-        [
-            total(branch_low),
-            total(grad_first * normal_one),
-            total(grad_first),
-            total(down_low),
-            total(cotangent * normal_two),
-            total(cotangent),
-        ]
-    )
-    rest = rows_whole.reshape(6, 4, local)
-    rest = jnp.pad(rest, ((2, 8), (0, 0), (0, 0))).transpose(1, 0, 2)
-    in_rows = total(pre_low).reshape(4, -1, local)
-    in_rows = jnp.pad(in_rows, ((0, 0), (0, 16 - in_rows.shape[1]), (0, 2 * local)))
-    rest = jnp.concatenate([rest, in_rows], axis=2).reshape(64, width)
-    operands = (hidden, pre_low, first_low, mixed, down_low, branch_low)
-    final = output.astype(jnp.bfloat16)
+    rows_low = jnp.stack([total(down_low), total(cotangent * normal_two), total(cotangent)])
     home, *sums = last_pass(
-        mixed_grad, skip, qkv, weight_qkv, ids, full, rest, operands, final, size
+        weight_qkv,
+        ids,
+        vector_rows[3:4],
+        inverse_one,
+        jnp.pad(rows_low, ((5, 0), (0, 0))),
+        (grad_second, normal_one, qkv, full.reshape(-1, width), slope),
+        (weight_out, weight_in, weight_down),
+        (hidden, first_low, mixed, down_low, output.astype(jnp.bfloat16)),
+        size,
     )
     sums = [part.astype(jnp.float32)[None] for part in sums]
     rest = sums[4]

time: 544 us -> 523 us (0.961)
  the two profiles are of different devices: /device:TPU:0 before, /device:TPU:4 now
where the time goes in v5:
time: 523 us; the launch traced here: 514 us
  Pallas kernels  428 us (82%)
  matrix products  49.7 us (10%)
  other arithmetic  24.1 us (5%)
  local copies, waits for them, and re-layouts  10.7 us (2%)
    pallas_call x1, Pallas kernels, last_pass(): pl.pallas_call(functools.partial(last_kernel, chunks, size), in_specs=[in...  214 us
    pallas_call x1, Pallas kernels, first_pass(): pl.pallas_call(functools.partial(first_kernel, size), in_specs=[anywhere]...  117 us
    pallas_call x1, Pallas kernels, back_pass(): pl.pallas_call(functools.partial(back_kernel, size), in_specs=[inside] *...  52.5 us
    dot_general x9, matrix products, dot(): lax.dot_general(left, right, (dims, ((), ())), preferred_element_type=jnp...  49.7 us
    pallas_call x1, Pallas kernels, second_pass(): pl.pallas_call(functools.partial(second_kernel, size), in_specs=[anywhere...  45 us

profile of v5, /device:TPU:4, one launch (start us, length us, event | category | flops | bytes accessed | tf_op | source)
XLA Modules:
  0.0 514.3 jit_solution(17839919632502857162)
XLA Ops:
  2.2 0.7 reduce
  3.1 0.7 fusion.23.refs_5_
  4.8 1.1 copy-done.4
  5.9 1.0 copy-done.6
  7.0 116.6 %first_pass.1 = (bf16[3,128,1024]{2,1,0:T(8,128)(2,1)S(1)}, bf16[1024,768]{1,0:T(8,128)(2,1)S(1)}, bf16[1024,1024]{1,0:T(8,128)(2,1)}, bf16[1024,4096]{1,0:T(8,1...) custom-call(bf16[3,128,1024]{2,1,0:T(8,128)(2,1)S(1)} %bitcast.89, ...), custom_call_target="tpu_custom_call" | custom-call | tf_op jit(solution)/shard_map/first_pass/pallas_call | solution.py:836
  123.6 0.9 copy-done.8
  126.0 3.1 fusion.31
  129.3 0.8 copy-done.10
  130.1 9.3 %fusion.3 = bf16[384,4096]{1,0:T(8,128)(2,1)S(1)} fusion(bf16[1024,4096]{1,0:T(8,128)(2,1)S(1)} %copy-done.10, f32[4096]{0:T(1024)S(1)} %bitcast.126, f32[384,1024]{1,0:T(8,128)S(1)} %get-tuple-element.68, f32[1024]{0:T(1024)S(1)} %bitcast.118, f32[1024]{0:T(1024)S(1)} %bitcast.112, f32[384]{0:T(512)S(1)} %add_rsqrt_fusion.3, ...), kind=kOutput, calls=%fused_computation.7 | convolution fusion | flops 3259367424 | bytes 13134848 | tf_op jit(solution)/shard_map/dot_general | solution.py:389
  139.5 3.7 fusion.32
  143.8 45.0 %second_pass.1 = (bf16[3,512,1024]{2,1,0:T(8,128)(2,1)}, bf16[3,512,768]{2,1,0:T(8,128)(2,1)}, bf16[384,1024]{1,0:T(8,128)(2,1)S(1)}) custom-call(bf16[3,128,1024]{2,1,0:T(8,128)(2,1)S(1)} %get-tuple-element.27.refs_0_, bf16[3,128,1024]{2,1,0:T(8,128)(2,1)S(1)} %bitcast.88, bf16[1024,768]{1,0:T(8,128)(2,1)S(1)} %get-tuple-element.25.refs_2_.refs_3_.refs_0_, ...), custom_call_target="tpu_custom_call" | custom-call | tf_op jit(solution)/shard_map/second_pass/pallas_call | solution.py:937
  188.8 1.5 constant_dynamic-slice_fusion
  190.2 2.7 fusion.33
  193.3 0.8 rsqrt.34.refs_4_
  194.5 10.2 %fusion.9 = (bf16[384,4096]{1,0:T(8,128)(2,1)}, bf16[384,4096]{1,0:T(8,128)(2,1)S(1)}) fusion(f32[4096]{0:T(1024)S(1)} %bitcast.127, bf16[384,1024]{1,0:T(8,128)(2,1)S(1)} %get-tuple-element.54.refs_15_, bf16[1024,4096]{1,0:T(8,128)(2,1)S(1)} %copy-done.10), kind=kOutput, calls=%fused_computation.13 | convolution fusion | flops 3263692800 | bytes 15482880 | tf_op jit(solution)/shard_map/dot_general | solution.py:389
  204.7 3.7 fusion.34
  208.7 1.7 multiply_reduce_fusion.9
  210.4 2.0 subtract_multiply_fusion.2
  212.4 9.8 %multiply_convert_fusion = bf16[384,4096]{1,0:T(8,128)(2,1)} fusion(bf16[384,4096]{1,0:T(8,128)(2,1)} %get-tuple-element.56.refs_10_, bf16[4096,1024]{1,0:T(8,128)(2,1)} %get-tuple-element.31.refs_13_, f32[384,1024]{1,0:T(8,128)} %subtract_multiply_fusion.2), kind=kOutput, calls=%fused_computation.14 | convolution fusion | flops 3226337280 | bytes 16252928 | tf_op jit(solution)/shard_map/dot_general | solution.py:389
  222.2 6.3 %fusion.28 = (f32[384]{0:T(512)S(1)}, f32[384]{0:T(512)S(1)}, f32[384,1024]{1,0:T(8,128)S(1)}) fusion(f32[384,1024]{1,0:T(8,128)S(1)} %get-tuple-element.55.refs_7_, f32[1024]{0:T(1024)S(1)} %bitcast.116, f32[384,1024]{1,0:T(8,128)} %subtract_multiply_fusion.2, bf16[384,4096]{1,0:T(8,128)(2,1)} %multiply_convert_fusion, bf16[1024,4096]{1,0:T(8,128)(2,1)S(1)} %copy-done.10), kind=kOutput, calls=%fused_computation.101 | convolution fusion | flops 3223190528 | bytes 16260096 | tf_op jit(solution)/shard_map/dot_general | solution.py:389
  228.9 1.3 copy-done.13
  230.1 1.0 convolution_convert_fusion.refs_0_
  231.2 52.5 %back_pass.1 = bf16[384,1024]{1,0:T(8,128)(2,1)S(1)} custom-call(bf16[384,1024]{1,0:T(8,128)(2,1)S(1)} %convolution_convert_fusion.refs_0_, f32[384,1024]{1,0:T(8,128)S(1)} %subtract_multiply_fusion.1.refs_1_, bf16[3,512,768]{2,1,0:T(8,128)(2,1)} %get-tuple-element.36.refs_2_.refs_8_, bf16[1024,768]{1,0:T(8,128)(2,1)S(1)} %get-tuple-element.25.refs_2_.refs_3_.refs_0_, ...), custom_call_target="tpu_custom_call" | custom-call | tf_op jit(solution)/shard_map/back_pass/pallas_call | solution.py:1121
  283.7 1.2 multiply_reduce_fusion.8
  285.0 2.4 convert_reduce_fusion
  288.0 213.8 %last_pass.1 = (bf16[3,128,1024]{2,1,0:T(8,128)(2,1)}, bf16[256,3072]{1,0:T(8,128)(2,1)}, bf16[256,1024]{1,0:T(8,128)(2,1)}, bf16[256,4096]{1,0:T(8,128)(2,1)}, ...) custom-call(bf16[1024,768]{1,0:T(8,128)(2,1)} %copy-done.3, s32[3,1,512]{2,1,0:T(1,128)} %copy-done.7, ...), custom_call_target="tpu_custom_call" | custom-call | tf_op jit(solution)/shard_map/last_pass/pallas_call | solution.py:1658
  501.8 0.9 bitcast_convert_fusion.4
  503.9 2.1 bitcast_convert_fusion.3
  506.0 2.0 bitcast_convert_fusion.2
  508.2 2.5 bitcast_convert_fusion.1
  510.7 2.5 bitcast_convert_fusion
  513.2 0.9 copy.36
  (90 shorter events, 7.7 us)
Async XLA Ops:
  0.6 0.7 copy-start
  3.0 228.1 %copy-start.7 = (s32[3,1,512]{2,1,0:T(1,128)}, s32[3,1,512]{2,1,0:T(1,128)S(1)}, u32[]{:S(2)}) copy-start(s32[3,1,512]{2,1,0:T(1,128)S(1)} %broadcast_in_dim.72.refs_8_.refs_4_.refs_1_) | copy-start | bytes 18436
  4.8 1.1 copy-start.4
  5.9 1.0 copy-start.6
  7.0 224.2 %copy-start.2 = (s32[3,512,1]{2,1,0:T(8,128)}, s32[3,512,1]{2,1,0:T(8,128)S(1)}, u32[]{:S(2)}) copy-start(s32[3,512,1]{2,1,0:T(8,128)S(1)} %copy.25.refs_9_.refs_5_.refs_2_) | copy-start | bytes 18436
  123.6 0.9 copy-start.8
  124.5 106.7 %copy-start.3 = (bf16[1024,768]{1,0:T(8,128)(2,1)}, bf16[1024,768]{1,0:T(8,128)(2,1)S(1)}, u32[]{:S(2)}) copy-start(bf16[1024,768]{1,0:T(8,128)(2,1)S(1)} %get-tuple-element.25.refs_2_.refs_3_.refs_0_) | copy-start | bytes 4718596
  125.9 4.3 copy-start.10
  125.9 96.3 %copy-start.18 = (f32[1,4,256]{2,0,1:T(1,128)}, f32[1,4,256]{2,0,1:T(1,128)S(1)}, u32[]{:S(2)}) copy-start(f32[1,4,256]{2,0,1:T(1,128)S(1)} %get-tuple-element.64) | copy-start | bytes 12292
  129.0 10.4 %slice-start = ((s8[8388608]{0:T(1024)(128)(4,1)}), s8[4194304]{0:T(1024)(128)(4,1)S(1)}, s32[]{:S(2)}) async-start(s8[8388608]{0:T(1024)(128)(4,1)} %bitcast.91), calls=%async_computation | async-start | bytes 8388608
  130.1 9.3 %slice-start.1 = ((s8[8388608]{0:T(1024)(128)(4,1)}), s8[4194304]{0:T(1024)(128)(4,1)S(1)}, s32[]{:S(2)}) async-start(s8[8388608]{0:T(1024)(128)(4,1)} %bitcast.91), calls=%async_computation.1 | async-start | bytes 8388608
  188.8 4.2 copy-start.5
  194.1 10.6 %slice-start.2 = ((s8[8388608]{0:T(1024)(128)(4,1)}), s8[4194304]{0:T(1024)(128)(4,1)S(1)}, s32[]{:S(2)}) async-start(s8[8388608]{0:T(1024)(128)(4,1)} %bitcast.93), calls=%async_computation.2 | async-start | bytes 8388608
  194.4 10.2 %copy-start.12 = (bf16[384,1024]{1,0:T(8,128)(2,1)}, bf16[384,1024]{1,0:T(8,128)(2,1)S(1)}, u32[]{:S(2)}) copy-start(bf16[384,1024]{1,0:T(8,128)(2,1)S(1)} %get-tuple-element.54.refs_15_) | copy-start | bytes 2359300
  194.4 34.1 %copy-start.9 = (f32[384,1024]{1,0:T(8,128)}, f32[384,1024]{1,0:T(8,128)S(1)}, u32[]{:S(2)}) copy-start(f32[384,1024]{1,0:T(8,128)S(1)} %get-tuple-element.55.refs_7_) | copy-start | bytes 4718596
  194.4 10.2 %slice-start.3 = ((s8[8388608]{0:T(1024)(128)(4,1)}), s8[4194304]{0:T(1024)(128)(4,1)S(1)}, s32[]{:S(2)}) async-start(s8[8388608]{0:T(1024)(128)(4,1)} %bitcast.93), calls=%async_computation.3 | async-start | bytes 8388608
  204.6 3.7 copy-start.11
  228.6 1.6 copy-start.13
  501.8 4.2 copy-start.16
  506.0 2.2 copy-start.15
  508.2 2.5 copy-start.14
  510.7 2.5 copy-start.17
  510.7 3.4 copy-start.1

commit v6 on v5

--- a/solution.py
+++ b/solution.py
@@ -600,24 +600,72 @@
             self.mixed_rows.at[pl.ds(m * self.rows, self.rows), heads],
         )
 
-    def finish(self, m):
+    def arrived_back(self, m):
+        for copy in self.back(m):
+            copy.wait_recv()
+        self.own_back(m).wait()
+
+    def end(self, m):
         for copy in (self.to_sibling(m), self.to_across(m), self.passed(m)):
             copy.wait_send()
         for copy in self.back(m):
-            copy.wait()
-        self.own_back(m).wait()
+            copy.wait_send()
 
 
 def project(full, weight, bias, qkv):
     qkv[...] = (dot(full[...], weight[...]) + bias[...]).astype(jnp.bfloat16)
+
+
+BLOCK = 512
+
+
+def feed_start(states, mixed, weight_out, rows):
+    summed = states.astype(jnp.float32) + (dot(mixed, weight_out) + rows[2:3, :])
+    normal, inverse = norm_parts(summed)
+    return normal, inverse, normal * rows[3:4, :] + rows[4:5, :]
+
+
+def feed_forward(at, states, mixed, weights, rows, in_bias, kept):
+    weight_out, weight_in, weight_down = weights
+    normal, inverse, first = feed_start(states, mixed, weight_out[...], rows)
+    kept["normal_one"][at, :] = normal
+    kept["inverse_one"][at, :] = inverse
+    low = first.astype(jnp.bfloat16)
+    kept["first"][at, :] = low
+    total = first + rows[5:6, :]
+    for column in range(0, weight_in.shape[1], BLOCK):
+        columns = pl.ds(column, BLOCK)
+        hidden, slope = gelu_both(dot(low, weight_in[:, columns]) + in_bias[:, columns])
+        hidden = hidden.astype(jnp.bfloat16)
+        kept["hidden"][at, columns] = hidden
+        kept["slope"][at, columns] = slope.astype(jnp.bfloat16)
+        total = total + dot(hidden, weight_down[columns, :])
+    normal, inverse = norm_parts(total)
+    kept["normal_two"][at, :] = normal
+    kept["inverse_two"][at, :] = inverse
+    return normal * rows[6:7, :] + rows[7:8, :]
+
+
+def feed_backward(at, grad, weights, rows, kept):
+    weight_out, weight_in, weight_down = weights
+    total = norm_back(grad, rows[6:7, :], kept["normal_two"][at, :], kept["inverse_two"][at, :])
+    low = total.astype(jnp.bfloat16)
+    for column in range(0, weight_in.shape[1], BLOCK):
+        columns = pl.ds(column, BLOCK)
+        inner = dot(low, weight_down[columns, :], ((1,), (1,)))
+        inner = (inner * kept["slope"][at, columns].astype(jnp.float32)).astype(jnp.bfloat16)
+        total = total + dot(inner, weight_in[:, columns], ((1,), (1,)))
+    total = norm_back(total, rows[3:4, :], kept["normal_one"][at, :], kept["inverse_one"][at, :])
+    branch = total.astype(jnp.bfloat16)
+    return total, dot(branch, weight_out[...], ((1,), (1,))).astype(jnp.bfloat16)
 
 
 def first_kernel(size, *refs):
     block, shard_qkv, shard_out, shard_in, shard_down, small, marks, bias = refs[:8]
     ids_row, ids_col = refs[8:10]
-    own, weight, whole_out, whole_in, whole_down, smalls, own_marks, count = refs[10:18]
-    mixed_rows, full, qkv, mixed, marks_wt, marks_ctx = refs[18:24]
-    held_out, held_in, held_down, sems = refs[24:]
+    own, weight, kept_out, kept_in, kept_down, layer_rows, in_bias, own_marks, count = refs[10:19]
+    leaving, full, qkv, mixed, marks_wt, marks_ctx = refs[19:25]
+    whole_out, whole_in, whole_down, smalls, mixed_rows, first, inner, total, sems = refs[25:]
     micro, rows, width = block.shape
     local = small.shape[1]
     hidden = shard_in.shape[1]
@@ -719,17 +767,15 @@
             index
         ]
         size = shard.shape[0]
-        held = (held_out, held_in, held_down)[index]
-        place = whole.at[pl.ds(w * size, size), :]
-        return (
-            wires.local(("shard in", index), shard, held),
-            wires.local(("shard own", index), held, place),
-        )
+        return wires.local(("shard", index), shard, whole.at[pl.ds(w * size, size), :])
+
+    def shard_ready(index):
+        shard_own(index).wait()
+        shard_sibling(index).wait_recv()
 
     @pl.when(moves)
     def _():
-        for m in range(micro):
-            swap(m).start()
+        swap(0).start()
         swap_marks().start()
 
     @pl.when(jnp.logical_not(moves))
@@ -759,18 +805,21 @@
     def own_copy(m):
         return wires.local(("own", m), spread.stripe(m, w), own.at[m])
 
+    @pl.when(moves)
+    def _():
+        swap(0).wait_send()
+        for m in range(1, micro):
+            swap(m).start()
+
     for m in range(micro):
         arrive(m)
         spread.send(m)
         own_copy(m).start()
-    for k in range(chunks):
+    for k in range(micro):
         y_copy(k).start()
     for index in range(3):
         shard_sibling(index).start()
-        shard_own(index)[0].start()
-    for index in range(3):
-        shard_own(index)[0].wait()
-        shard_own(index)[1].start()
+        shard_own(index).start()
     for index in range(3):
         marks_copy(index).wait_recv()
     count[...] = marks[...] + marks_wt[0] + marks_wt[1] + marks_wt[2]
@@ -780,47 +829,115 @@
         for index in range(3):
             head_copy(part, index).wait_recv()
         head_own(part).wait()
+    def passing(k):
+        y_copy(k).wait_recv()
+        if k + micro < chunks:
+            y_copy(k + micro).start()
+        z_copy(k).start()
+        core_copy(k, 0).start()
+
+    def passed(k):
+        z_copy(k).wait_recv()
+        core_copy(k, 1).start()
+
+    def stored(k):
+        if k == 0:
+            return [wires.local(("stored", k), whole_out, kept_out)]
+        if k <= columns:
+            at = pl.ds((k - 1) * width, width)
+            return [wires.local(("stored", k), whole_in.at[:, at], kept_in.at[:, at])]
+        return [
+            wires.local(("stored", k, row), whole_down.at[at, :], kept_down.at[at, :])
+            for row, at in pair_rows(k)
+        ]
+
+    def pair_rows(k):
+        if (k - columns) % 2 == 1:
+            return []
+        first_row = (k - 2 - columns) * deep
+        return [
+            (row, pl.ds(row, 2 * deep)) for row in range(first_row, hidden, 4 * deep)
+        ]
+
+    def compute(k):
+        core_copy(k, 0).wait_recv()
+        core_copy(k, 1).wait_recv()
+        if k == 0:
+            shard_ready(0)
+            for m in range(micro):
+                spread.arrived_back(m)
+            states = [spread.stripe(m, w)[...] for m in range(micro)]
+            states = jnp.concatenate(states, axis=0)
+            values = feed_start(states, mixed_rows[...], whole_out[...], layer_rows)[2]
+            first[...] = values.astype(jnp.bfloat16)
+            total[...] = values + layer_rows[5:6, :]
+        elif k <= columns:
+            if k == 1:
+                shard_ready(1)
+            for column in range((k - 1) * width, k * width, BLOCK):
+                at = pl.ds(column, BLOCK)
+                values = gelu_both(dot(first[...], whole_in[:, at]) + in_bias[:, at])[0]
+                inner[:, at] = values.astype(jnp.bfloat16)
+        else:
+            if k == columns + 1:
+                shard_ready(2)
+            for _, at in pair_rows(k):
+                total[...] += dot(inner[:, at], whole_down[at, :])
+        for copy in stored(k):
+            copy.start()
+
+    for index in range(3):
+        small_copy(index).wait_recv()
+    for j in range(4):
+        at = pl.ds(j * local, local)
+        layer_rows[:, at] = smalls[j, :8, :].astype(jnp.float32)
+        for row in range(columns):
+            at = pl.ds(j * 8 * deep + row * local, local)
+            in_bias[:, at] = smalls[j, 8 + row : 9 + row, :].astype(jnp.float32)
     for m in range(micro):
         spread.hand_on(m)
         spread.settle(m)
         project(full.at[m], weight, bias, qkv.at[0])
         attend_pack(size, ids_col[m] == ids_row[m], qkv.at[0], mixed.at[m])
         spread.send_back(m)
-        y_copy(m).wait_recv()
-        z_copy(m).start()
-        core_copy(m, 0).start()
+        passing(m)
+    passed(0)
     for k in range(micro, chunks):
-        y_copy(k).wait_recv()
-        z_copy(k).start()
-        core_copy(k, 0).start()
-        z_copy(k - micro).wait_recv()
-        core_copy(k - micro, 1).start()
-    for k in range(chunks - micro, chunks):
-        z_copy(k).wait_recv()
-        core_copy(k, 1).start()
+        passing(k)
+        passed(k - 2)
+        if k >= micro + 2:
+            compute(k - micro - 2)
+    passed(chunks - 2)
+    for k in range(chunks - micro - 2, chunks):
+        if k == chunks - 2:
+            passed(chunks - 1)
+        compute(k)
+    values = norm_parts(total[...])[0] * layer_rows[6:7, :] + layer_rows[7:8, :]
+    leaving[...] = values.astype(jnp.bfloat16)
     for index in range(3):
         count_copy(index).wait()
     count[...] = count[...] + marks_ctx[0] + marks_ctx[1] + marks_ctx[2]
     for m in range(micro):
-        spread.finish(m)
+        spread.end(m)
         own_copy(m).wait()
     for part in range(3):
         for index in range(3):
             head_copy(part, index).wait_send()
     for index in range(3):
-        small_copy(index).wait()
+        small_copy(index).wait_send()
         marks_copy(index).wait_send()
-        shard_sibling(index).wait()
-        shard_own(index)[1].wait()
+        shard_sibling(index).wait_send()
     for k in range(chunks):
         y_copy(k).wait_send()
         z_copy(k).wait_send()
         for side in range(2):
-            core_copy(k, side).wait()
+            core_copy(k, side).wait_send()
+        for copy in stored(k):
+            copy.wait()
 
     @pl.when(moves)
     def _():
-        for m in range(micro):
+        for m in range(1, micro):
             swap(m).wait_send()
         swap_marks().wait()
 
@@ -829,129 +946,49 @@
     micro, rows, width = block.shape
     local = small.shape[1]
     pack = ids.shape[1]
+    tokens, hidden = micro * rows, shards[2].shape[1]
     anywhere = pl.BlockSpec(memory_space=pl.ANY)
     inside = pl.BlockSpec(memory_space=pltpu.VMEM)
     low = lambda *shape: jax.ShapeDtypeStruct(shape, jnp.bfloat16)
-    word = jax.ShapeDtypeStruct(marks.shape, jnp.float32)
+    word = lambda *shape: jax.ShapeDtypeStruct(shape, jnp.float32)
+    room = lambda *shape: pltpu.VMEM(shape, jnp.bfloat16)
     return pl.pallas_call(
         functools.partial(first_kernel, size),
         in_specs=[anywhere] * 5 + [inside] * 5,
-        out_specs=[anywhere, inside] + [anywhere] * 3 + [inside] * 4,
+        out_specs=[anywhere, inside] + [anywhere] * 3 + [inside] * 5,
         out_shape=[
             low(micro, rows, width),
             low(width, 3 * local),
-            low(4 * shards[1].shape[0], shards[1].shape[1]),
-            low(4 * shards[2].shape[0], shards[2].shape[1]),
-            low(4 * shards[3].shape[0], shards[3].shape[1]),
-            low(4, *small.shape),
-            word,
-            word,
-            low(micro * rows, width),
+            low(width, width),
+            low(width, hidden),
+            low(hidden, width),
+            word(8, width),
+            word(1, hidden),
+            word(*marks.shape),
+            word(*marks.shape),
+            low(tokens, width),
         ],
         scratch_shapes=[
-            pltpu.VMEM((micro, pack, width), jnp.bfloat16),
-            pltpu.VMEM((1, pack, 3 * local), jnp.bfloat16),
-            pltpu.VMEM((micro, pack, local), jnp.bfloat16),
+            room(micro, pack, width),
+            room(1, pack, 3 * local),
+            room(micro, pack, local),
             pltpu.VMEM((3,) + marks.shape, jnp.float32),
             pltpu.VMEM((3,) + marks.shape, jnp.float32),
-        ]
-        + [pltpu.VMEM(shard.shape, jnp.bfloat16) for shard in shards[1:]]
-        + [
-            pltpu.SemaphoreType.DMA((256,)),
+            room(width, width),
+            room(width, hidden),
+            room(hidden, width),
+            room(4, *small.shape),
+            room(tokens, width),
+            room(tokens, width),
+            room(tokens, hidden),
+            pltpu.VMEM((tokens, width), jnp.float32),
+            pltpu.SemaphoreType.DMA((320,)),
         ],
         compiler_params=pltpu.CompilerParams(
-            collective_id=2, has_side_effects=True, vmem_limit_bytes=48 * 2**20
+            collective_id=2, has_side_effects=True, vmem_limit_bytes=60 * 2**20
         ),
         name="first_pass",
     )(block, *shards, small, marks, bias, ids[:, None, :], ids[:, :, None])
-
-
-def second_kernel(size, *refs):
-    states, leaving, weight, bias, ids_row, ids_col = refs[:6]
-    full, qkv, mixed_rows, mixed, sems = refs[6:]
-    micro, rows, width = states.shape
-    wires = Wires(sems)
-    section = lax.axis_index("section")
-    spread = Spread(wires, full, mixed, mixed_rows, rows, weight.shape[1] // 3)
-    w, sibling, across, across_sibling = wt_places()
-    greet(
-        [{"wt": partner} for partner in (across, across_sibling, sibling)]
-        + [{"section": 1 - section}],
-        [],
-    )
-
-    def relay_copy(m):
-        return wires.remote(("relay", m), leaving.at[m], spread.stripe(m, w), section=1 - section)
-
-    def stay(m):
-        return wires.local(("stay", m), states.at[m], spread.stripe(m, w))
-
-    @pl.when(section == 0)
-    def _():
-        for m in range(micro):
-            relay_copy(m).start()
-            stay(m).start()
-
-    def arrive(m):
-        @pl.when(section == 0)
-        def _():
-            stay(m).wait()
-
-        @pl.when(section == 1)
-        def _():
-            relay_copy(m).wait_recv()
-
-        spread.send(m)
-
-    def work(m):
-        spread.settle(m)
-        project(full.at[m], weight, bias, qkv.at[m])
-        attend_pack(size, ids_col[m] == ids_row[m], qkv.at[m], mixed.at[m])
-        spread.send_back(m)
-
-    arrive(0)
-    arrive(1)
-    spread.hand_on(0)
-    work(0)
-    arrive(2)
-    spread.hand_on(1)
-    work(1)
-    spread.hand_on(2)
-    work(2)
-    for m in range(micro):
-        spread.finish(m)
-
-    @pl.when(section == 0)
-    def _():
-        for m in range(micro):
-            relay_copy(m).wait_send()
-
-
-def second_pass(states, leaving, weight, bias, ids, size):
-    micro, rows, width = states.shape
-    local = weight.shape[1] // 3
-    pack = ids.shape[1]
-    anywhere = pl.BlockSpec(memory_space=pl.ANY)
-    inside = pl.BlockSpec(memory_space=pltpu.VMEM)
-    low = lambda *shape: jax.ShapeDtypeStruct(shape, jnp.bfloat16)
-    return pl.pallas_call(
-        functools.partial(second_kernel, size),
-        in_specs=[anywhere] * 2 + [inside] * 4,
-        out_specs=[inside] * 3,
-        out_shape=[
-            low(micro, pack, width),
-            low(micro, pack, 3 * local),
-            low(micro * rows, width),
-        ],
-        scratch_shapes=[
-            pltpu.VMEM((micro, pack, local), jnp.bfloat16),
-            pltpu.SemaphoreType.DMA((80,)),
-        ],
-        compiler_params=pltpu.CompilerParams(
-            collective_id=3, has_side_effects=True, vmem_limit_bytes=48 * 2**20
-        ),
-        name="second_pass",
-    )(states, leaving, weight, bias, ids[:, None, :], ids[:, :, None])
 
 
 class Back:
@@ -1068,15 +1105,100 @@
     return wires.local(("home", m), block, target.at[m])
 
 
-def back_kernel(size, *refs):
-    returned, grad_states, projected = refs[6:9]
+def mid_kernel(size, *refs):
+    states, leaving, weight_out, weight_in, weight_down = refs[:5]
+    weight, bias, ids_row, ids_col, layer_rows, in_bias, covered = refs[5:12]
+    outs = refs[12:22]
+    inverse_one, inverse_two, returned = refs[22:25]
+    held = refs[25:28]
+    full, qkv, mixed_rows, mixed = refs[28:32]
+    saved = dict(zip(SAVED, refs[32:39]))
+    skip, rows_grad, projected, grad_states = refs[39:43]
+    micro, rows, width = states.shape
     wires = Wires(refs[-1])
     section = lax.axis_index("section")
-    qkv = lambda m: refs[2].at[m]
-    given = (refs[0], refs[1], qkv, refs[3], refs[4:6])
-    back = Back(wires, size, given + (projected, grad_states) + refs[9:-1])
-    greet([{"wt": partner} for partner in back.partners] + [{"section": 1 - section}], [])
-    back.begin(0)
+    spread = Spread(wires, full, mixed, mixed_rows, rows, weight.shape[1] // 3)
+    given = (rows_grad, skip, lambda m: qkv.at[m], weight, (ids_row, ids_col))
+    back = Back(wires, size, given + (projected, grad_states) + refs[43:-1])
+    w = spread.w
+    kept = dict(saved, inverse_one=inverse_one, inverse_two=inverse_two)
+
+    def stay(m):
+        return wires.local(("stay", m), states.at[m], spread.stripe(m, w))
+
+    def teacher_copy(m):
+        return wires.local(("teacher", m), states.at[m], grad_states.at[pl.ds(m * rows, rows), :])
+
+    def weight_copies():
+        for index, source in enumerate((weight_out, weight_in, weight_down)):
+            yield wires.local(("weight", index), source, held[index])
+
+    def own_loads():
+        @pl.when(section == 0)
+        def _():
+            for m in range(micro):
+                stay(m).start()
+
+        for copy in weight_copies():
+            copy.start()
+        for m in range(micro):
+            teacher_copy(m).start()
+
+    greet(
+        [{"wt": partner} for partner in back.partners] + [{"section": 1 - section}],
+        [],
+        own_loads,
+    )
+
+    def relay_copy(m):
+        return wires.remote(("relay", m), leaving.at[m], spread.stripe(m, w), section=1 - section)
+
+    @pl.when(section == 0)
+    def _():
+        for m in range(micro):
+            relay_copy(m).start()
+
+    def arrive(m):
+        @pl.when(section == 0)
+        def _():
+            stay(m).wait()
+
+        @pl.when(section == 1)
+        def _():
+            relay_copy(m).wait_recv()
+
+        spread.send(m)
+
+    def attend(m):
+        spread.settle(m)
+        project(full.at[m], weight, bias, qkv.at[m])
+        attend_pack(size, ids_col[m] == ids_row[m], qkv.at[m], mixed.at[m])
+        spread.send_back(m)
+        for name, source in (("full", full), ("qkv", qkv)):
+            store(name, m, source.at[m], outs[OUTS.index(name)].at[m]).start()
+
+    def store(name, m, source, target):
+        return wires.local(("store", name, m), source, target)
+
+    def stores(m):
+        at = pl.ds(m * rows, rows)
+        for name, ref in [("mixed", mixed_rows)] + list(saved.items()):
+            yield store(name, m, ref.at[at, :], outs[OUTS.index(name)].at[at, :])
+
+    def feed(m):
+        spread.arrived_back(m)
+        at = pl.ds(m * rows, rows)
+        block = spread.stripe(m, w)[...]
+        output = feed_forward(at, block, mixed_rows[at, :], held, layer_rows, in_bias, kept)
+        saved["final"][at, :] = output.astype(jnp.bfloat16)
+        teacher_copy(m).wait()
+        teacher = grad_states[at, :].astype(jnp.float32)
+        grad = covered[at, :] * (output - teacher)
+        saved["grad"][at, :] = grad
+        skip[at, :], rows_grad[at, :] = feed_backward(at, grad, held, layer_rows, kept)
+        for copy in stores(m):
+            copy.start()
+        back.begin(m)
 
     def back_copy(m):
         place = back.place(m)
@@ -1091,17 +1213,36 @@
         def _():
             back_copy(m).start()
 
-    back.work(0, 1)
+    arrive(0)
+    arrive(1)
+    spread.hand_on(0)
+    attend(0)
+    arrive(2)
+    spread.hand_on(1)
+    attend(1)
+    spread.hand_on(2)
+    for copy in weight_copies():
+        copy.wait()
+    feed(0)
+    attend(2)
+    feed(1)
+    back.work(0)
     back.cross(0)
-    back.work(1, 2)
+    feed(2)
+    back.work(1)
     back.cross(1)
     finish(0)
     back.work(2)
     back.cross(2)
     finish(1)
     finish(2)
-    for m in range(back.micro):
+    for m in range(micro):
+        spread.end(m)
         back.end(m)
+        for name, source in (("full", full), ("qkv", qkv)):
+            store(name, m, source.at[m], outs[OUTS.index(name)].at[m]).wait()
+        for copy in stores(m):
+            copy.wait()
 
         @pl.when(section == 1)
         def _():
@@ -1109,31 +1250,68 @@
 
         @pl.when(section == 0)
         def _():
+            relay_copy(m).wait_send()
             back_copy(m).wait_recv()
 
 
-def back_pass(rows_grad, skip, qkv, weight, ids, size):
-    micro, pack, local = qkv.shape
-    local = local // 3
-    tokens, width = rows_grad.shape
+SAVED = ("normal_one", "first", "hidden", "slope", "normal_two", "final", "grad")
+OUTS = ("full", "qkv", "mixed") + SAVED
+
+
+def mid_pass(states, leaving, weights, weight, bias, ids, layer_rows, in_bias, covered, size):
+    micro, rows, width = states.shape
+    local = weight.shape[1] // 3
+    pack = ids.shape[1]
+    tokens, hidden = micro * rows, weights[1].shape[1]
+    anywhere = pl.BlockSpec(memory_space=pl.ANY)
     inside = pl.BlockSpec(memory_space=pltpu.VMEM)
     low = lambda *shape: jax.ShapeDtypeStruct(shape, jnp.bfloat16)
-    return pl.pallas_call(
-        functools.partial(back_kernel, size),
-        in_specs=[inside] * 6,
-        out_specs=inside,
-        out_shape=low(tokens, width),
-        scratch_shapes=[
-            pltpu.VMEM((tokens, width), jnp.bfloat16),
-            pltpu.VMEM((micro * pack, 3 * local), jnp.bfloat16),
+    word = lambda *shape: jax.ShapeDtypeStruct(shape, jnp.float32)
+    held = [
+        word(tokens, width),
+        low(tokens, width),
+        low(tokens, hidden),
+        low(tokens, hidden),
+        word(tokens, width),
+        low(tokens, width),
+        word(tokens, width),
+    ]
+    room = lambda shape: pltpu.VMEM(shape.shape, shape.dtype)
+    kept = [low(micro, pack, width), low(micro, pack, 3 * local), low(tokens, width)]
+    *results, inverse_one, inverse_two, returned = pl.pallas_call(
+        functools.partial(mid_kernel, size),
+        in_specs=[anywhere] * 5 + [inside] * 7,
+        out_specs=[anywhere] * 10 + [inside] * 3,
+        out_shape=kept + held + [word(tokens, 1), word(tokens, 1), low(tokens, width)],
+        scratch_shapes=[pltpu.VMEM(part.shape, jnp.bfloat16) for part in weights]
+        + [room(shape) for shape in kept]
+        + [room(low(micro, pack, local))]
+        + [room(shape) for shape in held]
+        + [
+            room(word(tokens, width)),
+            room(low(tokens, width)),
+            room(low(micro * pack, 3 * local)),
+            room(low(tokens, width)),
         ]
         + back_scratch(micro, pack, local, width)
-        + [pltpu.SemaphoreType.DMA((96,))],
+        + [pltpu.SemaphoreType.DMA((200,))],
         compiler_params=pltpu.CompilerParams(
-            collective_id=4, has_side_effects=True, vmem_limit_bytes=48 * 2**20
+            collective_id=4, has_side_effects=True, vmem_limit_bytes=62 * 2**20
         ),
-        name="back_pass",
-    )(rows_grad, skip, qkv, weight, ids[:, None, :], ids[:, :, None])
+        name="mid_pass",
+    )(
+        states,
+        leaving,
+        *weights,
+        weight,
+        bias,
+        ids[:, None, :],
+        ids[:, :, None],
+        layer_rows,
+        in_bias,
+        covered,
+    )
+    return dict(zip(OUTS, results)), inverse_one, inverse_two, returned
 
 
 CHUNK = 128
@@ -1731,66 +1909,36 @@
     small = jnp.pad(small, ((0, 16 - small.shape[0]), (0, 0)))
     marks = jnp.pad(valid.astype(jnp.float32), ((0, 8 - micro), (0, 0)))
     shards = (w_qkv[0], w_out[0], w_in[0], w_down[0])
-    own, weight_qkv, weight_out, weight_in, weight_down, smalls, marks, counts, mixed = first_pass(
+    own, weight_qkv, *weights, layer_rows, in_bias, marks, counts, leaving = first_pass(
         boundary[0], shards, small, marks, qkv_bias, ids, size
     )
-    vector_rows = smalls[:, :8].transpose(1, 0, 2).reshape(8, width).astype(jnp.float32)
-    in_bias = smalls[:, 8 : 8 + w_in.shape[2] // width].reshape(-1).astype(jnp.float32)
-    marks = marks[:micro].reshape(tokens, 1)
     factor = LOSS_SCALE / jnp.sum(counts)
-    flat = own.reshape(tokens, width)
-
-    def forward(states, mixed):
-        summed = states.astype(jnp.float32) + (dot(mixed, weight_out) + vector_rows[2])
-        normal_one, inverse_one = norm_parts(summed)
-        first = normal_one * vector_rows[3] + vector_rows[4]
-        first_low = first.astype(jnp.bfloat16)
-        hidden, slope = gelu_both(dot(first_low, weight_in) + in_bias)
-        hidden = lax.optimization_barrier(hidden.astype(jnp.bfloat16))
-        second = first + (dot(hidden, weight_down) + vector_rows[5])
-        normal_two, inverse_two = norm_parts(second)
-        output = normal_two * vector_rows[6] + vector_rows[7]
-        slope = slope.astype(jnp.bfloat16)
-        return (
-            output,
-            (normal_one, inverse_one, first_low, hidden, slope, normal_two, inverse_two),
-        )
-
-    def backward(grad, kept):
-        normal_one, inverse_one, first_low, hidden, slope, normal_two, inverse_two = kept
-        grad_second = norm_back(grad, vector_rows[6], normal_two, inverse_two)
-        down_low = grad_second.astype(jnp.bfloat16)
-        pre_low = (dot(down_low, weight_down, ((1,), (1,))) * slope).astype(jnp.bfloat16)
-        pre_low = lax.optimization_barrier(pre_low)
-        grad_first = grad_second + dot(pre_low, weight_in, ((1,), (1,)))
-        grad_summed = norm_back(grad_first, vector_rows[3], normal_one, inverse_one)
-        branch_low = grad_summed.astype(jnp.bfloat16)
-        mixed_grad = dot(branch_low, weight_out, ((1,), (1,))).astype(jnp.bfloat16)
-        return (mixed_grad, grad_summed, (down_low, pre_low, grad_first, branch_low))
-
-    output, _ = forward(flat, mixed)
-    leaving = output.astype(jnp.bfloat16).reshape(micro, rows, width)
-    full, qkv, mixed = second_pass(own, leaving, weight_qkv, qkv_bias, ids, size)
-    states = lax.dynamic_slice_in_dim(full, wt_at * rows, rows, 1).reshape(tokens, width)
-    output, kept = forward(states, mixed)
-    cotangent = factor * marks * (output - flat.astype(jnp.float32))
-    mixed_grad, skip, _ = backward(cotangent, kept)
-    returned = back_pass(mixed_grad, skip, qkv, weight_qkv, ids, size)
-    cotangent = jnp.where(section_at == 1, cotangent, returned.astype(jnp.float32))
-    normal_one, inverse_one, first_low, hidden, slope, normal_two, inverse_two = kept
-    grad_second = norm_back(cotangent, vector_rows[6], normal_two, inverse_two)
+    covered = factor * marks[:micro].reshape(tokens, 1)
+    leaving = leaving.reshape(micro, rows, width)
+    kept, inverse_one, inverse_two, returned = mid_pass(
+        own, leaving, weights, weight_qkv, qkv_bias, ids, layer_rows, in_bias, covered, size
+    )
+    cotangent = jnp.where(section_at == 1, kept["grad"], returned.astype(jnp.float32))
+    normal_two = kept["normal_two"]
+    grad_second = norm_back(cotangent, layer_rows[6], normal_two, inverse_two)
     down_low = grad_second.astype(jnp.bfloat16)
     total = lambda values: jnp.sum(values.astype(jnp.float32), axis=0)
     rows_low = jnp.stack([total(down_low), total(cotangent * normal_two), total(cotangent)])
     home, *sums = last_pass(
         weight_qkv,
         ids,
-        vector_rows[3:4],
+        layer_rows[3:4],
         inverse_one,
         jnp.pad(rows_low, ((5, 0), (0, 0))),
-        (grad_second, normal_one, qkv, full.reshape(-1, width), slope),
-        (weight_out, weight_in, weight_down),
-        (hidden, first_low, mixed, down_low, output.astype(jnp.bfloat16)),
+        (
+            grad_second,
+            kept["normal_one"],
+            kept["qkv"],
+            kept["full"].reshape(-1, width),
+            kept["slope"],
+        ),
+        weights,
+        (kept["hidden"], kept["first"], kept["mixed"], down_low, kept["final"]),
         size,
     )
     sums = [part.astype(jnp.float32)[None] for part in sums]

time: 523 us -> 500 us (0.956)
  matrix products: 49.7 us -> 0 us
  Pallas kernels: 428 us -> 462 us
    dot_general x9 -> x0, matrix products: 49.7 us -> none  [dot(): lax.dot_general(left, right, (dims, ((), ())), preferred_element_type=jnp...]
    pallas_call x2 -> x1, Pallas kernels: 97.5 us -> 119 us  [mid_pass(): pl.pallas_call(functools.partial(mid_kernel, size), in_specs=[anywhere] *...]
    pallas_call x1, Pallas kernels: 117 us -> 128 us  [first_pass(): pl.pallas_call(functools.partial(first_kernel, size), in_specs=[anywhere]...]
where the time goes in v6:
time: 500 us; the launch traced here: 493 us
  Pallas kernels  462 us (92%)
  other arithmetic  21.7 us (4%)
  local copies, waits for them, and re-layouts  8.11 us (2%)
    pallas_call x1, Pallas kernels, last_pass(): pl.pallas_call(functools.partial(last_kernel, chunks, size), in_specs=[in...  214 us
    pallas_call x1, Pallas kernels, first_pass(): pl.pallas_call(functools.partial(first_kernel, size), in_specs=[anywhere]...  128 us
    pallas_call x1, Pallas kernels, mid_pass(): pl.pallas_call(functools.partial(mid_kernel, size), in_specs=[anywhere] *...  119 us
    broadcast_in_dim x5, other arithmetic, relay(): sums = [part.astype(jnp.float32)[None] for part in sums]  10 us

profile of v6, /device:TPU:4, one launch (start us, length us, event | category | flops | bytes accessed | tf_op | source)
XLA Modules:
  0.0 493.0 jit_solution(9876757571354568743)
XLA Ops:
  0.7 0.1 add_bitcast_fusion
  0.8 0.6 copy-done
  1.3 0.2 reduce_window_sum.14
  1.5 0.7 convert_element_type.29
  2.2 0.6 pad.13.refs_6_
  2.8 0.7 reduce
  3.5 0.1 convert_reduce_fusion.1
  3.6 0.6 broadcast_in_dim.56.refs_8_.refs_7_.refs_1_
  4.2 1.3 fusion.2.refs_5_
  5.5 0.7 bitcast_convert_fusion.5
  6.2 0.6 broadcast_in_dim.55.refs_7_.refs_6_
  6.8 1.2 copy.23.refs_9_.refs_8_.refs_2_
  8.0 128.5 %first_pass.1 = (bf16[3,128,1024]{2,1,0:T(8,128)(2,1)}, bf16[1024,768]{1,0:T(8,128)(2,1)}, bf16[1024,1024]{1,0:T(8,128)(2,1)}, bf16[1024,4096]{1,0:T(8,128)(2,1)...) custom-call(bf16[3,128,1024]{2,1,0:T(8,128)(2,1)} %bitcast.54, ...), custom_call_target="tpu_custom_call" | custom-call | tf_op jit(solution)/shard_map/first_pass/pallas_call | solution.py:955
  136.5 1.3 reduce_sum.64
  138.4 0.7 multiply_bitcast_fusion
  139.1 1.4 fusion.6
  140.6 0.8 copy.29
  141.4 118.7 %mid_pass.1 = (bf16[3,512,1024]{2,1,0:T(8,128)(2,1)}, bf16[3,512,768]{2,1,0:T(8,128)(2,1)}, bf16[384,1024]{1,0:T(8,128)(2,1)}, f32[384,1024]{1,0:T(8,128)}, bf16...) custom-call(bf16[3,128,1024]{2,1,0:T(8,128)(2,1)} %get-tuple-element, ...), custom_call_target="tpu_custom_call" | custom-call | tf_op jit(solution)/shard_map/mid_pass/pallas_call | solution.py:1281
  260.1 1.1 reduce.1
  261.2 2.4 multiply_reduce_fusion.1
  263.7 1.8 convert_reduce_fusion
  265.5 0.6 select_maximum_fusion.refs_5_
  266.1 214.4 %last_pass.1 = (bf16[3,128,1024]{2,1,0:T(8,128)(2,1)}, bf16[256,3072]{1,0:T(8,128)(2,1)}, bf16[256,1024]{1,0:T(8,128)(2,1)}, bf16[256,4096]{1,0:T(8,128)(2,1)}, ...) custom-call(bf16[1024,768]{1,0:T(8,128)(2,1)} %get-tuple-element.36.refs_5_.refs_0_, ...), custom_call_target="tpu_custom_call" | custom-call | tf_op jit(solution)/shard_map/last_pass/pallas_call | solution.py:1836
  480.6 0.9 bitcast_convert_fusion.4
  481.4 0.6 slice.31
  482.0 0.6 copy.30
  482.6 2.1 bitcast_convert_fusion.3
  484.8 2.0 bitcast_convert_fusion.2
  486.8 0.2 copy-done.4
  487.0 2.5 bitcast_convert_fusion.1
  489.5 2.5 bitcast_convert_fusion
  492.0 0.9 copy.36
  (23 shorter events, 0.1 us)
Async XLA Ops:
  0.6 0.7 copy-start
  261.2 2.5 copy-start.2
  480.5 4.2 copy-start.5
  484.8 2.2 copy-start.4
  487.0 2.5 copy-start.3
  489.5 2.5 copy-start.6
  489.5 3.4 copy-start.1

commit v7 on v6

--- a/solution.py
+++ b/solution.py
@@ -498,6 +498,22 @@
     pl.semaphore_wait(barrier, waits)
 
 
+def same_document(lengths, m, rows):
+    z = lax.axis_index("ctx")
+    pack = turned(z)
+    ends = [lengths[m, pack, 0]]
+    for document in range(1, lengths.shape[2]):
+        ends.append(ends[-1] + lengths[m, pack, document])
+
+    def ids(axis):
+        shape = (rows, 1) if axis == 0 else (1, rows)
+        first = lax.broadcasted_iota(jnp.int32, shape, axis) * 4
+        place = jnp.concatenate([first + stripe_of(z, j) for j in range(4)], axis=axis)
+        return sum((place >= end).astype(jnp.int32) for end in ends)
+
+    return ids(0) == ids(1)
+
+
 def attend_pack(size, same, qkv, mixed):
     local = mixed.shape[1]
     masks = head_lanes(size)
@@ -613,7 +629,11 @@
 
 
 def project(full, weight, bias, qkv):
-    qkv[...] = (dot(full[...], weight[...]) + bias[...]).astype(jnp.bfloat16)
+    qkv[...] = (dot(full[...], weight[...]) + bias).astype(jnp.bfloat16)
+
+
+def bias_of(rows):
+    return jnp.concatenate([rows[0:1], jnp.zeros_like(rows[0:1]), rows[1:2]], axis=1)
 
 
 BLOCK = 512
@@ -661,11 +681,12 @@
 
 
 def first_kernel(size, *refs):
-    block, shard_qkv, shard_out, shard_in, shard_down, small, marks, bias = refs[:8]
-    ids_row, ids_col = refs[8:10]
-    own, weight, kept_out, kept_in, kept_down, layer_rows, in_bias, own_marks, count = refs[10:19]
-    leaving, full, qkv, mixed, marks_wt, marks_ctx = refs[19:25]
-    whole_out, whole_in, whole_down, smalls, mixed_rows, first, inner, total, sems = refs[25:]
+    block, shard_qkv, shard_out, shard_in, shard_down, vectors, own_bias, valid = refs[:8]
+    lengths = refs[8]
+    own, weight, kept_out, kept_in, kept_down, layer_rows, in_bias, own_marks, count = refs[9:18]
+    leaving, full, qkv, mixed, marks_wt, marks_ctx = refs[18:24]
+    whole_out, whole_in, whole_down, smalls, mixed_rows, first, inner, total = refs[24:32]
+    small, marks, sems = refs[32:]
     micro, rows, width = block.shape
     local = small.shape[1]
     hidden = shard_in.shape[1]
@@ -680,10 +701,22 @@
     neighbor = z + 1 - 2 * level
     moves, place = is_moving(z, w), plane_place(z, w)
     others = [lax.rem(z + step, 4) for step in (1, 2, 3)]
+
+    def own_parts():
+        small[...] = jnp.zeros_like(small)
+        small[:8, :] = vectors[...].astype(jnp.float32)
+        for row in range(own_bias.shape[1] // local):
+            at = pl.ds(row * local, local)
+            small[8 + row : 9 + row, :] = own_bias[:, at].astype(jnp.float32)
+        marks[...] = jnp.zeros_like(marks)
+        marks[: valid.shape[0], :] = valid[...].astype(jnp.float32)
+
     greet(
         [{"wt": partner} for partner in partners] + [{"ctx": other} for other in others],
         [(moves, place), (moves, home_place(z, w))],
+        own_parts,
     )
+    bias = bias_of(small)
 
     def swap(m):
         return wires.remote(
@@ -890,15 +923,15 @@
         small_copy(index).wait_recv()
     for j in range(4):
         at = pl.ds(j * local, local)
-        layer_rows[:, at] = smalls[j, :8, :].astype(jnp.float32)
+        layer_rows[:, at] = smalls[j, :8, :]
         for row in range(columns):
             at = pl.ds(j * 8 * deep + row * local, local)
-            in_bias[:, at] = smalls[j, 8 + row : 9 + row, :].astype(jnp.float32)
+            in_bias[:, at] = smalls[j, 8 + row : 9 + row, :]
     for m in range(micro):
         spread.hand_on(m)
         spread.settle(m)
         project(full.at[m], weight, bias, qkv.at[0])
-        attend_pack(size, ids_col[m] == ids_row[m], qkv.at[0], mixed.at[m])
+        attend_pack(size, same_document(lengths, m, rows), qkv.at[0], mixed.at[m])
         spread.send_back(m)
         passing(m)
     passed(0)
@@ -942,10 +975,11 @@
         swap_marks().wait()
 
 
-def first_pass(block, shards, small, marks, bias, ids, size):
+def first_pass(block, shards, vectors, bias, valid, lengths, size):
     micro, rows, width = block.shape
-    local = small.shape[1]
-    pack = ids.shape[1]
+    local = vectors.shape[1]
+    pack = 4 * rows
+    marks = (8, rows)
     tokens, hidden = micro * rows, shards[2].shape[1]
     anywhere = pl.BlockSpec(memory_space=pl.ANY)
     inside = pl.BlockSpec(memory_space=pltpu.VMEM)
@@ -954,7 +988,7 @@
     room = lambda *shape: pltpu.VMEM(shape, jnp.bfloat16)
     return pl.pallas_call(
         functools.partial(first_kernel, size),
-        in_specs=[anywhere] * 5 + [inside] * 5,
+        in_specs=[anywhere] * 5 + [inside] * 3 + [pl.BlockSpec(memory_space=pltpu.SMEM)],
         out_specs=[anywhere, inside] + [anywhere] * 3 + [inside] * 5,
         out_shape=[
             low(micro, rows, width),
@@ -964,37 +998,39 @@
             low(hidden, width),
             word(8, width),
             word(1, hidden),
-            word(*marks.shape),
-            word(*marks.shape),
+            word(*marks),
+            word(*marks),
             low(tokens, width),
         ],
         scratch_shapes=[
             room(micro, pack, width),
             room(1, pack, 3 * local),
             room(micro, pack, local),
-            pltpu.VMEM((3,) + marks.shape, jnp.float32),
-            pltpu.VMEM((3,) + marks.shape, jnp.float32),
+            pltpu.VMEM((3,) + marks, jnp.float32),
+            pltpu.VMEM((3,) + marks, jnp.float32),
             room(width, width),
             room(width, hidden),
             room(hidden, width),
-            room(4, *small.shape),
+            pltpu.VMEM((4, 16, local), jnp.float32),
             room(tokens, width),
             room(tokens, width),
             room(tokens, hidden),
             pltpu.VMEM((tokens, width), jnp.float32),
+            pltpu.VMEM((16, local), jnp.float32),
+            pltpu.VMEM(marks, jnp.float32),
             pltpu.SemaphoreType.DMA((320,)),
         ],
         compiler_params=pltpu.CompilerParams(
             collective_id=2, has_side_effects=True, vmem_limit_bytes=60 * 2**20
         ),
         name="first_pass",
-    )(block, *shards, small, marks, bias, ids[:, None, :], ids[:, :, None])
+    )(block, *shards, vectors, bias, valid, lengths)
 
 
 class Back:
     def __init__(self, wires, size, refs):
         self.wires, self.size = wires, size
-        self.rows_grad, self.skip, self.qkv, self.weight, self.ids = refs[:5]
+        self.rows_grad, self.skip, self.qkv, self.weight, self.lengths = refs[:5]
         self.projected, self.grad_states = refs[5:7]
         self.heads_grad, self.part, self.from_sibling, self.far, self.from_across = refs[7:]
         self.micro, self.pack, self.local = self.heads_grad.shape
@@ -1052,10 +1088,9 @@
         self.arrive(m)
         if following is not None:
             self.begin(following)
-        ids_row, ids_col = self.ids
         whole = pl.ds(m * self.pack, self.pack)
         projected = self.projected.at[whole, :]
-        same = ids_col[m] == ids_row[m]
+        same = same_document(self.lengths, m, self.rows)
         qkv = self.qkv(m)
         attend_pack_back(self.size, same, qkv, self.heads_grad.at[m], projected)
         product = dot(projected[...], self.weight[...], ((1,), (1,)))
@@ -1107,20 +1142,21 @@
 
 def mid_kernel(size, *refs):
     states, leaving, weight_out, weight_in, weight_down = refs[:5]
-    weight, bias, ids_row, ids_col, layer_rows, in_bias, covered = refs[5:12]
-    outs = refs[12:22]
-    inverse_one, inverse_two, returned = refs[22:25]
-    held = refs[25:28]
-    full, qkv, mixed_rows, mixed = refs[28:32]
-    saved = dict(zip(SAVED, refs[32:39]))
-    skip, rows_grad, projected, grad_states = refs[39:43]
+    weight, layer_rows, in_bias, marks, count, lengths = refs[5:11]
+    outs = refs[11:21]
+    inverse_one, inverse_two, returned = refs[21:24]
+    held = refs[24:27]
+    full, qkv, mixed_rows, mixed = refs[27:31]
+    saved = dict(zip(SAVED, refs[31:38]))
+    skip, rows_grad, projected, grad_states = refs[38:42]
     micro, rows, width = states.shape
     wires = Wires(refs[-1])
     section = lax.axis_index("section")
     spread = Spread(wires, full, mixed, mixed_rows, rows, weight.shape[1] // 3)
-    given = (rows_grad, skip, lambda m: qkv.at[m], weight, (ids_row, ids_col))
-    back = Back(wires, size, given + (projected, grad_states) + refs[43:-1])
+    given = (rows_grad, skip, lambda m: qkv.at[m], weight, lengths)
+    back = Back(wires, size, given + (projected, grad_states) + refs[42:-1])
     w = spread.w
+    bias = bias_of(layer_rows[:2, pl.ds(w * spread.local, spread.local)])
     kept = dict(saved, inverse_one=inverse_one, inverse_two=inverse_two)
 
     def stay(m):
@@ -1131,7 +1167,14 @@
 
     def weight_copies():
         for index, source in enumerate((weight_out, weight_in, weight_down)):
-            yield wires.local(("weight", index), source, held[index])
+            step = source.shape[0] if index == 0 else source.shape[0] // 4
+            for row in range(0, source.shape[0], step):
+                at = pl.ds(row, step)
+                yield wires.local(("weight", index, row), source.at[at, :], held[index].at[at, :])
+
+    def load_weights(first, last):
+        for copy in list(weight_copies())[first:last]:
+            copy.start()
 
     def own_loads():
         @pl.when(section == 0)
@@ -1139,10 +1182,7 @@
             for m in range(micro):
                 stay(m).start()
 
-        for copy in weight_copies():
-            copy.start()
-        for m in range(micro):
-            teacher_copy(m).start()
+        load_weights(0, 3)
 
     greet(
         [{"wt": partner} for partner in back.partners] + [{"section": 1 - section}],
@@ -1172,7 +1212,7 @@
     def attend(m):
         spread.settle(m)
         project(full.at[m], weight, bias, qkv.at[m])
-        attend_pack(size, ids_col[m] == ids_row[m], qkv.at[m], mixed.at[m])
+        attend_pack(size, same_document(lengths, m, rows), qkv.at[m], mixed.at[m])
         spread.send_back(m)
         for name, source in (("full", full), ("qkv", qkv)):
             store(name, m, source.at[m], outs[OUTS.index(name)].at[m]).start()
@@ -1185,20 +1225,29 @@
         for name, ref in [("mixed", mixed_rows)] + list(saved.items()):
             yield store(name, m, ref.at[at, :], outs[OUTS.index(name)].at[at, :])
 
-    def feed(m):
-        spread.arrived_back(m)
-        at = pl.ds(m * rows, rows)
-        block = spread.stripe(m, w)[...]
+    def covered(m):
+        total = jnp.sum(jnp.sum(count[...], axis=0, keepdims=True), axis=1, keepdims=True)
+        shape = (rows, rows)
+        here = lax.broadcasted_iota(jnp.int32, shape, 0) == lax.broadcasted_iota(jnp.int32, shape, 1)
+        column = jnp.sum(jnp.where(here, marks[m : m + 1, :], 0.0), axis=1, keepdims=True)
+        return LOSS_SCALE / total * column
+
+    def feed(*packs):
+        for m in packs:
+            spread.arrived_back(m)
+            teacher_copy(m).wait()
+        at = pl.ds(packs[0] * rows, len(packs) * rows)
+        block = jnp.concatenate([spread.stripe(m, w)[...] for m in packs], axis=0)
         output = feed_forward(at, block, mixed_rows[at, :], held, layer_rows, in_bias, kept)
         saved["final"][at, :] = output.astype(jnp.bfloat16)
-        teacher_copy(m).wait()
-        teacher = grad_states[at, :].astype(jnp.float32)
-        grad = covered[at, :] * (output - teacher)
+        factor = jnp.concatenate([covered(m) for m in packs], axis=0)
+        grad = factor * (output - grad_states[at, :].astype(jnp.float32))
         saved["grad"][at, :] = grad
         skip[at, :], rows_grad[at, :] = feed_backward(at, grad, held, layer_rows, kept)
-        for copy in stores(m):
-            copy.start()
-        back.begin(m)
+        for m in packs:
+            for copy in stores(m):
+                copy.start()
+            back.begin(m)
 
     def back_copy(m):
         place = back.place(m)
@@ -1214,21 +1263,26 @@
             back_copy(m).start()
 
     arrive(0)
+    load_weights(3, 5)
     arrive(1)
+    load_weights(5, 6)
     spread.hand_on(0)
     attend(0)
     arrive(2)
+    load_weights(6, 8)
     spread.hand_on(1)
     attend(1)
+    load_weights(8, 9)
+    for m in range(micro):
+        teacher_copy(m).start()
     spread.hand_on(2)
     for copy in weight_copies():
         copy.wait()
     feed(0)
     attend(2)
-    feed(1)
+    feed(1, 2)
     back.work(0)
     back.cross(0)
-    feed(2)
     back.work(1)
     back.cross(1)
     finish(0)
@@ -1258,10 +1312,10 @@
 OUTS = ("full", "qkv", "mixed") + SAVED
 
 
-def mid_pass(states, leaving, weights, weight, bias, ids, layer_rows, in_bias, covered, size):
+def mid_pass(states, leaving, weights, weight, layer_rows, in_bias, marks, count, lengths, size):
     micro, rows, width = states.shape
     local = weight.shape[1] // 3
-    pack = ids.shape[1]
+    pack = 4 * rows
     tokens, hidden = micro * rows, weights[1].shape[1]
     anywhere = pl.BlockSpec(memory_space=pl.ANY)
     inside = pl.BlockSpec(memory_space=pltpu.VMEM)
@@ -1280,7 +1334,7 @@
     kept = [low(micro, pack, width), low(micro, pack, 3 * local), low(tokens, width)]
     *results, inverse_one, inverse_two, returned = pl.pallas_call(
         functools.partial(mid_kernel, size),
-        in_specs=[anywhere] * 5 + [inside] * 7,
+        in_specs=[anywhere] * 5 + [inside] * 5 + [pl.BlockSpec(memory_space=pltpu.SMEM)],
         out_specs=[anywhere] * 10 + [inside] * 3,
         out_shape=kept + held + [word(tokens, 1), word(tokens, 1), low(tokens, width)],
         scratch_shapes=[pltpu.VMEM(part.shape, jnp.bfloat16) for part in weights]
@@ -1304,12 +1358,11 @@
         leaving,
         *weights,
         weight,
-        bias,
-        ids[:, None, :],
-        ids[:, :, None],
         layer_rows,
         in_bias,
-        covered,
+        marks,
+        count,
+        lengths,
     )
     return dict(zip(OUTS, results)), inverse_one, inverse_two, returned
 
@@ -1357,10 +1410,10 @@
 
 
 def last_kernel(chunks, size, *refs):
-    weight, ids_row, ids_col, gain, inverse_one, rows_low = refs[:6]
-    grad_second, normal_one, qkv_all, full_all, slope = refs[6:11]
-    weight_out, weight_in, weight_down = refs[11:14]
-    hidden, first, mixed, down, final = refs[14:19]
+    weight, layer_rows, inverse_one, inverse_two, lengths = refs[:5]
+    grad, returned, normal_two, normal_one, qkv_all, full_all, slope = refs[5:12]
+    weight_out, weight_in, weight_down = refs[12:15]
+    hidden, first, mixed, final = refs[15:19]
     home = refs[19]
     results = dict(zip(("qkv", "out", "in", "down", "rest"), refs[20:25]))
     grad_states, projected, full, product = refs[25:29]
@@ -1369,7 +1422,7 @@
     skip, normal, slopes, qkv_one, rows_grad, rest = refs[41:47]
     wires = Wires(refs[-1])
     z, section = lax.axis_index("ctx"), lax.axis_index("section")
-    tokens, width = down.shape
+    tokens, width = final.shape
     count = len(chunks)
     micro = qkv_all.shape[0]
 
@@ -1380,7 +1433,7 @@
         qkv_copy(m).wait()
         return qkv_one
 
-    given = (rows_grad, skip, qkv_of, weight, (ids_row, ids_col))
+    given = (rows_grad, skip, qkv_of, weight, lengths)
     back = Back(wires, size, given + (projected, grad_states) + refs[47:-1])
     w, sibling, across, across_sibling = wt_places()
     partners = (sibling, across, across_sibling)
@@ -1408,17 +1461,21 @@
         for copy in tile_copies(b):
             copy.start()
 
-    def skip_copy():
-        return wires.local("skip", grad_second, skip)
+    def first_copies():
+        return [
+            wires.local("grad", grad, skip),
+            wires.local("returned", returned, rows_grad),
+            wires.local("normal two", normal_two, normal),
+        ]
 
     def normal_copy():
         return wires.local("normal", normal_one, normal)
 
     def own_loads():
+        for copy in first_copies():
+            copy.start()
         start_tiles(0)
         start_tiles(1)
-        skip_copy().start()
-        normal_copy().start()
         qkv_copy(0).start()
 
     greet(
@@ -1432,9 +1489,31 @@
         own_loads,
     )
 
+    def step_first():
+        for copy in first_copies():
+            copy.wait()
+
+        @pl.when(section == 0)
+        def _():
+            skip[...] = rows_grad[...].astype(jnp.float32)
+
+        values = skip[...]
+        rest_rows[6] = jnp.sum(values * normal[...], axis=0, keepdims=True)
+        rest_rows[7] = jnp.sum(values, axis=0, keepdims=True)
+        values = norm_back(values, layer_rows[6:7, :], normal[...], inverse_two[...])
+        skip[...] = values
+        low = values.astype(jnp.bfloat16)
+        down_both[own_rows, :] = low
+        to_sibling("down", down_both, 0).start()
+        rest_rows[5] = dot(jnp.ones((16, tokens), jnp.bfloat16), low)[:1]
+        for r, row in rest_rows.items():
+            for j in range(4):
+                rest[j * 16 + r : j * 16 + r + 1, :local] = row[:, j * local : (j + 1) * local]
+        normal_copy().start()
+
+    rest_rows = {}
+
     def step_back(b):
-        if b == 0:
-            skip_copy().wait()
         for copy in tile_copies(b):
             copy.wait()
         columns = pl.ds(b * TILE, TILE)
@@ -1457,17 +1536,16 @@
         normal_copy().wait()
         ones = jnp.ones((16, tokens), jnp.bfloat16)
         grad_first = skip[...]
-        rows = {r: rows_low[r : r + 1, :] for r in (5, 6, 7)}
+        rows = {}
         rows[3] = jnp.sum(grad_first * normal[...], axis=0, keepdims=True)
         rows[4] = jnp.sum(grad_first, axis=0, keepdims=True)
-        grad_summed = norm_back(grad_first, gain[...], normal[...], inverse_one[...])
+        grad_summed = norm_back(grad_first, layer_rows[3:4, :], normal[...], inverse_one[...])
         skip[...] = grad_summed
         branch = grad_summed.astype(jnp.bfloat16)
         branch_both[own_rows, :] = branch
         to_sibling("branch", branch_both, 0).start()
         rows[2] = dot(ones, branch)[:1]
         sums = dot(ones, pre_both[own_rows, :])[:1]
-        rest[...] = jnp.zeros_like(rest)
         for j in range(4):
             for r, row in rows.items():
                 rest[j * 16 + r : j * 16 + r + 1, :local] = row[:, j * local : (j + 1) * local]
@@ -1523,10 +1601,6 @@
     def out_block(half):
         return sides(("out", half), mixed, lambda j: j * local + half * CHUNK, outs.at[half])
 
-    def whole(key, source, target, column):
-        at = pl.ds(column * width, width)
-        return both((key, column), source, target, at, at, at)
-
     def rest_copies():
         for side, k in enumerate((sibling, across_sibling)):
             yield wires.remote(
@@ -1535,8 +1609,7 @@
 
     halves = local // CHUNK
     columns = hidden.shape[1] // width
-    loads = [lambda: whole("down", down, down_both, 0)]
-    loads += [lambda index=index: down_block(index) for index in range(deep // CHUNK)]
+    loads = [lambda index=index: down_block(index) for index in range(deep // CHUNK)]
     loads += [lambda half=half: in_block(half) for half in range(halves)]
     loads += [lambda half=half: out_block(half) for half in range(halves)]
 
@@ -1549,7 +1622,7 @@
         copies = []
         if kind == "down":
             if index == 0:
-                copies += whole("down", down, down_both, 0)
+                to_sibling("down", down_both, 0).wait_recv()
             copies += down_block(index)
         elif kind == "in":
             if column == 0:
@@ -1768,6 +1841,8 @@
     for load in loads:
         for copy in load():
             copy.start()
+    rest[...] = jnp.zeros_like(rest)
+    step_first()
     stages = (settle, aside, finish, forward)
     begun, first_piece = 0, min(k for k in range(count) if is_piece(k))
     for tick in range(count + LAGS[-1]):
@@ -1793,6 +1868,7 @@
     for column in range(columns):
         to_sibling("pre", pre_both, column).wait_send()
     to_sibling("branch", branch_both, 0).wait_send()
+    to_sibling("down", down_both, 0).wait_send()
     for k in direct:
         if base_of(k) in bases[-RING:]:
             across_copy(k).wait_send()
@@ -1820,8 +1896,8 @@
         on(k, 1, owner)
 
 
-def last_pass(weight, ids, gain, inverse_one, rows_low, arrays, weights, operands, size):
-    micro, pack, local = arrays[2].shape
+def last_pass(weight, layer_rows, inverses, lengths, arrays, weights, operands, size):
+    micro, pack, local = arrays[4].shape
     local = local // 3
     tokens, width = operands[3].shape
     hidden = operands[0].shape[1]
@@ -1835,7 +1911,7 @@
     halves = local // CHUNK
     return pl.pallas_call(
         functools.partial(last_kernel, chunks, size),
-        in_specs=[inside] * 6 + [anywhere] * 13,
+        in_specs=[inside] * 4 + [pl.BlockSpec(memory_space=pltpu.SMEM)] + [anywhere] * 14,
         out_specs=[anywhere] * 6,
         out_shape=[
             low(micro, pack // 4, width),
@@ -1877,75 +1953,77 @@
         name="last_pass",
     )(
         weight,
-        ids[:, None, :],
-        ids[:, :, None],
-        gain,
-        inverse_one,
-        rows_low,
+        layer_rows,
+        *inverses,
+        lengths,
         *arrays,
         *weights,
         *operands,
     )
 
 
+def widen_kernel(*refs):
+    count = len(refs) // 2
+    for source, target in zip(refs[: count - 1], refs[count:]):
+        target[0] = source[...].astype(jnp.float32)
+    rest, (bias, rows) = refs[count - 1], refs[-2:]
+    local = rows.shape[2]
+    rows[0] = rest[:8, :local].astype(jnp.float32)
+    for row in range(bias.shape[1] // local):
+        part = rest[row : row + 1, local : 2 * local]
+        bias[:, row * local : (row + 1) * local] = part.astype(jnp.float32)
+
+
+def widen(sums, steps=8):
+    *sums, rest = sums
+    local = sums[1].shape[0]
+    cut = lambda part: (part.shape[0] // steps, part.shape[1])
+    word = lambda *shape: jax.ShapeDtypeStruct(shape, jnp.float32)
+    still = lambda *shape: pl.BlockSpec(shape, lambda step: (0,) * len(shape))
+    return pl.pallas_call(
+        widen_kernel,
+        grid=(steps,),
+        in_specs=[pl.BlockSpec(cut(part), lambda step: (step, 0)) for part in sums]
+        + [still(*rest.shape)],
+        out_specs=[pl.BlockSpec((1,) + cut(part), lambda step: (0, step, 0)) for part in sums]
+        + [still(1, sums[3].shape[0]), still(1, 8, local)],
+        out_shape=[word(1, *part.shape) for part in sums]
+        + [word(1, sums[3].shape[0]), word(1, 8, local)],
+        name="widen",
+    )(*sums, rest)
+
+
 def relay(boundary, lengths, valid, w_qkv, w_out, w_in, w_down, bias_in, vectors):
-    section_at = lax.axis_index("section")
-    count_ctx = lax.axis_size("ctx")
-    ctx_at = lax.axis_index("ctx")
-    wt_at = lax.axis_index("wt")
     micro, rows, width = boundary.shape[1:]
-    pack = rows * count_ctx
     size = width // HEADS
-    local = width // lax.axis_size("wt")
-    tokens = micro * rows
-    own_rows = vectors[0].astype(jnp.float32)
-    qkv_bias = jnp.concatenate([own_rows[0], jnp.zeros((local,), jnp.float32), own_rows[1]])[None]
-    my_lengths = lax.dynamic_index_in_dim(lengths, turned(ctx_at), 1, keepdims=False)
-    ends = jnp.cumsum(my_lengths, axis=1)
-    stripes = stripe_of(ctx_at, jnp.arange(count_ctx, dtype=jnp.int32))
-    places = jnp.arange(rows, dtype=jnp.int32)[None, :] * count_ctx + stripes[:, None]
-    ids = jnp.sum((places.reshape(1, pack, 1) >= ends[:, None, :]).astype(jnp.int32), axis=2)
-    small = jnp.concatenate([vectors[0], bias_in[0].reshape(-1, local)], axis=0)
-    small = jnp.pad(small, ((0, 16 - small.shape[0]), (0, 0)))
-    marks = jnp.pad(valid.astype(jnp.float32), ((0, 8 - micro), (0, 0)))
+    local = vectors.shape[2]
     shards = (w_qkv[0], w_out[0], w_in[0], w_down[0])
-    own, weight_qkv, *weights, layer_rows, in_bias, marks, counts, leaving = first_pass(
-        boundary[0], shards, small, marks, qkv_bias, ids, size
+    own, weight_qkv, *weights, layer_rows, in_bias, marks, count, leaving = first_pass(
+        boundary[0], shards, vectors[0], bias_in, valid, lengths, size
     )
-    factor = LOSS_SCALE / jnp.sum(counts)
-    covered = factor * marks[:micro].reshape(tokens, 1)
     leaving = leaving.reshape(micro, rows, width)
     kept, inverse_one, inverse_two, returned = mid_pass(
-        own, leaving, weights, weight_qkv, qkv_bias, ids, layer_rows, in_bias, covered, size
+        own, leaving, weights, weight_qkv, layer_rows, in_bias, marks, count, lengths, size
     )
-    cotangent = jnp.where(section_at == 1, kept["grad"], returned.astype(jnp.float32))
-    normal_two = kept["normal_two"]
-    grad_second = norm_back(cotangent, layer_rows[6], normal_two, inverse_two)
-    down_low = grad_second.astype(jnp.bfloat16)
-    total = lambda values: jnp.sum(values.astype(jnp.float32), axis=0)
-    rows_low = jnp.stack([total(down_low), total(cotangent * normal_two), total(cotangent)])
     home, *sums = last_pass(
         weight_qkv,
-        ids,
-        layer_rows[3:4],
-        inverse_one,
-        jnp.pad(rows_low, ((5, 0), (0, 0))),
+        layer_rows,
+        (inverse_one, inverse_two),
+        lengths,
         (
-            grad_second,
+            kept["grad"],
+            returned,
+            kept["normal_two"],
             kept["normal_one"],
             kept["qkv"],
             kept["full"].reshape(-1, width),
             kept["slope"],
         ),
         weights,
-        (kept["hidden"], kept["first"], kept["mixed"], down_low, kept["final"]),
+        (kept["hidden"], kept["first"], kept["mixed"], kept["final"]),
         size,
     )
-    sums = [part.astype(jnp.float32)[None] for part in sums]
-    rest = sums[4]
-    in_rows = w_in.shape[2] // width
-    bias_back = rest[:, :in_rows, local : 2 * local].reshape(1, -1)
-    return (home[None], *sums[:4], bias_back, rest[:, :8, :local])
+    return (home[None], *widen(sums))
 
 
 def solution(mesh):

time: 500 us -> 487 us (0.974)
  other arithmetic: 21.7 us -> 0 us
  Pallas kernels: 462 us -> 478 us
  local copies, waits for them, and re-layouts: 8.11 us -> 0.89 us
    broadcast_in_dim x5 -> x0, other arithmetic: 10 us -> none  [relay(): sums = [part.astype(jnp.float32)[None] for part in sums]]
    pallas_call x0 -> x1, Pallas kernels: none -> 8.68 us  [widen(): pl.pallas_call(widen_kernel, grid=(steps,), in_specs=[pl.BlockSpec(cut(pa...]
    pallas_call x1, Pallas kernels: 119 us -> 125 us  [mid_pass(): pl.pallas_call(functools.partial(mid_kernel, size), in_specs=[anywhere] *...]
    reduce_sum x4 -> x0, other arithmetic: 5.65 us -> none  [the longest x1 2.45 us: norm_back(): along = jnp.mean(inner * normal, axis=-1, keepdims=True)]
where the time goes in v7:
time: 487 us; the launch traced here: 480 us
  Pallas kernels  478 us (98%)
    pallas_call x1, Pallas kernels, last_pass(): pl.pallas_call(functools.partial(last_kernel, chunks, size), in_specs=[in...  216 us
    pallas_call x1, Pallas kernels, first_pass(): pl.pallas_call(functools.partial(first_kernel, size), in_specs=[anywhere]...  129 us
    pallas_call x1, Pallas kernels, mid_pass(): pl.pallas_call(functools.partial(mid_kernel, size), in_specs=[anywhere] *...  125 us

profile of v7, /device:TPU:4, one launch (start us, length us, event | category | flops | bytes accessed | tf_op | source)
XLA Modules:
  0.0 480.5 jit_solution(9898431888236414382)
XLA Ops:
  0.6 128.6 %first_pass.1 = (bf16[3,128,1024]{2,1,0:T(8,128)(2,1)}, bf16[1024,768]{1,0:T(8,128)(2,1)}, bf16[1024,1024]{1,0:T(8,128)(2,1)}, bf16[1024,4096]{1,0:T(8,128)(2,1)...) custom-call(bf16[3,128,1024]{2,1,0:T(8,128)(2,1)} %bitcast.14, ...), custom_call_target="tpu_custom_call" | custom-call | tf_op jit(solution)/shard_map/first_pass/pallas_call | solution.py:989
  129.2 125.4 %mid_pass.1 = (bf16[3,512,1024]{2,1,0:T(8,128)(2,1)}, bf16[3,512,768]{2,1,0:T(8,128)(2,1)}, bf16[384,1024]{1,0:T(8,128)(2,1)}, f32[384,1024]{1,0:T(8,128)}, bf16...) custom-call(bf16[3,128,1024]{2,1,0:T(8,128)(2,1)} %get-tuple-element, ...), custom_call_target="tpu_custom_call" | custom-call | tf_op jit(solution)/shard_map/mid_pass/pallas_call | solution.py:1335
  254.6 215.8 %last_pass.1 = (bf16[3,128,1024]{2,1,0:T(8,128)(2,1)}, bf16[256,3072]{1,0:T(8,128)(2,1)}, bf16[256,1024]{1,0:T(8,128)(2,1)}, bf16[256,4096]{1,0:T(8,128)(2,1)}, ...) custom-call(bf16[1024,768]{1,0:T(8,128)(2,1)} %get-tuple-element.42.refs_5_.refs_0_, ...), custom_call_target="tpu_custom_call" | custom-call | tf_op jit(solution)/shard_map/last_pass/pallas_call | solution.py:1912
  470.4 0.0 copy-start
  470.5 8.7 %widen.1 = (f32[1,256,3072]{2,1,0:T(8,128)}, f32[1,256,1024]{2,1,0:T(8,128)}, f32[1,256,4096]{2,1,0:T(8,128)}, f32[1,1024,1024]{2,1,0:T(8,128)}, f32[1,1024]{1,0:T(1,128)}, /*index=5*/f32[1,8,256]{2,1,0:T(8,128)}) custom-call(bf16[256,3072]{1,0:T(8,128)(2,1)} %get-tuple-element.66.refs_0_, bf16[256,1024]{1,0:T(8,128)(2,1)} %get-tuple-element.67.refs_1_, ...), custom_call_target="tpu_custom_call" | custom-call | tf_op jit(solution)/shard_map/widen/pallas_call | solution.py:1983
  479.1 0.0 copy-done
  479.1 0.9 copy.17
Async XLA Ops:
  470.4 8.7 %copy-start = (bf16[3,128,1024]{2,1,0:T(8,128)(2,1)S(1)}, bf16[3,128,1024]{2,1,0:T(8,128)(2,1)}, u32[]{:S(2)}) copy-start(bf16[3,128,1024]{2,1,0:T(8,128)(2,1)} %get-tuple-element.65) | copy-start | bytes 2359300

commit v8 on v7

--- a/solution.py
+++ b/solution.py
@@ -1069,10 +1069,12 @@
             wt=self.sibling,
         )
 
-    def across_copy(self, m):
-        return self.wires.remote(
-            ("to across", m), self.far.at[m], self.from_across.at[m], wt=self.across
-        )
+    def half(self, part):
+        return pl.ds(part * (self.rows // 2), self.rows // 2)
+
+    def across_copy(self, m, part):
+        source, target = self.far.at[m, self.half(part), :], self.from_across.at[m, self.half(part), :]
+        return self.wires.remote(("to across", m, part), source, target, wt=self.across)
 
     def begin(self, m):
         for index in range(3):
@@ -1104,21 +1106,29 @@
         total = self.stripe(m, self.across)[...].astype(jnp.float32)
         total = total + self.from_sibling[m, 0].astype(jnp.float32)
         self.far[m] = total.astype(jnp.bfloat16)
-        self.across_copy(m).start()
-
-    def finish(self, m):
-        self.across_copy(m).wait_recv()
-        total = self.skip[self.place(m), :] + self.stripe(m, self.w)[...].astype(jnp.float32)
-        total = total + self.from_sibling[m, 1].astype(jnp.float32)
-        total = total + self.from_across[m].astype(jnp.float32)
-        self.grad_states[self.place(m), :] = total.astype(jnp.bfloat16)
+        for part in range(2):
+            self.across_copy(m, part).start()
+
+    def finish(self, m, then=lambda part: None):
+        half = self.rows // 2
+        for part in range(2):
+            self.across_copy(m, part).wait_recv()
+            at = self.half(part)
+            place = pl.ds(m * self.rows + part * half, half)
+            own = self.part.at[m, pl.ds(self.w * self.rows + part * half, half), :]
+            total = self.skip[place, :] + own[...].astype(jnp.float32)
+            total = total + self.from_sibling[m, 1, at, :].astype(jnp.float32)
+            total = total + self.from_across[m, at, :].astype(jnp.float32)
+            self.grad_states[place, :] = total.astype(jnp.bfloat16)
+            then(part)
 
     def end(self, m):
         for index in range(3):
             self.heads_copy(m, index).wait_send()
         for index in range(2):
             self.sibling_copy(m, index).wait_send()
-        self.across_copy(m).wait_send()
+        for part in range(2):
+            self.across_copy(m, part).wait_send()
 
 
 def back_scratch(micro, pack, local, width):
@@ -1249,18 +1259,18 @@
                 copy.start()
             back.begin(m)
 
-    def back_copy(m):
-        place = back.place(m)
-        return wires.remote(
-            ("return", m), grad_states.at[place, :], returned.at[place, :], section=1 - section
-        )
+    def back_copy(m, part):
+        place = pl.ds(m * rows + part * (rows // 2), rows // 2)
+        source, target = grad_states.at[place, :], returned.at[place, :]
+        return wires.remote(("return", m, part), source, target, section=1 - section)
 
     def finish(m):
-        back.finish(m)
-
-        @pl.when(section == 1)
-        def _():
-            back_copy(m).start()
+        def then(part):
+            @pl.when(section == 1)
+            def _():
+                back_copy(m, part).start()
+
+        back.finish(m, then)
 
     arrive(0)
     load_weights(3, 5)
@@ -1300,12 +1310,14 @@
 
         @pl.when(section == 1)
         def _():
-            back_copy(m).wait_send()
+            for part in range(2):
+                back_copy(m, part).wait_send()
 
         @pl.when(section == 0)
         def _():
             relay_copy(m).wait_send()
-            back_copy(m).wait_recv()
+            for part in range(2):
+                back_copy(m, part).wait_recv()
 
 
 SAVED = ("normal_one", "first", "hidden", "slope", "normal_two", "final", "grad")

time: 487 us -> 486 us (level)
  no operation moved by 1% of the time
where the time goes in v8:
time: 486 us; the launch traced here: 479 us
  Pallas kernels  477 us (98%)
    pallas_call x1, Pallas kernels, last_pass(): pl.pallas_call(functools.partial(last_kernel, chunks, size), in_specs=[in...  216 us
    pallas_call x1, Pallas kernels, first_pass(): pl.pallas_call(functools.partial(first_kernel, size), in_specs=[anywhere]...  129 us
    pallas_call x1, Pallas kernels, mid_pass(): pl.pallas_call(functools.partial(mid_kernel, size), in_specs=[anywhere] *...  124 us

profile of v8, /device:TPU:4, one launch (start us, length us, event | category | flops | bytes accessed | tf_op | source)
XLA Modules:
  0.0 479.0 jit_solution(3349614498683187504)
XLA Ops:
  0.6 128.6 %first_pass.1 = (bf16[3,128,1024]{2,1,0:T(8,128)(2,1)}, bf16[1024,768]{1,0:T(8,128)(2,1)}, bf16[1024,1024]{1,0:T(8,128)(2,1)}, bf16[1024,4096]{1,0:T(8,128)(2,1)...) custom-call(bf16[3,128,1024]{2,1,0:T(8,128)(2,1)} %bitcast.14, ...), custom_call_target="tpu_custom_call" | custom-call | tf_op jit(solution)/shard_map/first_pass/pallas_call | solution.py:989
  129.2 124.0 %mid_pass.1 = (bf16[3,512,1024]{2,1,0:T(8,128)(2,1)}, bf16[3,512,768]{2,1,0:T(8,128)(2,1)}, bf16[384,1024]{1,0:T(8,128)(2,1)}, f32[384,1024]{1,0:T(8,128)}, bf16...) custom-call(bf16[3,128,1024]{2,1,0:T(8,128)(2,1)} %get-tuple-element, ...), custom_call_target="tpu_custom_call" | custom-call | tf_op jit(solution)/shard_map/mid_pass/pallas_call | solution.py:1347
  253.2 215.7 %last_pass.1 = (bf16[3,128,1024]{2,1,0:T(8,128)(2,1)}, bf16[256,3072]{1,0:T(8,128)(2,1)}, bf16[256,1024]{1,0:T(8,128)(2,1)}, bf16[256,4096]{1,0:T(8,128)(2,1)}, ...) custom-call(bf16[1024,768]{1,0:T(8,128)(2,1)} %get-tuple-element.42.refs_5_.refs_0_, ...), custom_call_target="tpu_custom_call" | custom-call | tf_op jit(solution)/shard_map/last_pass/pallas_call | solution.py:1924
  468.9 0.0 copy-start
  469.0 8.7 %widen.1 = (f32[1,256,3072]{2,1,0:T(8,128)}, f32[1,256,1024]{2,1,0:T(8,128)}, f32[1,256,4096]{2,1,0:T(8,128)}, f32[1,1024,1024]{2,1,0:T(8,128)}, f32[1,1024]{1,0:T(1,128)}, /*index=5*/f32[1,8,256]{2,1,0:T(8,128)}) custom-call(bf16[256,3072]{1,0:T(8,128)(2,1)} %get-tuple-element.66.refs_0_, bf16[256,1024]{1,0:T(8,128)(2,1)} %get-tuple-element.67.refs_1_, ...), custom_call_target="tpu_custom_call" | custom-call | tf_op jit(solution)/shard_map/widen/pallas_call | solution.py:1995
  477.6 0.0 copy-done
  477.6 0.9 copy.17
Async XLA Ops:
  468.9 8.7 %copy-start = (bf16[3,128,1024]{2,1,0:T(8,128)(2,1)S(1)}, bf16[3,128,1024]{2,1,0:T(8,128)(2,1)}, u32[]{:S(2)}) copy-start(bf16[3,128,1024]{2,1,0:T(8,128)(2,1)} %get-tuple-element.65) | copy-start | bytes 2359300
